TPU v7x, 256 devices: a whole 4x4x8 slice. The times are simulated.
256 devices in a mesh: gx: 4 (over y), gy: 4 (over z_lo), gz: 16 (over z_hi, x, core).
Axes of the slice: x: 4, y: 4, z: 8 (z_hi: 2, z_lo: 4; z = z_hi * 4 + z_lo), core: 2. Of those that a mesh axis runs over, the one named last changes fastest.
Arguments:
- offsets: float32 [8, 8, 32, 3, 1024], P('gx', 'gy', 'gz'), may hold values from 0 to 1
- probes: bfloat16 [8, 8, 32, 32, 1024], P('gx', 'gy', 'gz'), may hold values from -6 to 6
- counts: int32 [8, 8, 32], P('gx', 'gy', 'gz'), may hold values from 1 to 1024, as said below
- req_box: int32 [4, 4, 16, 64, 2], P('gx', 'gy', 'gz'), may hold values from -1 to 7, as said below
- req_tgt: int32 [4, 4, 16, 64, 2], P('gx', 'gy', 'gz'), may hold values from 0 to 7, as said below
Outputs:
- kv: bfloat16 [8, 8, 32, 32, 1024], P('gx', 'gy', 'gz')
- quad: float32 [32], replicated
Inputs may be any that keep to these rules, and one draw needn't show every extreme that they name: `counts`: every device has a box with 1024 points. `req_box`: A local box index of the peer, or -1 for an unused slot; the live slots of a pair come first; a pair whose gy indices and gz indices both differ by less than 2 has no live slot; some pair has all 2 slots live. `req_tgt`: A local box index of the requesting device.
All inputs are finite; a program needn't handle non-finite values.
Results may differ from a plain program's by a relative error of at most 0.0012.
The roundings to bfloat16 on the way count: a program that leaves them out, or rounds other values in their place, can miss the bound.
Values may be sent and summed in bfloat16 or wider, within the bound.
No kernel may reach another device: no remote copies, remote signals or barrier semaphores. Data moves between devices by JAX's collectives and lax.ppermute only.
A program may use at most 64 MiB of HBM per device.

v0:
```python
import math

import jax
import jax.numpy as jnp
from jax import lax
from jax.sharding import PartitionSpec as P

ORDER = 4


neighbour_shifts = ((0, 0, 0), (1, 0, 0), (-1, 0, 0), (0, 1, 0), (0, -1, 0), (0, 0, 1), (0, 0, -1))


def with_halo(block, sides, width):
    for axis, dim in sides:
        count = lax.axis_size(axis)
        forward = [(i, i + 1) for i in range(count - 1)]
        backward = [(target, source) for source, target in forward]
        low = lax.ppermute(
            lax.slice_in_dim(block, block.shape[dim] - width, None, axis=dim), axis, forward
        )
        high = lax.ppermute(lax.slice_in_dim(block, 0, width, axis=dim), axis, backward)
        block = jnp.concatenate([low, block, high], axis=dim)
    return block


def cheb_nodes():
    counter = jnp.arange(ORDER, dtype=jnp.float32)
    return 0.5 + 0.5 * jnp.cos((2.0 * counter + 1.0) * math.pi / (2.0 * ORDER))


def cheb_terms(unit_pos):
    series = [unit_pos, 2.0 * unit_pos * unit_pos - 1.0]
    series.append(2.0 * unit_pos * series[-1] - series[-2])
    return jnp.stack(series[: ORDER - 1])


def axis_weights(coord_row):
    at_points = cheb_terms(2.0 * coord_row - 1.0)
    at_nodes = cheb_terms(2.0 * cheb_nodes() - 1.0)
    return 1.0 / ORDER + 2.0 / ORDER * jnp.dot(
        at_nodes.T, at_points, precision=lax.Precision.HIGHEST
    )


def interp_table(point_offsets):
    first_w = axis_weights(point_offsets[0])
    second_w = axis_weights(point_offsets[1])
    third_w = axis_weights(point_offsets[2])
    product = first_w[:, None, None, :] * second_w[None, :, None, :] * third_w[None, None, :, :]
    return product.reshape(ORDER * ORDER * ORDER, point_offsets.shape[-1])


def node_grid():
    node_pos = cheb_nodes()
    full_shape = (ORDER, ORDER, ORDER)
    first_c = jnp.broadcast_to(node_pos[:, None, None], full_shape).reshape(-1)
    second_c = jnp.broadcast_to(node_pos[None, :, None], full_shape).reshape(-1)
    third_c = jnp.broadcast_to(node_pos[None, None, :], full_shape).reshape(-1)
    return jnp.stack([first_c, second_c, third_c])


def translate(delta, picked, target_hot):
    grid_pos = node_grid()
    terms = grid_pos.shape[1]
    squares = jnp.zeros((delta.shape[0], terms, terms), jnp.float32)
    for axis_num in range(3):
        separation = (
            delta[:, axis_num][:, None, None]
            + grid_pos[axis_num][None, None, :]
            - grid_pos[axis_num][None, :, None]
        )
        squares = squares + separation * separation
    coupling = lax.rsqrt(1.0 + squares).astype(jnp.bfloat16)
    stacked = picked.reshape(picked.shape[0], terms, -1)
    local_terms = jnp.einsum("sqp,spr->sqr", coupling, stacked, preferred_element_type=jnp.float32)
    flat_terms = local_terms.reshape(picked.shape[0], -1)
    return jnp.dot(target_hot, flat_terms, precision=lax.Precision.HIGHEST)


def near_field(ext_offsets, ext_vectors, first_i, second_i, third_i):
    points = ext_offsets.shape[-1]
    probe_count = ext_vectors.shape[-2]
    zero_i = jnp.zeros((), jnp.int32)
    first_i = jnp.asarray(first_i)
    second_i = jnp.asarray(second_i)
    third_i = jnp.asarray(third_i)
    one_i = jnp.ones((), jnp.int32)
    target = lax.dynamic_slice(
        ext_offsets,
        (first_i + one_i, second_i + one_i, third_i + one_i, zero_i, zero_i),
        (1, 1, 1, 3, points),
    )[0, 0, 0]
    source_rows = []
    source_vecs = []
    for neighbour in neighbour_shifts:
        begin = (
            first_i + 1 + neighbour[0],
            second_i + 1 + neighbour[1],
            third_i + 1 + neighbour[2],
            zero_i,
            zero_i,
        )
        source = lax.dynamic_slice(ext_offsets, begin, (1, 1, 1, 3, points))[0, 0, 0]
        shift_col = jnp.array(neighbour, jnp.float32)[:, None]
        source_rows.append(source + shift_col)
        source_vecs.append(
            lax.dynamic_slice(ext_vectors, begin, (1, 1, 1, probe_count, points))[0, 0, 0]
        )
    all_sources = jnp.concatenate(source_rows, axis=1)
    all_vectors = jnp.concatenate(source_vecs, axis=1)
    squares = jnp.zeros((all_sources.shape[1], points), jnp.float32)
    for axis_num in range(3):
        separation = all_sources[axis_num][:, None] - target[axis_num][None, :]
        squares = squares + separation * separation
    kernel_tile = lax.rsqrt(1.0 + squares).astype(jnp.bfloat16)
    return jnp.dot(all_vectors, kernel_tile, preferred_element_type=jnp.float32)


def shards(offsets, probes, counts, req_box, req_tgt):
    box_x, box_y, box_z, three_c, points = offsets.shape
    probe_count = probes.shape[3]
    boxes = box_x * box_y * box_z
    width_pr = probe_count * ORDER * ORDER * ORDER
    slot_ids = jnp.arange(points, dtype=jnp.int32)
    live_mask = slot_ids[None, None, None, :] < counts[..., None]
    vectors = jnp.where(live_mask[:, :, :, None, :], probes, jnp.zeros_like(probes))
    ext_offsets = with_halo(offsets, (("gx", 0), ("gy", 1), ("gz", 2)), 1)
    ext_vectors = with_halo(vectors, (("gx", 0), ("gy", 1), ("gz", 2)), 1)

    def near_one(box_id):
        return near_field(
            ext_offsets,
            ext_vectors,
            box_id // (box_y * box_z),
            box_id // box_z % box_y,
            box_id % box_z,
        )

    near = lax.map(near_one, jnp.arange(boxes, dtype=jnp.int32))
    tables = jax.vmap(interp_table)(offsets.reshape(boxes, 3, points)).astype(jnp.bfloat16)
    flat_vectors = vectors.reshape(boxes, probe_count, points)
    moments = jnp.einsum("bpn,brn->bpr", tables, flat_vectors, preferred_element_type=jnp.float32)
    moments = moments.astype(jnp.bfloat16).reshape(boxes, width_pr)
    size_gz = lax.axis_size("gz")
    peers = lax.axis_size("gy") * size_gz
    capacity = req_box.shape[4]
    asked_here = req_box.reshape(peers, capacity)
    wanted = req_tgt.reshape(peers, capacity)
    peer_ids = jnp.broadcast_to(jnp.arange(peers, dtype=jnp.int32)[:, None], (peers, capacity))
    box_range = jnp.arange(boxes, dtype=jnp.int32)
    global_ids = jnp.where(asked_here >= 0, peer_ids * boxes + asked_here, -1).reshape(-1)
    piece = lax.all_gather(moments, ("gy", "gz"), axis=0, tiled=True)
    rows_here = piece.shape[0]
    select_hot = (global_ids[:, None] == jnp.arange(rows_here, dtype=jnp.int32)[None, :]).astype(
        jnp.bfloat16
    )
    picked = jnp.dot(select_hot, piece, preferred_element_type=jnp.float32).astype(jnp.bfloat16)
    my_y = lax.axis_index("gy")
    my_z = lax.axis_index("gz")
    delta_x = asked_here // (box_y * box_z) - wanted // (box_y * box_z)
    delta_y = (
        (peer_ids // size_gz - my_y) * box_y + asked_here // box_z % box_y - wanted // box_z % box_y
    )
    delta_z = (peer_ids % size_gz - my_z) * box_z + asked_here % box_z - wanted % box_z
    delta = jnp.stack([delta_x, delta_y, delta_z], axis=-1).reshape(-1, 3).astype(jnp.float32)
    target_hot = (wanted.reshape(-1)[None, :] == box_range[:, None]).astype(jnp.float32)
    local_exp = translate(delta, picked, target_hot).astype(jnp.bfloat16)
    local_exp = local_exp.reshape(boxes, ORDER * ORDER * ORDER, probe_count)
    far = jnp.einsum("bqr,bqn->brn", local_exp, tables, preferred_element_type=jnp.float32)
    total = ((near + far) * (1.0 / math.sqrt(7.0 * points))).reshape(
        box_x, box_y, box_z, probe_count, points
    )
    kv = jnp.where(live_mask[:, :, :, None, :], total, 0.0).astype(jnp.bfloat16)
    partial_sums = jnp.sum(vectors.astype(jnp.float32) * total, axis=(0, 1, 2, 4))
    live_total = jnp.sum(live_mask.astype(jnp.float32))
    summed, counted = lax.psum((partial_sums, live_total), ("gx", "gy", "gz"))
    quad = summed / counted
    return (kv, quad)


def solution(mesh):
    placed = (
        P("gx", "gy", "gz", None, None),
        P("gx", "gy", "gz", None, None),
        P("gx", "gy", "gz"),
        P("gx", "gy", "gz", None, None),
        P("gx", "gy", "gz", None, None),
    )
    return jax.shard_map(
        shards,
        mesh=mesh,
        in_specs=placed,
        out_specs=(P("gx", "gy", "gz", None, None), P()),
        check_vma=False,
    )
```

profile of v0, /device:TPU:1, one launch (start us, length us, event | category | flops | bytes accessed | tf_op | source)
XLA Modules:
  0.0 383.2 jit_solution(9977545158280187520)
XLA Ops:
  12.3 4.1 %collective-permute-start = (bf16[1,2,2,32,1024]{4,3,2,1,0:T(8,128)(2,1)S(1)}, bf16[1,2,2,32,1024]{4,3,2,1,0:T(8,128)(2,1)S(1)}, u32[]{:S(2)}, u32[]{:S(2)}) collective-permute-start(bf16[1,2,2,32,1024]{4,3,2,1,0:T(8,128)(2,1)S(1)} %get-tuple-element.361), channel_id=1, source_target_pairs={{0,64},{64,128},{128,192},{1,65},{65,129},{129,193},{2,66},{66,130... | collective-permute-start | bytes 786440 | tf_op jit(solution)/shard_map/ppermute | solution.py:19
  17.7 4.6 %collective-permute-start.6 = (f32[1,2,2,3,1024]{4,3,2,1,0:T(4,128)S(1)}, f32[1,2,2,3,1024]{4,3,2,1,0:T(4,128)}, u32[]{:S(2)}, u32[]{:S(2)}) collective-permute-start(f32[1,2,2,3,1024]{4,3,2,1,0:T(4,128)S(1)} %copy.61), channel_id=1, source_target_pairs={{0,64},{64,128},{128,192},{1,65},{65,129},{129,193},{2,66},{66,130... | collective-permute-start | bytes 147464 | tf_op jit(solution)/shard_map/ppermute | solution.py:19
  28.6 3.5 collective-permute-start.2
  35.5 7.7 %collective-permute-done.2 = bf16[4,1,2,32,1024]{4,3,2,1,0:T(8,128)(2,1)S(1)} collective-permute-done((bf16[4,1,2,32,1024]{4,3,2,1,0:T(8,128)(2,1)}, bf16[4,1,2,32,1024]{4,3,2,1,0:T(8,128)(2,1)S(1)}, u32[]{:S(2)}, u32[]{:S(2)}) %collective-permute-start.2) | collective-permute-done | bytes 524320 | tf_op jit(solution)/shard_map/ppermute | solution.py:19
  43.2 4.2 %collective-permute-done.3 = bf16[4,1,2,32,1024]{4,3,2,1,0:T(8,128)(2,1)S(1)} collective-permute-done((bf16[4,1,2,32,1024]{4,3,2,1,0:T(8,128)(2,1)}, bf16[4,1,2,32,1024]{4,3,2,1,0:T(8,128)(2,1)S(1)}, u32[]{:S(2)}, u32[]{:S(2)}) %collective-permute-start.3) | collective-permute-done | bytes 524320 | tf_op jit(solution)/shard_map/ppermute | solution.py:22
  48.0 4.3 %collective-permute-start.4 = (bf16[4,4,1,32,1024]{4,3,2,1,0:T(8,128)(2,1)S(1)}, bf16[4,4,1,32,1024]{4,3,2,1,0:T(8,128)(2,1)S(1)}, u32[]{:S(2)}, u32[]{:S(2)}) collective-permute-start(bf16[4,4,1,32,1024]{4,3,2,1,0:T(8,128)(2,1)S(1)} %get-tuple-element.355), channel_id=1, source_target_pairs={{0,1},{1,2},{2,3},{3,4},{4,5},{5,6},{6,7},{7,8},{8,9},{9,10},{10,1... | collective-permute-start | bytes 3145736 | tf_op jit(solution)/shard_map/ppermute | solution.py:19
  54.2 5.0 %collective-permute-start.8 = (f32[4,1,2,3,1024]{4,3,2,1,0:T(4,128)S(1)}, f32[4,1,2,3,1024]{4,3,2,1,0:T(4,128)S(1)}, u32[]{:S(2)}, u32[]{:S(2)}) collective-permute-start(f32[4,1,2,3,1024]{4,3,2,1,0:T(4,128)S(1)} %get-tuple-element.363), channel_id=1, source_target_pairs={{0,16},{16,32},{32,48},{1,17},{17,33},{33,49},{2,18},{18,34},{34,5... | collective-permute-start | bytes 294920 | tf_op jit(solution)/shard_map/ppermute | solution.py:19
  61.3 4.1 %collective-permute-done.9 = f32[4,1,2,3,1024]{4,3,2,1,0:T(4,128)S(1)} collective-permute-done((f32[4,1,2,3,1024]{4,3,2,1,0:T(4,128)S(1)}, f32[4,1,2,3,1024]{4,3,2,1,0:T(4,128)S(1)}, u32[]{:S(2)}, u32[]{:S(2)}) %collective-permute-start.9) | collective-permute-done | bytes 98336 | tf_op jit(solution)/shard_map/ppermute | solution.py:22
  65.6 4.6 %collective-permute-start.10 = (f32[4,4,1,3,1024]{4,3,2,1,0:T(4,128)S(1)}, f32[4,4,1,3,1024]{4,3,2,1,0:T(4,128)S(1)}, u32[]{:S(2)}, u32[]{:S(2)}) collective-permute-start(f32[4,4,1,3,1024]{4,3,2,1,0:T(4,128)S(1)} %get-tuple-element.359), channel_id=1, source_target_pairs={{0,1},{1,2},{2,3},{3,4},{4,5},{5,6},{6,7},{7,8},{8,9},{9,10},{10,1... | collective-permute-start | bytes 589832 | tf_op jit(solution)/shard_map/ppermute | solution.py:19
  73.9 4.6 %collective-permute-done.11 = f32[4,4,1,3,1024]{4,3,2,1,0:T(4,128)S(1)} collective-permute-done((f32[4,4,1,3,1024]{4,3,2,1,0:T(4,128)S(1)}, f32[4,4,1,3,1024]{4,3,2,1,0:T(4,128)S(1)}, u32[]{:S(2)}, u32[]{:S(2)}) %collective-permute-start.11) | collective-permute-done | bytes 196640 | tf_op jit(solution)/shard_map/ppermute | solution.py:22
  78.9 2.4 pad_maximum_fusion
  81.3 167.6 %while.16 = (s32[]{:T(128)}, f32[8,32,1024]{2,1,0:T(8,128)}, s32[8]{0:T(128)S(1)}, bf16[4,4,4,32,1024]{4,3,2,1,0:T(8,128)(2,1)}, f32[4,4,4,3,1024]{4,3,2,1,0:T(4...) while((s32[]{:T(128)}, f32[8,32,1024]{2,1,0:T(8,128)}, ...), condition=%wide.region_1.2_spmd.clone, body=%wide.region_0.1_spmd.sunk.clone.sunk | while | flops 543180864 | bytes 2032294 | solution.py:140
  91.0 11.3 %fusion.69 = f32[8,32,1024]{2,1,0:T(8,128)} fusion(f32[8,32,1024]{2,1,0:T(8,128)} %get-tuple-element.455, s32[]{:T(128)} %get-tuple-element.454, bf16[32,7168]{1,0:T(8,128)(2,1)S(1)} %bitcast_dynamic-update-slice_fusion.20, f32[1024]{0:T(1024)S(1)} %bitcast.163, f32[7168]{0:T(1024)S(1)} %bitcast.160, f32[1024]{0:T(1024)S(1)} %bitcast.164, ...), kind=kOutput, calls=%fused_computation.3.clone.1 | convolution fusion | flops 543162368 | bytes 688640 | tf_op jit(solution)/shard_map/while/body/eval_jaxpr/dot_general | solution.py:117
  112.0 11.3 %fusion.69 = f32[8,32,1024]{2,1,0:T(8,128)} fusion(f32[8,32,1024]{2,1,0:T(8,128)} %get-tuple-element.455, s32[]{:T(128)} %get-tuple-element.454, bf16[32,7168]{1,0:T(8,128)(2,1)S(1)} %bitcast_dynamic-update-slice_fusion.20, f32[1024]{0:T(1024)S(1)} %bitcast.163, f32[7168]{0:T(1024)S(1)} %bitcast.160, f32[1024]{0:T(1024)S(1)} %bitcast.164, ...), kind=kOutput, calls=%fused_computation.3.clone.1 | convolution fusion | flops 543162368 | bytes 688640 | tf_op jit(solution)/shard_map/while/body/eval_jaxpr/dot_general | solution.py:117
  132.9 11.2 %fusion.69 = f32[8,32,1024]{2,1,0:T(8,128)} fusion(f32[8,32,1024]{2,1,0:T(8,128)} %get-tuple-element.455, s32[]{:T(128)} %get-tuple-element.454, bf16[32,7168]{1,0:T(8,128)(2,1)S(1)} %bitcast_dynamic-update-slice_fusion.20, f32[1024]{0:T(1024)S(1)} %bitcast.163, f32[7168]{0:T(1024)S(1)} %bitcast.160, f32[1024]{0:T(1024)S(1)} %bitcast.164, ...), kind=kOutput, calls=%fused_computation.3.clone.1 | convolution fusion | flops 543162368 | bytes 688640 | tf_op jit(solution)/shard_map/while/body/eval_jaxpr/dot_general | solution.py:117
  153.9 11.2 %fusion.69 = f32[8,32,1024]{2,1,0:T(8,128)} fusion(f32[8,32,1024]{2,1,0:T(8,128)} %get-tuple-element.455, s32[]{:T(128)} %get-tuple-element.454, bf16[32,7168]{1,0:T(8,128)(2,1)S(1)} %bitcast_dynamic-update-slice_fusion.20, f32[1024]{0:T(1024)S(1)} %bitcast.163, f32[7168]{0:T(1024)S(1)} %bitcast.160, f32[1024]{0:T(1024)S(1)} %bitcast.164, ...), kind=kOutput, calls=%fused_computation.3.clone.1 | convolution fusion | flops 543162368 | bytes 688640 | tf_op jit(solution)/shard_map/while/body/eval_jaxpr/dot_general | solution.py:117
  174.8 11.2 %fusion.69 = f32[8,32,1024]{2,1,0:T(8,128)} fusion(f32[8,32,1024]{2,1,0:T(8,128)} %get-tuple-element.455, s32[]{:T(128)} %get-tuple-element.454, bf16[32,7168]{1,0:T(8,128)(2,1)S(1)} %bitcast_dynamic-update-slice_fusion.20, f32[1024]{0:T(1024)S(1)} %bitcast.163, f32[7168]{0:T(1024)S(1)} %bitcast.160, f32[1024]{0:T(1024)S(1)} %bitcast.164, ...), kind=kOutput, calls=%fused_computation.3.clone.1 | convolution fusion | flops 543162368 | bytes 688640 | tf_op jit(solution)/shard_map/while/body/eval_jaxpr/dot_general | solution.py:117
  195.8 11.3 %fusion.69 = f32[8,32,1024]{2,1,0:T(8,128)} fusion(f32[8,32,1024]{2,1,0:T(8,128)} %get-tuple-element.455, s32[]{:T(128)} %get-tuple-element.454, bf16[32,7168]{1,0:T(8,128)(2,1)S(1)} %bitcast_dynamic-update-slice_fusion.20, f32[1024]{0:T(1024)S(1)} %bitcast.163, f32[7168]{0:T(1024)S(1)} %bitcast.160, f32[1024]{0:T(1024)S(1)} %bitcast.164, ...), kind=kOutput, calls=%fused_computation.3.clone.1 | convolution fusion | flops 543162368 | bytes 688640 | tf_op jit(solution)/shard_map/while/body/eval_jaxpr/dot_general | solution.py:117
  216.7 11.2 %fusion.69 = f32[8,32,1024]{2,1,0:T(8,128)} fusion(f32[8,32,1024]{2,1,0:T(8,128)} %get-tuple-element.455, s32[]{:T(128)} %get-tuple-element.454, bf16[32,7168]{1,0:T(8,128)(2,1)S(1)} %bitcast_dynamic-update-slice_fusion.20, f32[1024]{0:T(1024)S(1)} %bitcast.163, f32[7168]{0:T(1024)S(1)} %bitcast.160, f32[1024]{0:T(1024)S(1)} %bitcast.164, ...), kind=kOutput, calls=%fused_computation.3.clone.1 | convolution fusion | flops 543162368 | bytes 688640 | tf_op jit(solution)/shard_map/while/body/eval_jaxpr/dot_general | solution.py:117
  237.7 11.2 %fusion.69 = f32[8,32,1024]{2,1,0:T(8,128)} fusion(f32[8,32,1024]{2,1,0:T(8,128)} %get-tuple-element.455, s32[]{:T(128)} %get-tuple-element.454, bf16[32,7168]{1,0:T(8,128)(2,1)S(1)} %bitcast_dynamic-update-slice_fusion.20, f32[1024]{0:T(1024)S(1)} %bitcast.163, f32[7168]{0:T(1024)S(1)} %bitcast.160, f32[1024]{0:T(1024)S(1)} %bitcast.164, ...), kind=kOutput, calls=%fused_computation.3.clone.1 | convolution fusion | flops 543162368 | bytes 688640 | tf_op jit(solution)/shard_map/while/body/eval_jaxpr/dot_general | solution.py:117
  253.1 3.0 fusion.4
  256.1 3.1 copy.51
  260.4 2.3 select_convert_fusion
  263.0 112.2 %all-reduce = (f32[32]{0:T(128)S(1)}, f32[]{:T(128)}) all-reduce(f32[32]{0:T(128)S(1)} %multiply_reduce_fusion, f32[]{:T(128)} %convert_reduce_fusion), channel_id=1, replica_groups=mesh['gx'=4,'gy'=4,'gz'=16] {'gx','gy','gz'}, use_global_device_ids=true, to_apply=%region_3.4 | all-reduce | flops 33 | bytes 264 | tf_op jit(solution)/shard_map/psum | solution.py:177
  (284 shorter events, 88.0 us)
Async XLA Ops:
  7.2 241.8 %all-gather.2.cloned.1.call-start = ((), (), s32[]{:S(2)}) async-start(), calls=%async_computation | async-start | bytes 2129920 | tf_op jit(solution)/shard_map/all_gather | solution.py:153
  9.7 7.9 %copy-start.4 = (f32[2,2,2,3,1024]{4,2,3,1,0:T(2,128)S(1)}, f32[2,2,2,3,1024]{4,2,3,1,0:T(2,128)}, u32[]{:S(2)}) copy-start(f32[2,2,2,3,1024]{4,2,3,1,0:T(2,128)} %param.14) | copy-start | bytes 294916
  9.9 13.9 %copy-start.24 = (s32[1,1,1,64,2]{3,4,2,1,0:T(2,128)S(1)}, s32[1,1,1,64,2]{3,4,2,1,0:T(2,128)}, u32[]{:S(2)}) copy-start(s32[1,1,1,64,2]{3,4,2,1,0:T(2,128)} %param.17) | copy-start | bytes 1540
  9.9 14.6 %copy-start.25 = (s32[1,1,1,64,2]{3,4,2,1,0:T(2,128)S(1)}, s32[1,1,1,64,2]{3,4,2,1,0:T(2,128)}, u32[]{:S(2)}) copy-start(s32[1,1,1,64,2]{3,4,2,1,0:T(2,128)} %param.18) | copy-start | bytes 1540
  10.7 17.9 %copy-start = (bf16[8,64,1024]{2,1,0:T(8,128)(2,1)}, bf16[8,64,1024]{2,1,0:T(8,128)(2,1)S(1)}, u32[]{:S(2)}) copy-start(bf16[8,64,1024]{2,1,0:T(8,128)(2,1)S(1)} %convert_element_type.45) | copy-start | bytes 3145732
  10.8 17.8 %copy-start.5 = (pred[2,2,2,1024]{3,2,1,0:T(4,128)(4,1)}, pred[2,2,2,1024]{3,2,1,0:T(4,128)(4,1)S(1)}, u32[]{:S(2)}) copy-start(pred[2,2,2,1024]{3,2,1,0:T(4,128)(4,1)S(1)} %iota_compare_fusion.2) | copy-start | bytes 24580
  12.3 15.1 %collective-permute-start = (bf16[1,2,2,32,1024]{4,3,2,1,0:T(8,128)(2,1)S(1)}, bf16[1,2,2,32,1024]{4,3,2,1,0:T(8,128)(2,1)S(1)}, u32[]{:S(2)}, u32[]{:S(2)}) collective-permute-start(bf16[1,2,2,32,1024]{4,3,2,1,0:T(8,128)(2,1)S(1)} %get-tuple-element.361), channel_id=1, source_target_pairs={{0,64},{64,128},{128,192},{1,65},{65,129},{129,193},{2,66},{66,130... | collective-permute-start | bytes 786440 | tf_op jit(solution)/shard_map/ppermute | solution.py:19
  16.3 11.0 %collective-permute-start.1 = (bf16[1,2,2,32,1024]{4,3,2,1,0:T(8,128)(2,1)S(1)}, bf16[1,2,2,32,1024]{4,3,2,1,0:T(8,128)(2,1)S(1)}, u32[]{:S(2)}, u32[]{:S(2)}) collective-permute-start(bf16[1,2,2,32,1024]{4,3,2,1,0:T(8,128)(2,1)S(1)} %get-tuple-element.362), channel_id=1, source_target_pairs={{64,0},{128,64},{192,128},{65,1},{129,65},{193,129},{66,2},{130,66... | collective-permute-start | bytes 786440 | tf_op jit(solution)/shard_map/ppermute | solution.py:22
  17.7 16.8 %collective-permute-start.6 = (f32[1,2,2,3,1024]{4,3,2,1,0:T(4,128)S(1)}, f32[1,2,2,3,1024]{4,3,2,1,0:T(4,128)}, u32[]{:S(2)}, u32[]{:S(2)}) collective-permute-start(f32[1,2,2,3,1024]{4,3,2,1,0:T(4,128)S(1)} %copy.61), channel_id=1, source_target_pairs={{0,64},{64,128},{128,192},{1,65},{65,129},{129,193},{2,66},{66,130... | collective-permute-start | bytes 147464 | tf_op jit(solution)/shard_map/ppermute | solution.py:19
  22.3 13.1 %collective-permute-start.7 = (f32[1,2,2,3,1024]{4,3,2,1,0:T(4,128)S(1)}, f32[1,2,2,3,1024]{4,3,2,1,0:T(4,128)S(1)}, u32[]{:S(2)}, u32[]{:S(2)}) collective-permute-start(f32[1,2,2,3,1024]{4,3,2,1,0:T(4,128)S(1)} %copy.62), channel_id=1, source_target_pairs={{64,0},{128,64},{192,128},{65,1},{129,65},{193,129},{66,2},{130,66... | collective-permute-start | bytes 147464 | tf_op jit(solution)/shard_map/ppermute | solution.py:22
  24.9 7.2 %copy-start.18 = (f32[64]{0:T(128)}, f32[64]{0:T(128)S(1)}, u32[]{:S(2)}) copy-start(f32[64]{0:T(128)S(1)} %add.970) | copy-start | bytes 772
  25.1 7.1 %copy-start.20 = (f32[64]{0:T(128)}, f32[64]{0:T(128)S(1)}, u32[]{:S(2)}) copy-start(f32[64]{0:T(128)S(1)} %add.964) | copy-start | bytes 772
  26.7 5.5 %copy-start.22 = (f32[64]{0:T(128)}, f32[64]{0:T(128)S(1)}, u32[]{:S(2)}) copy-start(f32[64]{0:T(128)S(1)} %add.959) | copy-start | bytes 772
  28.6 14.7 %collective-permute-start.2 = (bf16[4,1,2,32,1024]{4,3,2,1,0:T(8,128)(2,1)}, bf16[4,1,2,32,1024]{4,3,2,1,0:T(8,128)(2,1)S(1)}, u32[]{:S(2)}, u32[]{:S(2)}) collective-permute-start(bf16[4,1,2,32,1024]{4,3,2,1,0:T(8,128)(2,1)} %get-tuple-element.357), channel_id=1, source_target_pairs={{0,16},{16,32},{32,48},{1,17},{17,33},{33,49},{2,18},{18,34},{34,5... | collective-permute-start | bytes 1572872 | tf_op jit(solution)/shard_map/ppermute | solution.py:19
  32.1 15.3 %collective-permute-start.3 = (bf16[4,1,2,32,1024]{4,3,2,1,0:T(8,128)(2,1)}, bf16[4,1,2,32,1024]{4,3,2,1,0:T(8,128)(2,1)S(1)}, u32[]{:S(2)}, u32[]{:S(2)}) collective-permute-start(bf16[4,1,2,32,1024]{4,3,2,1,0:T(8,128)(2,1)} %get-tuple-element.358), channel_id=1, source_target_pairs={{16,0},{32,16},{48,32},{17,1},{33,17},{49,33},{18,2},{34,18},{50,3... | collective-permute-start | bytes 1572872 | tf_op jit(solution)/shard_map/ppermute | solution.py:22
  48.0 30.9 %collective-permute-start.4 = (bf16[4,4,1,32,1024]{4,3,2,1,0:T(8,128)(2,1)S(1)}, bf16[4,4,1,32,1024]{4,3,2,1,0:T(8,128)(2,1)S(1)}, u32[]{:S(2)}, u32[]{:S(2)}) collective-permute-start(bf16[4,4,1,32,1024]{4,3,2,1,0:T(8,128)(2,1)S(1)} %get-tuple-element.355), channel_id=1, source_target_pairs={{0,1},{1,2},{2,3},{3,4},{4,5},{5,6},{6,7},{7,8},{8,9},{9,10},{10,1... | collective-permute-start | bytes 3145736 | tf_op jit(solution)/shard_map/ppermute | solution.py:19
  52.3 26.6 %collective-permute-start.5 = (bf16[4,4,1,32,1024]{4,3,2,1,0:T(8,128)(2,1)S(1)}, bf16[4,4,1,32,1024]{4,3,2,1,0:T(8,128)(2,1)S(1)}, u32[]{:S(2)}, u32[]{:S(2)}) collective-permute-start(bf16[4,4,1,32,1024]{4,3,2,1,0:T(8,128)(2,1)S(1)} %get-tuple-element.356), channel_id=1, source_target_pairs={{1,0},{2,1},{3,2},{4,3},{5,4},{6,5},{7,6},{8,7},{9,8},{10,9},{11,1... | collective-permute-start | bytes 3145736 | tf_op jit(solution)/shard_map/ppermute | solution.py:22
  54.2 7.0 %collective-permute-start.8 = (f32[4,1,2,3,1024]{4,3,2,1,0:T(4,128)S(1)}, f32[4,1,2,3,1024]{4,3,2,1,0:T(4,128)S(1)}, u32[]{:S(2)}, u32[]{:S(2)}) collective-permute-start(f32[4,1,2,3,1024]{4,3,2,1,0:T(4,128)S(1)} %get-tuple-element.363), channel_id=1, source_target_pairs={{0,16},{16,32},{32,48},{1,17},{17,33},{33,49},{2,18},{18,34},{34,5... | collective-permute-start | bytes 294920 | tf_op jit(solution)/shard_map/ppermute | solution.py:19
  59.2 6.2 %collective-permute-start.9 = (f32[4,1,2,3,1024]{4,3,2,1,0:T(4,128)S(1)}, f32[4,1,2,3,1024]{4,3,2,1,0:T(4,128)S(1)}, u32[]{:S(2)}, u32[]{:S(2)}) collective-permute-start(f32[4,1,2,3,1024]{4,3,2,1,0:T(4,128)S(1)} %get-tuple-element.364), channel_id=1, source_target_pairs={{16,0},{32,16},{48,32},{17,1},{33,17},{49,33},{18,2},{34,18},{50,3... | collective-permute-start | bytes 294920 | tf_op jit(solution)/shard_map/ppermute | solution.py:22
  65.6 8.3 %collective-permute-start.10 = (f32[4,4,1,3,1024]{4,3,2,1,0:T(4,128)S(1)}, f32[4,4,1,3,1024]{4,3,2,1,0:T(4,128)S(1)}, u32[]{:S(2)}, u32[]{:S(2)}) collective-permute-start(f32[4,4,1,3,1024]{4,3,2,1,0:T(4,128)S(1)} %get-tuple-element.359), channel_id=1, source_target_pairs={{0,1},{1,2},{2,3},{3,4},{4,5},{5,6},{6,7},{7,8},{8,9},{9,10},{10,1... | collective-permute-start | bytes 589832 | tf_op jit(solution)/shard_map/ppermute | solution.py:19
  70.2 8.3 %collective-permute-start.11 = (f32[4,4,1,3,1024]{4,3,2,1,0:T(4,128)S(1)}, f32[4,4,1,3,1024]{4,3,2,1,0:T(4,128)S(1)}, u32[]{:S(2)}, u32[]{:S(2)}) collective-permute-start(f32[4,4,1,3,1024]{4,3,2,1,0:T(4,128)S(1)} %get-tuple-element.360), channel_id=1, source_target_pairs={{1,0},{2,1},{3,2},{4,3},{5,4},{6,5},{7,6},{8,7},{9,8},{10,9},{11,1... | collective-permute-start | bytes 589832 | tf_op jit(solution)/shard_map/ppermute | solution.py:22
  81.3 167.7 %copy-start.26 = (s32[128]{0:T(128)S(1)}, s32[128]{0:T(128)}, u32[]{:S(2)}) copy-start(s32[128]{0:T(128)} %compare_select_fusion.4) | copy-start | bytes 1540
  253.1 6.1 %copy-start.17 = (s32[128]{0:T(128)S(1)}, s32[128]{0:T(128)}, u32[]{:S(2)}) copy-start(s32[128]{0:T(128)} %eq.39) | copy-start | bytes 1540
  256.1 4.3 %copy-start.6 = (pred[2,2,2,1024]{3,2,1,0:T(4,128)(4,1)S(1)}, pred[2,2,2,1024]{3,2,1,0:T(4,128)(4,1)}, u32[]{:S(2)}) copy-start(pred[2,2,2,1024]{3,2,1,0:T(4,128)(4,1)} %copy-done.5) | copy-start | bytes 24580
  (16 other events, 54.2 us)
Sparse Core Ops, SparseCore 0:
  12.3 128.2 all-gather.1
where the time goes:
time: 387 us; the launch traced here: 383 us
  blocking collectives  112 us (29%)
  matrix products  97.5 us (25%)
  local copies, waits for them, and re-layouts  65.4 us (17%)
  starting transfers between devices  35.3 us (9%)
  waiting for transfers between devices  21.7 us (6%)
  loops' own time  20.7 us (5%)
  other arithmetic  15.4 us (4%)
  between operations  14.9 us (4%)
    psum x1, blocking collectives, shards(): summed, counted = lax.psum((partial_sums, live_total), ('gx', 'gy', 'gz'))  112 us
    dot_general x8, matrix products, near_field(): return jnp.dot(all_vectors, kernel_tile, preferred_element_type=jnp.float32)  90 us
    while x56, local copies, waits for them, and re-layouts  40.6 us
    ppermute x6, starting transfers between devices, with_halo(): lax.ppermute(lax.slice_in_dim(block, block.shape[dim] - width, None, axis...  26.1 us
    another operation x1, loops' own time, shards(): near = lax.map(near_one, jnp.arange(boxes, dtype=jnp.int32))  20.7 us
    ppermute x6, waiting for transfers between devices, with_halo(): lax.ppermute(lax.slice_in_dim(block, 0, width, axis=dim), axis, backward)  12.9 us
    ppermute x6, starting transfers between devices, with_halo(): lax.ppermute(lax.slice_in_dim(block, 0, width, axis=dim), axis, backward)  9.19 us
    ppermute x6, waiting for transfers between devices, with_halo(): lax.ppermute(lax.slice_in_dim(block, block.shape[dim] - width, None, axis...  8.75 us
  transfers between devices with their start and end apart: 13, of which 5 were waited for; matrix products, arithmetic and copies ran while one was open for 41% of the time, Pallas kernels for 0%

commit v1 on v0

v1 whole, which is shorter than its diff:
```python
import functools
import math

import jax
import jax.numpy as jnp
from jax import lax
from jax.experimental import pallas as pl
from jax.experimental.pallas import tpu as pltpu
from jax.sharding import PartitionSpec as P

ORDER = 4
CHUNK = 128
BOXES = 8
FEATS = 48
ROWS = 48
F32 = jnp.float32
BF16 = jnp.bfloat16
NODES = [math.cos((2.0 * a + 1.0) * math.pi / (2.0 * ORDER)) for a in range(ORDER)]
FACES = ((0, -1), (0, 1), (1, -1), (1, 1), (2, -1), (2, 1))


def box_id(axis, at, first, second):
    place = [0, 0, 0]
    rest = [d for d in range(3) if d != axis]
    place[axis] = at
    place[rest[0]] = first
    place[rest[1]] = second
    return (place[0] * 2 + place[1]) * 2 + place[2]


def face_boxes(axis, at):
    return [box_id(axis, at, i, j) for i in range(2) for j in range(2)]


def split3(value):
    high = value.astype(BF16).astype(F32)
    rest = value - high
    mid = rest.astype(BF16).astype(F32)
    return high, mid, rest - mid


def row_ids(points):
    return lax.broadcasted_iota(jnp.int32, (8, points), 0)


def source_rows(pos, row):
    p1, p2, p3 = split3(pos)
    n1, n2, n3 = split3(1.0 + jnp.sum(pos * pos, axis=0, keepdims=True))
    s1 = jnp.where(row < 3, p1, jnp.where(row == 3, n1, jnp.where(row == 4, n2, jnp.where(row == 5, n3, 1.0))))
    s2 = p2 + pltpu.roll(p3, 3, 0)
    return jnp.concatenate([s1, s1, s2, s2, s1, jnp.zeros_like(s1)], axis=0).astype(BF16)


def target_rows(pos, row):
    p1, p2, p3 = split3(-2.0 * pos)
    m1, m2, m3 = split3(jnp.sum(pos * pos, axis=0, keepdims=True))
    qa = jnp.where(row < 3, p1, jnp.where(row < 6, 1.0, jnp.where(row == 6, m1, m2)))
    qb = jnp.where(row < 3, p2, jnp.where(row == 6, m3, 0.0))
    qc = p1 + pltpu.roll(p1, 3, 0)
    return jnp.concatenate([qa, qb, qc, p2, p3, jnp.zeros_like(qa)], axis=0).astype(BF16)


def prep_kernel(counts, offs, probes, pay, fa, fb, tab, mom, momf, f0, f1, f2, f3, f4, f5, pad):
    points = offs.shape[-1]
    row = row_ids(points)
    lane = lax.broadcasted_iota(jnp.int32, (1, points), 1)
    faces = (f0, f1, f2, f3, f4, f5)
    for k in range(BOXES):
        place = (k // 4, k // 2 % 2, k % 2)
        pad[...] = jnp.zeros_like(pad)
        pad[0:3, :] = offs[k]
        off = pad[...]
        shift = jnp.where(row == 0, place[0] - 1.0, jnp.where(row == 1, place[1] - 1.0, jnp.where(row == 2, place[2] - 1.0, 0.0)))
        pos = off + shift
        src = source_rows(pos, row)
        fa[k] = src
        fb[k] = target_rows(pos, row)
        if k == 0:
            fa[BOXES] = src
        count = counts[k]
        vec = jnp.where(lane < count, probes[k].astype(F32), 0.0).astype(BF16)
        chunks = ((count + CHUNK - 1) // CHUNK).astype(F32)
        p1, p2, p3 = split3(pos)
        rows_a = jnp.where(row == 6, chunks, p1 + pltpu.roll(p2, 3, 0))
        tail = jnp.concatenate([rows_a, p3], axis=0).astype(BF16)
        pay[k, 0:32, :] = vec
        pay[k, 32:48, :] = tail
        for at in range(2):
            for axis in range(3):
                if place[axis] == at:
                    other = [d for d in range(3) if d != axis]
                    out = faces[2 * axis + at]
                    slot = place[other[0]] * 2 + place[other[1]]
                    out[slot, 0:32, :] = vec
                    out[slot, 32:48, :] = tail
        unit = 2.0 * off - 1.0
        t2 = 2.0 * unit * unit - 1.0
        t3 = 2.0 * unit * t2 - unit
        weights = []
        for c in NODES:
            e2 = 2.0 * c * c - 1.0
            e3 = 2.0 * c * e2 - c
            weights.append(0.25 + 0.5 * (c * unit + e2 * t2 + e3 * t3))
        third = jnp.zeros_like(off)
        for d in range(ORDER):
            third = jnp.where(row % 4 == d, weights[d][2:3, :], third)
        seconds = []
        for half in range(2):
            seconds.append(jnp.where(row < 4, weights[2 * half][1:2, :], weights[2 * half + 1][1:2, :]))
        parts = []
        for a in range(ORDER):
            for half in range(2):
                parts.append(weights[a][0:1, :] * seconds[half] * third)
        table = jnp.concatenate(parts, axis=0).astype(BF16)
        tab[k] = table
        moment = lax.dot_general(table, vec, (((1,), (1,)), ((), ())), preferred_element_type=F32)
        momf[:, k * 32:(k + 1) * 32] = moment
    mom[...] = momf[...].astype(BF16)
    pay[BOXES] = jnp.zeros_like(pay[BOXES])


def run_steps(targets, sources_of, chunks_of, dummy, two_way, fa, vec, fb, own, out, tiles, steps, owner):
    at = jnp.int32(0)
    for b in targets:
        for s in sources_of(b):
            count = chunks_of(s)

            def put(c, carry, s=s, b=b, at=at):
                steps[at + c] = s * 8 + c
                owner[(at + c) >> 1] = b
                return carry

            lax.fori_loop(0, count, put, 0)
            at = at + count
        steps[at] = dummy * 8
        at = at + (at & 1)
    for extra in range(6):
        steps[at + extra] = dummy * 8
        owner[(at >> 1) + (extra >> 1)] = targets[0]
    total = at >> 1

    def columns(index):
        return pl.ds(pl.multiple_of((index & 7) * CHUNK, CHUNK), CHUNK)

    def make(t, slot):
        target = fb[owner[t]]
        for h in range(2):
            index = steps[2 * t + h]
            source = fa[index >> 3, :, columns(index)]
            squares = lax.dot_general(source, target, (((0,), (0,)), ((), ())), preferred_element_type=F32)
            tiles[slot, h * CHUNK:(h + 1) * CHUNK, :] = lax.rsqrt(squares).astype(BF16)

    def use(t, slot):
        b = owner[t]
        first = steps[2 * t]
        second = steps[2 * t + 1]
        tile = tiles[slot]
        both = jnp.concatenate([vec[first >> 3, 0:32, columns(first)], vec[second >> 3, 0:32, columns(second)]], axis=1)
        out[b] += jnp.dot(both, tile, preferred_element_type=F32)
        if two_way:
            back = lax.dot_general(own[b, 0:32, :], tile, (((1,), (1,)), ((), ())), preferred_element_type=F32)
            out[first >> 3, :, columns(first)] += back[:, 0:CHUNK]
            out[second >> 3, :, columns(second)] += back[:, CHUNK:]

    make(0, 0)

    def body(k, carry):
        t = 2 * k
        make(t + 1, 1)
        use(t, 0)
        make(t + 2, 0)
        use(t + 1, 1)
        return carry

    lax.fori_loop(0, (total + 1) >> 1, body, 0)


INNER = {4: (0,), 2: (0,), 1: (0,), 6: (2, 4), 5: (1, 4), 3: (1, 2), 7: (3, 5, 6)}


def inner_kernel(targets, sources_of, two_way, counts, fa, pay, fb, acc_in, token, acc, token_out, out, tiles, steps, owner):
    if acc_in is None:
        out[...] = jnp.zeros_like(out)
    else:
        out[0:BOXES] = acc_in[...]
        out[BOXES] = jnp.zeros_like(out[BOXES])
    run_steps(
        targets, sources_of, lambda s: (counts[s] + CHUNK - 1) >> 7, BOXES, two_way,
        fa, pay, fb, pay, out, tiles, steps, owner,
    )
    acc[...] = out[0:BOXES]


def outer_kernel(faces, fb, acc_in, *refs):
    halos = refs[:len(faces)]
    acc, fa, vec, tiles, steps, owner, chunk_no = refs[len(faces):]
    points = fb.shape[-1]
    row = row_ids(points)
    acc[...] = acc_in[...]
    sources = {b: [] for b in range(BOXES)}
    spare = 4 * len(faces)
    for d, (axis, sign) in enumerate(faces):
        halo = halos[d]
        targets = face_boxes(axis, 0 if sign < 0 else 1)
        for i in range(4):
            s = d * 4 + i
            sources[targets[i]].append(s)
            tail = halo[i, 32:48, :].astype(F32)
            rows_a = tail[0:8]
            pos = rows_a + pltpu.roll(rows_a, 5, 0) + tail[8:16]
            pos = jnp.where(row < 3, pos + jnp.where(row == axis, 2.0 * sign, 0.0), 0.0)
            feats = source_rows(pos, row)
            fa[s] = feats
            if s == 0:
                fa[spare] = feats
            vec[s] = halo[i, 0:32, :]
            chunk_no[s] = jnp.max(rows_a[6:7, 0:128]).astype(jnp.int32)
    vec[spare] = jnp.zeros_like(vec[spare])
    order = [b for b in range(BOXES) if sources[b]]
    run_steps(
        order, lambda b: sources[b], lambda s: chunk_no[s], spare, False,
        fa, vec, fb, None, acc, tiles, steps, owner,
    )


def far_kernel(counts, req_box, req_tgt, here, there, near, tab, pay, kv, sums, slab, far_acc, live, sems):
    points = tab.shape[-1]
    first_copy = pltpu.make_async_copy(here, slab.at[pl.ds(0, 32)], sems.at[0])
    second_copy = pltpu.make_async_copy(there, slab.at[pl.ds(32, 32)], sems.at[1])
    first_copy.start()
    second_copy.start()
    my_y = lax.axis_index("gy")
    my_z = lax.axis_index("gz")
    far_acc[...] = jnp.zeros_like(far_acc)

    def keep(i, n):
        live[n] = i
        return n + (req_box[i] >= 0).astype(jnp.int32)

    used = lax.fori_loop(0, 128, keep, jnp.int32(0))
    shape = (64, 64)
    source_q = lax.broadcasted_iota(jnp.int32, shape, 1)
    target_q = lax.broadcasted_iota(jnp.int32, shape, 0)

    def node(index):
        value = jnp.full(shape, 0.5 + 0.5 * NODES[0], F32)
        for a in range(1, ORDER):
            value = jnp.where(index == a, 0.5 + 0.5 * NODES[a], value)
        return value

    gaps = [node((source_q >> s) & 3) - node((target_q >> s) & 3) for s in (4, 2, 0)]
    group = lax.broadcasted_iota(jnp.int32, (64, 256), 1) >> 5
    first_copy.wait()
    second_copy.wait()

    def step(g, carry):
        for u in range(4):
            k = g * 4 + u
            i = live[jnp.minimum(k, used - 1)]
            box = req_box[i]
            tgt = req_tgt[i]
            peer = i >> 1
            peer_y = peer >> 4
            peer_z = peer & 15
            dx = (box >> 2) - (tgt >> 2)
            dy = (peer_y - my_y) * 2 + ((box >> 1) & 1) - ((tgt >> 1) & 1)
            dz = (peer_z - my_z) * 2 + (box & 1) - (tgt & 1)
            ex = gaps[0] + dx.astype(F32)
            ey = gaps[1] + dy.astype(F32)
            ez = gaps[2] + dz.astype(F32)
            coupling = lax.rsqrt(1.0 + ex * ex + ey * ey + ez * ez).astype(BF16)
            rel_y = peer_y ^ my_y
            rel_z = peer_z ^ my_z
            at = (rel_z & 1) * 32 + ((rel_z >> 1) & 3) * 8 + rel_y * 2 + (rel_z >> 3)
            term = jnp.dot(coupling, slab[at], preferred_element_type=F32)
            wanted = jnp.where(k < used, box, -1)
            far_acc[tgt] += jnp.where(group == wanted, term, 0.0)
        return carry

    lax.fori_loop(0, (used + 3) >> 2, step, 0)
    lane = lax.broadcasted_iota(jnp.int32, (1, points), 1)
    total_sum = jnp.zeros((32, 128), F32)
    live_points = jnp.int32(0)
    for b in range(BOXES):
        wide = far_acc[b]
        half = wide[:, 0:128] + wide[:, 128:256]
        half = half + pltpu.roll(half, 64, 1)
        half = half + pltpu.roll(half, 32, 1)
        local_exp = half[:, 0:32].astype(BF16)
        far = lax.dot_general(local_exp, tab[b], (((0,), (0,)), ((), ())), preferred_element_type=F32)
        total = (near[b] + far) * (1.0 / math.sqrt(7.0 * points))
        kv[b] = jnp.where(lane < counts[b], total, 0.0).astype(BF16)
        weighted = pay[b, 0:32, :].astype(F32) * total
        for j in range(points // 128):
            total_sum = total_sum + weighted[:, j * 128:(j + 1) * 128]
        live_points = live_points + counts[b]
    lane128 = lax.broadcasted_iota(jnp.int32, (32, 128), 1)
    sums[...] = jnp.where(lane128 == 0, jnp.sum(total_sum, axis=1, keepdims=True), live_points.astype(F32))


VMEM = pl.BlockSpec(memory_space=pltpu.VMEM)
SMEM = pl.BlockSpec(memory_space=pltpu.SMEM)
ANY = pl.BlockSpec(memory_space=pl.ANY)
PARAMS = pltpu.CompilerParams(vmem_limit_bytes=48 * 2**20)


def xor_permute(value, axis, bits):
    count = lax.axis_size(axis)
    return lax.ppermute(value, axis, [(i, i ^ bits) for i in range(count)])


def shards(offsets, probes, counts, req_box, req_tgt):
    points = offsets.shape[-1]
    offs = offsets.reshape(BOXES, 3, points)
    probe = probes.reshape(BOXES, 32, points)
    count = counts.reshape(BOXES)
    shape = jax.ShapeDtypeStruct
    face = shape((4, ROWS, points), BF16)
    pay, fa, fb, tab, mom, momf, *faces = pl.pallas_call(
        prep_kernel,
        out_shape=[
            shape((BOXES + 1, ROWS, points), BF16),
            shape((BOXES + 1, FEATS, points), BF16),
            shape((BOXES, FEATS, points), BF16),
            shape((BOXES, 64, points), BF16),
            shape((64, 256), BF16),
            shape((64, 256), F32),
        ] + [face] * 6,
        in_specs=[SMEM, VMEM, VMEM],
        out_specs=[VMEM] * 12,
        scratch_shapes=[pltpu.VMEM((8, points), F32)],
        compiler_params=PARAMS,
        name="prep",
    )(count, offs, probe)

    acc_shape = shape((BOXES, 32, points), F32)

    def inner(name, targets, sources_of, two_way, acc, token):
        has_acc = acc is not None
        tokens = [token]

        def kernel(*refs):
            refs = list(refs)
            head = refs[:4]
            rest = refs[4:]
            acc_ref = rest.pop(0) if has_acc else None
            inner_kernel(targets, sources_of, two_way, *head, acc_ref, *rest)

        args = [count, fa, pay, fb] + ([acc] if has_acc else []) + tokens
        return pl.pallas_call(
            kernel,
            out_shape=[acc_shape, shape(token.shape, token.dtype)],
            in_specs=[SMEM, VMEM, VMEM, VMEM] + [VMEM] * has_acc + [ANY],
            out_specs=[VMEM, ANY],
            input_output_aliases={len(args) - 1: 1},
            scratch_shapes=[
                pltpu.VMEM((BOXES + 1, 32, points), F32),
                pltpu.VMEM((2, 2 * CHUNK, points), BF16),
                pltpu.SMEM((256,), jnp.int32),
                pltpu.SMEM((128,), jnp.int32),
            ],
            compiler_params=PARAMS,
            name=name,
        )(*args)

    got = []
    for (axis, sign) in FACES:
        name = ("gx", "gy", "gz")[axis]
        size = lax.axis_size(name)
        if sign < 0:
            pairs = [(i, i + 1) for i in range(size - 1)]
            got.append(lax.ppermute(faces[2 * axis + 1], name, pairs))
        else:
            pairs = [(i + 1, i) for i in range(size - 1)]
            got.append(lax.ppermute(faces[2 * axis], name, pairs))

    block = mom.reshape(1, 64, 256)
    block = jnp.concatenate([block, xor_permute(block, "gz", 8)], axis=0)
    acc, block = inner("self_tiles", list(range(BOXES)), lambda b: [b], False, None, block)
    block = jnp.concatenate([block] + [xor_permute(block, "gy", k) for k in (1, 2, 3)], axis=0)
    acc, block = inner("pairs_low", [1, 2, 4, 3], lambda b: INNER[b], True, acc, block)
    block = jnp.concatenate([block] + [xor_permute(block, "gz", 2 * k) for k in (1, 2, 3)], axis=0)
    acc, block = inner("pairs_high", [5, 6, 7], lambda b: INNER[b], True, acc, block)
    other = xor_permute(block, "gz", 1)

    def outer(name, which, acc):
        nsrc = 4 * len(which) + 1
        return pl.pallas_call(
            functools.partial(outer_kernel, [FACES[d] for d in which]),
            out_shape=acc_shape,
            in_specs=[VMEM] * (2 + len(which)),
            out_specs=VMEM,
            scratch_shapes=[
                pltpu.VMEM((nsrc, FEATS, points), BF16),
                pltpu.VMEM((nsrc, 32, points), BF16),
                pltpu.VMEM((2, 2 * CHUNK, points), BF16),
                pltpu.SMEM((256,), jnp.int32),
                pltpu.SMEM((128,), jnp.int32),
                pltpu.SMEM((32,), jnp.int32),
            ],
            compiler_params=PARAMS,
            name=name,
        )(fb, acc, *[got[d] for d in which])

    acc = outer("face_tiles", [0, 1, 2, 3, 4, 5], acc)
    kv, sums = pl.pallas_call(
        far_kernel,
        out_shape=[shape((BOXES, 32, points), BF16), shape((32, 128), F32)],
        in_specs=[SMEM, SMEM, SMEM, ANY, ANY, VMEM, VMEM, VMEM],
        out_specs=[VMEM, VMEM],
        scratch_shapes=[
            pltpu.VMEM((64, 64, 256), BF16),
            pltpu.VMEM((BOXES, 64, 256), F32),
            pltpu.SMEM((136,), jnp.int32),
            pltpu.SemaphoreType.DMA((2,)),
        ],
        compiler_params=PARAMS,
        name="far_total",
    )(count, req_box.reshape(128), req_tgt.reshape(128), block, other, acc, tab, pay)
    for axis, bits in (("gx", (1, 2)), ("gy", (1, 2)), ("gz", (1, 2, 4, 8))):
        for bit in bits:
            sums = sums + xor_permute(sums, axis, bit)
    quad = sums[:, 0] / sums[:, 1]
    return kv.reshape(probes.shape), quad


def solution(mesh):
    placed = (
        P("gx", "gy", "gz", None, None),
        P("gx", "gy", "gz", None, None),
        P("gx", "gy", "gz"),
        P("gx", "gy", "gz", None, None),
        P("gx", "gy", "gz", None, None),
    )
    return jax.shard_map(
        shards,
        mesh=mesh,
        in_specs=placed,
        out_specs=(P("gx", "gy", "gz", None, None), P()),
        check_vma=False,
    )
```

time: 387 us -> 174 us (0.45)
  the two profiles are of different devices: /device:TPU:1 before, /device:TPU:6 now
where the time goes in v1:
time: 174 us
  starting transfers between devices  62.4 us (36%)
  Pallas kernels  59.8 us (34%)
  waiting for transfers between devices  43.8 us (25%)
  local copies, waits for them, and re-layouts  5.96 us (3%)
    ppermute x16, starting transfers between devices, xor_permute(): return lax.ppermute(value, axis, [(i, i ^ bits) for i in range(count)])  46.8 us
    ppermute x16, waiting for transfers between devices, xor_permute(): return lax.ppermute(value, axis, [(i, i ^ bits) for i in range(count)])  34.4 us
    pallas_call x3, Pallas kernels, inner(): pl.pallas_call(kernel, out_shape=[acc_shape, shape(token.shape, token.dty...  30.5 us
    pallas_call x1, Pallas kernels, outer(): pl.pallas_call(functools.partial(outer_kernel, [FACES[d] for d in which])...  19 us
    ppermute x3, starting transfers between devices, shards(): got.append(lax.ppermute(faces[2 * axis + 1], name, pairs))  9.39 us
    pallas_call x1, Pallas kernels, shards(): pl.pallas_call(far_kernel, out_shape=[shape((BOXES, 32, points), BF16), s...  6.93 us
    ppermute x3, starting transfers between devices, shards(): got.append(lax.ppermute(faces[2 * axis], name, pairs))  6.22 us
    ppermute x3, waiting for transfers between devices, shards(): got.append(lax.ppermute(faces[2 * axis], name, pairs))  5.26 us
  transfers between devices with their start and end apart: 22, of which 17 were waited for; matrix products, arithmetic and copies ran while one was open for 0% of the time, Pallas kernels for 11%

profile of v1, /device:TPU:6, one launch (start us, length us, event | category | flops | bytes accessed | tf_op | source)
XLA Modules:
  0.0 173.7 jit_solution(1164599553992153905)
XLA Ops:
  3.4 3.4 %prep.1 = (bf16[9,48,1024]{2,1,0:T(8,128)(2,1)S(1)}, bf16[9,48,1024]{2,1,0:T(8,128)(2,1)S(1)}, bf16[8,48,1024]{2,1,0:T(8,128)(2,1)S(1)}, bf16[8,64,1024]{2,1,0:T...) custom-call(s32[8]{0:T(128)S(1)} %reshape.26.counts.refs_0_, ...), custom_call_target="tpu_custom_call" | custom-call | tf_op jit(solution)/shard_map/prep/pallas_call | solution.py:319
  6.8 7.2 %collective-permute-start = (bf16[1,64,256]{2,1,0:T(8,128)(2,1)S(1)}, bf16[1,64,256]{2,1,0:T(8,128)(2,1)S(1)}, u32[]{:S(2)}, u32[]{:S(2)}) collective-permute-start(bf16[1,64,256]{2,1,0:T(8,128)(2,1)S(1)} %bitcast.10), channel_id=1, source_target_pairs={{0,8},{1,9},{2,10},{3,11},{4,12},{5,13},{6,14},{7,15},{8,0},{9,1},... | collective-permute-start | bytes 98312 | tf_op jit(solution)/shard_map/ppermute | solution.py:309
  15.9 9.0 %self_tiles.1 = (f32[8,32,1024]{2,1,0:T(8,128)S(1)}, bf16[2,64,256]{2,1,0:T(8,128)(2,1)S(1)}) custom-call(s32[8]{0:T(128)S(1)} %reshape.26.counts.refs_0_, bf16[9,48,1024]{2,1,0:T(8,128)(2,1)S(1)} %get-tuple-element.21.refs_1_, bf16[9,48,1024]{2,1,0:T(8,128)(2,1)S(1)} %get-tuple-element.22.refs_2_.pay, ...), custom_call_target="tpu_custom_call", output_to_operand_aliasing={{1}: (4, {})} | custom-call | tf_op jit(solution)/shard_map/self_tiles/pallas_call | solution.py:350
  25.0 3.9 %collective-permute-start.2 = (bf16[2,64,256]{2,1,0:T(8,128)(2,1)S(1)}, bf16[2,64,256]{2,1,0:T(8,128)(2,1)S(1)}, u32[]{:S(2)}, u32[]{:S(2)}) collective-permute-start(bf16[2,64,256]{2,1,0:T(8,128)(2,1)S(1)} %get-tuple-element.26), channel_id=1, source_target_pairs={{0,32},{16,48},{32,0},{48,16},{1,33},{17,49},{33,1},{49,17},{2,34}... | collective-permute-start | bytes 196616 | tf_op jit(solution)/shard_map/ppermute | solution.py:309
  29.4 4.2 %collective-permute-done.2 = bf16[2,64,256]{2,1,0:T(8,128)(2,1)S(1)} collective-permute-done((bf16[2,64,256]{2,1,0:T(8,128)(2,1)S(1)}, bf16[2,64,256]{2,1,0:T(8,128)(2,1)S(1)}, u32[]{:S(2)}, u32[]{:S(2)}) %collective-permute-start.2) | collective-permute-done | bytes 65568 | tf_op jit(solution)/shard_map/ppermute | solution.py:309
  35.0 9.9 %pairs_low.1 = (f32[8,32,1024]{2,1,0:T(8,128)S(1)}, bf16[8,64,256]{2,1,0:T(8,128)(2,1)S(1)}) custom-call(s32[8]{0:T(128)S(1)} %reshape.26.counts.refs_0_, bf16[9,48,1024]{2,1,0:T(8,128)(2,1)S(1)} %get-tuple-element.21.refs_1_, bf16[9,48,1024]{2,1,0:T(8,128)(2,1)S(1)} %get-tuple-element.22.refs_2_.pay, ...), custom_call_target="tpu_custom_call", output_to_operand_aliasing={{1}: (5, {})} | custom-call | tf_op jit(solution)/shard_map/pairs_low/pallas_call | solution.py:350
  46.0 3.7 %collective-permute-start.6 = (bf16[8,64,256]{2,1,0:T(8,128)(2,1)S(1)}, bf16[8,64,256]{2,1,0:T(8,128)(2,1)S(1)}, u32[]{:S(2)}, u32[]{:S(2)}) collective-permute-start(bf16[8,64,256]{2,1,0:T(8,128)(2,1)S(1)} %get-tuple-element.28), channel_id=1, source_target_pairs={{0,6},{1,7},{2,4},{3,5},{4,2},{5,3},{6,0},{7,1},{8,14},{9,15},{10,... | collective-permute-start | bytes 786440 | tf_op jit(solution)/shard_map/ppermute | solution.py:309
  49.7 3.9 %collective-permute-done.4 = bf16[8,64,256]{2,1,0:T(8,128)(2,1)S(1)} collective-permute-done((bf16[8,64,256]{2,1,0:T(8,128)(2,1)S(1)}, bf16[8,64,256]{2,1,0:T(8,128)(2,1)S(1)}, u32[]{:S(2)}, u32[]{:S(2)}) %collective-permute-start.4) | collective-permute-done | bytes 262176 | tf_op jit(solution)/shard_map/ppermute | solution.py:309
  55.3 2.8 %collective-permute-done.6 = bf16[8,64,256]{2,1,0:T(8,128)(2,1)S(1)} collective-permute-done((bf16[8,64,256]{2,1,0:T(8,128)(2,1)S(1)}, bf16[8,64,256]{2,1,0:T(8,128)(2,1)S(1)}, u32[]{:S(2)}, u32[]{:S(2)}) %collective-permute-start.6) | collective-permute-done | bytes 262176 | tf_op jit(solution)/shard_map/ppermute | solution.py:309
  58.2 11.7 %pairs_high.1 = (f32[8,32,1024]{2,1,0:T(8,128)S(1)}, bf16[32,64,256]{2,1,0:T(8,128)(2,1)S(1)}) custom-call(s32[8]{0:T(128)S(1)} %reshape.26.counts.refs_0_, bf16[9,48,1024]{2,1,0:T(8,128)(2,1)S(1)} %get-tuple-element.21.refs_1_, bf16[9,48,1024]{2,1,0:T(8,128)(2,1)S(1)} %get-tuple-element.22.refs_2_.pay, ...), custom_call_target="tpu_custom_call", output_to_operand_aliasing={{1}: (5, {})} | custom-call | tf_op jit(solution)/shard_map/pairs_high/pallas_call | solution.py:350
  70.8 2.5 %collective-permute-start.10 = (bf16[4,48,1024]{2,1,0:T(8,128)(2,1)S(1)}, bf16[4,48,1024]{2,1,0:T(8,128)(2,1)S(1)}, u32[]{:S(2)}, u32[]{:S(2)}) collective-permute-start(bf16[4,48,1024]{2,1,0:T(8,128)(2,1)S(1)} %get-tuple-element.33), channel_id=1, source_target_pairs={{0,16},{16,32},{32,48},{1,17},{17,33},{33,49},{2,18},{18,34},{34,5... | collective-permute-start | bytes 1179656 | tf_op jit(solution)/shard_map/ppermute | solution.py:372
  76.6 3.6 %collective-permute-start.13 = (bf16[4,48,1024]{2,1,0:T(8,128)(2,1)}, bf16[4,48,1024]{2,1,0:T(8,128)(2,1)}, u32[]{:S(2)}, u32[]{:S(2)}) collective-permute-start(bf16[4,48,1024]{2,1,0:T(8,128)(2,1)} %get-tuple-element.36), channel_id=1, source_target_pairs={{1,0},{2,1},{3,2},{4,3},{5,4},{6,5},{7,6},{8,7},{9,8},{10,9},{11,1... | collective-permute-start | bytes 1179656 | tf_op jit(solution)/shard_map/ppermute | solution.py:375
  81.8 5.0 %collective-permute-start.8 = (bf16[4,48,1024]{2,1,0:T(8,128)(2,1)}, bf16[4,48,1024]{2,1,0:T(8,128)(2,1)}, u32[]{:S(2)}, u32[]{:S(2)}) collective-permute-start(bf16[4,48,1024]{2,1,0:T(8,128)(2,1)} %get-tuple-element.31), channel_id=1, source_target_pairs={{0,64},{64,128},{128,192},{1,65},{65,129},{129,193},{2,66},{66,130... | collective-permute-start | bytes 1179656 | tf_op jit(solution)/shard_map/ppermute | solution.py:372
  91.6 5.3 %collective-permute-done.9.refs_1_ = bf16[4,48,1024]{2,1,0:T(8,128)(2,1)} collective-permute-done((bf16[4,48,1024]{2,1,0:T(8,128)(2,1)}, bf16[4,48,1024]{2,1,0:T(8,128)(2,1)}, u32[]{:S(2)}, u32[]{:S(2)}) %collective-permute-start.9) | collective-permute-done | bytes 393248 | tf_op jit(solution)/shard_map/ppermute | solution.py:375
  98.1 19.0 %face_tiles.1.near = f32[8,32,1024]{2,1,0:T(8,128)S(1)} custom-call(bf16[8,48,1024]{2,1,0:T(8,128)(2,1)S(1)} %get-tuple-element.23.refs_3_.fb, f32[8,32,1024]{2,1,0:T(8,128)S(1)} %copy-done.1, bf16[4,48,1024]{2,1,0:T(8,128)(2,1)} %collective-permute-done.8.refs_0_, bf16[4,48,1024]{2,1,0:T(8,128)(2,1)} %collective-permute-done.9.refs_1_, ...), custom_call_target="tpu_custom_call" | custom-call | tf_op jit(solution)/shard_map/face_tiles/pallas_call | solution.py:388
  117.1 6.9 %far_total.1 = (bf16[8,32,1024]{2,1,0:T(8,128)(2,1)}, f32[32,128]{1,0:T(8,128)S(1)}) custom-call(s32[8]{0:T(128)S(1)} %reshape.26.counts.refs_0_, s32[128]{0:T(128)S(1)} %reshape.27.req_box, s32[128]{0:T(128)S(1)} %reshape.28.req_tgt, bf16[32,64,256]{2,1,0:T(8,128)(2,1)S(1)} %get-tuple-element.29.here, bf16[32,64,256]{2,1,0:T(8,128)(2,1)} %collective-permute-done.7.there, ...), custom_call_target="tpu_custom_call" | custom-call | tf_op jit(solution)/shard_map/far_total/pallas_call | solution.py:406
  124.1 4.2 %collective-permute-start.14 = (f32[32,128]{1,0:T(8,128)S(1)}, f32[32,128]{1,0:T(8,128)S(1)}, u32[]{:S(2)}, u32[]{:S(2)}) collective-permute-start(f32[32,128]{1,0:T(8,128)S(1)} %get-tuple-element.39), channel_id=1, source_target_pairs={{0,64},{64,0},{128,192},{192,128},{1,65},{65,1},{129,193},{193,129... | collective-permute-start | bytes 49160 | tf_op jit(solution)/shard_map/ppermute | solution.py:309
  130.0 3.4 %collective-permute-start.15 = (f32[32,128]{1,0:T(8,128)S(1)}, f32[32,128]{1,0:T(8,128)S(1)}, u32[]{:S(2)}, u32[]{:S(2)}) collective-permute-start(f32[32,128]{1,0:T(8,128)S(1)} %add.24), channel_id=1, source_target_pairs={{0,128},{64,192},{128,0},{192,64},{1,129},{65,193},{129,1},{193,65... | collective-permute-start | bytes 49160 | tf_op jit(solution)/shard_map/ppermute | solution.py:309
  135.2 3.2 %collective-permute-start.16 = (f32[32,128]{1,0:T(8,128)S(1)}, f32[32,128]{1,0:T(8,128)S(1)}, u32[]{:S(2)}, u32[]{:S(2)}) collective-permute-start(f32[32,128]{1,0:T(8,128)S(1)} %add.25), channel_id=1, source_target_pairs={{0,16},{16,0},{32,48},{48,32},{1,17},{17,1},{33,49},{49,33},{2,18}... | collective-permute-start | bytes 49160 | tf_op jit(solution)/shard_map/ppermute | solution.py:309
  140.2 6.3 %collective-permute-start.17 = (f32[32,128]{1,0:T(8,128)S(1)}, f32[32,128]{1,0:T(8,128)S(1)}, u32[]{:S(2)}, u32[]{:S(2)}) collective-permute-start(f32[32,128]{1,0:T(8,128)S(1)} %add.26), channel_id=1, source_target_pairs={{0,32},{16,48},{32,0},{48,16},{1,33},{17,49},{33,1},{49,17},{2,34}... | collective-permute-start | bytes 49160 | tf_op jit(solution)/shard_map/ppermute | solution.py:309
  148.2 4.5 %collective-permute-start.18 = (f32[32,128]{1,0:T(8,128)S(1)}, f32[32,128]{1,0:T(8,128)S(1)}, u32[]{:S(2)}, u32[]{:S(2)}) collective-permute-start(f32[32,128]{1,0:T(8,128)S(1)} %add.27), channel_id=1, source_target_pairs={{0,1},{1,0},{2,3},{3,2},{4,5},{5,4},{6,7},{7,6},{8,9},{9,8},{10,11... | collective-permute-start | bytes 49160 | tf_op jit(solution)/shard_map/ppermute | solution.py:309
  153.5 3.7 %collective-permute-done.19 = f32[32,128]{1,0:T(8,128)S(1)} collective-permute-done((f32[32,128]{1,0:T(8,128)S(1)}, f32[32,128]{1,0:T(8,128)S(1)}, u32[]{:S(2)}, u32[]{:S(2)}) %collective-permute-start.19) | collective-permute-done | bytes 16416 | tf_op jit(solution)/shard_map/ppermute | solution.py:309
  157.3 5.2 %collective-permute-done.20 = f32[32,128]{1,0:T(8,128)S(1)} collective-permute-done((f32[32,128]{1,0:T(8,128)S(1)}, f32[32,128]{1,0:T(8,128)S(1)}, u32[]{:S(2)}, u32[]{:S(2)}) %collective-permute-start.20) | collective-permute-done | bytes 16416 | tf_op jit(solution)/shard_map/ppermute | solution.py:309
  162.5 8.8 %collective-permute-start.21 = (f32[32,128]{1,0:T(8,128)S(1)}, f32[32,128]{1,0:T(8,128)S(1)}, u32[]{:S(2)}, u32[]{:S(2)}) collective-permute-start(f32[32,128]{1,0:T(8,128)S(1)} %add.30), channel_id=1, source_target_pairs={{0,8},{1,9},{2,10},{3,11},{4,12},{5,13},{6,14},{7,15},{8,0},{9,1},... | collective-permute-start | bytes 49160 | tf_op jit(solution)/shard_map/ppermute | solution.py:309
  (56 shorter events, 31.8 us)
Async XLA Ops:
  6.8 9.1 %collective-permute-start = (bf16[1,64,256]{2,1,0:T(8,128)(2,1)S(1)}, bf16[1,64,256]{2,1,0:T(8,128)(2,1)S(1)}, u32[]{:S(2)}, u32[]{:S(2)}) collective-permute-start(bf16[1,64,256]{2,1,0:T(8,128)(2,1)S(1)} %bitcast.10), channel_id=1, source_target_pairs={{0,8},{1,9},{2,10},{3,11},{4,12},{5,13},{6,14},{7,15},{8,0},{9,1},... | collective-permute-start | bytes 98312 | tf_op jit(solution)/shard_map/ppermute | solution.py:309
  24.9 4.5 %collective-permute-start.1 = (bf16[2,64,256]{2,1,0:T(8,128)(2,1)S(1)}, bf16[2,64,256]{2,1,0:T(8,128)(2,1)S(1)}, u32[]{:S(2)}, u32[]{:S(2)}) collective-permute-start(bf16[2,64,256]{2,1,0:T(8,128)(2,1)S(1)} %get-tuple-element.26), channel_id=1, source_target_pairs={{0,16},{16,0},{32,48},{48,32},{1,17},{17,1},{33,49},{49,33},{2,18}... | collective-permute-start | bytes 196616 | tf_op jit(solution)/shard_map/ppermute | solution.py:309
  25.0 8.6 %collective-permute-start.2 = (bf16[2,64,256]{2,1,0:T(8,128)(2,1)S(1)}, bf16[2,64,256]{2,1,0:T(8,128)(2,1)S(1)}, u32[]{:S(2)}, u32[]{:S(2)}) collective-permute-start(bf16[2,64,256]{2,1,0:T(8,128)(2,1)S(1)} %get-tuple-element.26), channel_id=1, source_target_pairs={{0,32},{16,48},{32,0},{48,16},{1,33},{17,49},{33,1},{49,17},{2,34}... | collective-permute-start | bytes 196616 | tf_op jit(solution)/shard_map/ppermute | solution.py:309
  28.9 6.1 %collective-permute-start.3 = (bf16[2,64,256]{2,1,0:T(8,128)(2,1)S(1)}, bf16[2,64,256]{2,1,0:T(8,128)(2,1)S(1)}, u32[]{:S(2)}, u32[]{:S(2)}) collective-permute-start(bf16[2,64,256]{2,1,0:T(8,128)(2,1)S(1)} %get-tuple-element.26), channel_id=1, source_target_pairs={{0,48},{16,32},{32,16},{48,0},{1,49},{17,33},{33,17},{49,1},{2,50}... | collective-permute-start | bytes 196616 | tf_op jit(solution)/shard_map/ppermute | solution.py:309
  44.9 8.7 %collective-permute-start.4 = (bf16[8,64,256]{2,1,0:T(8,128)(2,1)S(1)}, bf16[8,64,256]{2,1,0:T(8,128)(2,1)S(1)}, u32[]{:S(2)}, u32[]{:S(2)}) collective-permute-start(bf16[8,64,256]{2,1,0:T(8,128)(2,1)S(1)} %get-tuple-element.28), channel_id=1, source_target_pairs={{0,2},{1,3},{2,0},{3,1},{4,6},{5,7},{6,4},{7,5},{8,10},{9,11},{10,... | collective-permute-start | bytes 786440 | tf_op jit(solution)/shard_map/ppermute | solution.py:309
  45.0 10.3 %collective-permute-start.5 = (bf16[8,64,256]{2,1,0:T(8,128)(2,1)S(1)}, bf16[8,64,256]{2,1,0:T(8,128)(2,1)S(1)}, u32[]{:S(2)}, u32[]{:S(2)}) collective-permute-start(bf16[8,64,256]{2,1,0:T(8,128)(2,1)S(1)} %get-tuple-element.28), channel_id=1, source_target_pairs={{0,4},{1,5},{2,6},{3,7},{4,0},{5,1},{6,2},{7,3},{8,12},{9,13},{10,... | collective-permute-start | bytes 786440 | tf_op jit(solution)/shard_map/ppermute | solution.py:309
  46.0 12.0 %collective-permute-start.6 = (bf16[8,64,256]{2,1,0:T(8,128)(2,1)S(1)}, bf16[8,64,256]{2,1,0:T(8,128)(2,1)S(1)}, u32[]{:S(2)}, u32[]{:S(2)}) collective-permute-start(bf16[8,64,256]{2,1,0:T(8,128)(2,1)S(1)} %get-tuple-element.28), channel_id=1, source_target_pairs={{0,6},{1,7},{2,4},{3,5},{4,2},{5,3},{6,0},{7,1},{8,14},{9,15},{10,... | collective-permute-start | bytes 786440 | tf_op jit(solution)/shard_map/ppermute | solution.py:309
  70.8 46.2 %collective-permute-start.7 = (bf16[32,64,256]{2,1,0:T(8,128)(2,1)S(1)}, bf16[32,64,256]{2,1,0:T(8,128)(2,1)}, u32[]{:S(2)}, u32[]{:S(2)}) collective-permute-start(bf16[32,64,256]{2,1,0:T(8,128)(2,1)S(1)} %get-tuple-element.29.here), channel_id=1, source_target_pairs={{0,1},{1,0},{2,3},{3,2},{4,5},{5,4},{6,7},{7,6},{8,9},{9,8},{10,11... | collective-permute-start | bytes 3145736 | tf_op jit(solution)/shard_map/ppermute | solution.py:309
  70.8 11.0 %collective-permute-start.10 = (bf16[4,48,1024]{2,1,0:T(8,128)(2,1)S(1)}, bf16[4,48,1024]{2,1,0:T(8,128)(2,1)S(1)}, u32[]{:S(2)}, u32[]{:S(2)}) collective-permute-start(bf16[4,48,1024]{2,1,0:T(8,128)(2,1)S(1)} %get-tuple-element.33), channel_id=1, source_target_pairs={{0,16},{16,32},{32,48},{1,17},{17,33},{33,49},{2,18},{18,34},{34,5... | collective-permute-start | bytes 1179656 | tf_op jit(solution)/shard_map/ppermute | solution.py:372
  73.3 13.5 %collective-permute-start.11 = (bf16[4,48,1024]{2,1,0:T(8,128)(2,1)S(1)}, bf16[4,48,1024]{2,1,0:T(8,128)(2,1)S(1)}, u32[]{:S(2)}, u32[]{:S(2)}) collective-permute-start(bf16[4,48,1024]{2,1,0:T(8,128)(2,1)S(1)} %get-tuple-element.34), channel_id=1, source_target_pairs={{16,0},{32,16},{48,32},{17,1},{33,17},{49,33},{18,2},{34,18},{50,3... | collective-permute-start | bytes 1179656 | tf_op jit(solution)/shard_map/ppermute | solution.py:375
  74.6 14.5 %collective-permute-start.12 = (bf16[4,48,1024]{2,1,0:T(8,128)(2,1)}, bf16[4,48,1024]{2,1,0:T(8,128)(2,1)}, u32[]{:S(2)}, u32[]{:S(2)}) collective-permute-start(bf16[4,48,1024]{2,1,0:T(8,128)(2,1)} %get-tuple-element.35), channel_id=1, source_target_pairs={{0,1},{1,2},{2,3},{3,4},{4,5},{5,6},{6,7},{7,8},{8,9},{9,10},{10,1... | collective-permute-start | bytes 1179656 | tf_op jit(solution)/shard_map/ppermute | solution.py:372
  76.6 12.6 %collective-permute-start.13 = (bf16[4,48,1024]{2,1,0:T(8,128)(2,1)}, bf16[4,48,1024]{2,1,0:T(8,128)(2,1)}, u32[]{:S(2)}, u32[]{:S(2)}) collective-permute-start(bf16[4,48,1024]{2,1,0:T(8,128)(2,1)} %get-tuple-element.36), channel_id=1, source_target_pairs={{1,0},{2,1},{3,2},{4,3},{5,4},{6,5},{7,6},{8,7},{9,8},{10,9},{11,1... | collective-permute-start | bytes 1179656 | tf_op jit(solution)/shard_map/ppermute | solution.py:375
  81.8 6.3 %copy-start.4 = (s32[1,1,1,64,2]{3,4,2,1,0:T(2,128)S(1)}, s32[1,1,1,64,2]{3,4,2,1,0:T(2,128)}, u32[]{:S(2)}) copy-start(s32[1,1,1,64,2]{3,4,2,1,0:T(2,128)} %param.8) | copy-start | bytes 1540
  81.8 9.8 %collective-permute-start.8 = (bf16[4,48,1024]{2,1,0:T(8,128)(2,1)}, bf16[4,48,1024]{2,1,0:T(8,128)(2,1)}, u32[]{:S(2)}, u32[]{:S(2)}) collective-permute-start(bf16[4,48,1024]{2,1,0:T(8,128)(2,1)} %get-tuple-element.31), channel_id=1, source_target_pairs={{0,64},{64,128},{128,192},{1,65},{65,129},{129,193},{2,66},{66,130... | collective-permute-start | bytes 1179656 | tf_op jit(solution)/shard_map/ppermute | solution.py:372
  86.8 10.1 %collective-permute-start.9 = (bf16[4,48,1024]{2,1,0:T(8,128)(2,1)}, bf16[4,48,1024]{2,1,0:T(8,128)(2,1)}, u32[]{:S(2)}, u32[]{:S(2)}) collective-permute-start(bf16[4,48,1024]{2,1,0:T(8,128)(2,1)} %get-tuple-element.32), channel_id=1, source_target_pairs={{64,0},{128,64},{192,128},{65,1},{129,65},{193,129},{66,2},{130,66... | collective-permute-start | bytes 1179656 | tf_op jit(solution)/shard_map/ppermute | solution.py:375
  98.1 19.0 %copy-start.2 = (bf16[8,64,1024]{2,1,0:T(8,128)(2,1)S(1)}, bf16[8,64,1024]{2,1,0:T(8,128)(2,1)}, u32[]{:S(2)}) copy-start(bf16[8,64,1024]{2,1,0:T(8,128)(2,1)} %get-tuple-element.37.tab) | copy-start | bytes 3145732
  124.1 5.9 %collective-permute-start.14 = (f32[32,128]{1,0:T(8,128)S(1)}, f32[32,128]{1,0:T(8,128)S(1)}, u32[]{:S(2)}, u32[]{:S(2)}) collective-permute-start(f32[32,128]{1,0:T(8,128)S(1)} %get-tuple-element.39), channel_id=1, source_target_pairs={{0,64},{64,0},{128,192},{192,128},{1,65},{65,1},{129,193},{193,129... | collective-permute-start | bytes 49160 | tf_op jit(solution)/shard_map/ppermute | solution.py:309
  130.0 5.2 %collective-permute-start.15 = (f32[32,128]{1,0:T(8,128)S(1)}, f32[32,128]{1,0:T(8,128)S(1)}, u32[]{:S(2)}, u32[]{:S(2)}) collective-permute-start(f32[32,128]{1,0:T(8,128)S(1)} %add.24), channel_id=1, source_target_pairs={{0,128},{64,192},{128,0},{192,64},{1,129},{65,193},{129,1},{193,65... | collective-permute-start | bytes 49160 | tf_op jit(solution)/shard_map/ppermute | solution.py:309
  135.2 4.9 %collective-permute-start.16 = (f32[32,128]{1,0:T(8,128)S(1)}, f32[32,128]{1,0:T(8,128)S(1)}, u32[]{:S(2)}, u32[]{:S(2)}) collective-permute-start(f32[32,128]{1,0:T(8,128)S(1)} %add.25), channel_id=1, source_target_pairs={{0,16},{16,0},{32,48},{48,32},{1,17},{17,1},{33,49},{49,33},{2,18}... | collective-permute-start | bytes 49160 | tf_op jit(solution)/shard_map/ppermute | solution.py:309
  140.2 8.0 %collective-permute-start.17 = (f32[32,128]{1,0:T(8,128)S(1)}, f32[32,128]{1,0:T(8,128)S(1)}, u32[]{:S(2)}, u32[]{:S(2)}) collective-permute-start(f32[32,128]{1,0:T(8,128)S(1)} %add.26), channel_id=1, source_target_pairs={{0,32},{16,48},{32,0},{48,16},{1,33},{17,49},{33,1},{49,17},{2,34}... | collective-permute-start | bytes 49160 | tf_op jit(solution)/shard_map/ppermute | solution.py:309
  148.2 5.3 %collective-permute-start.18 = (f32[32,128]{1,0:T(8,128)S(1)}, f32[32,128]{1,0:T(8,128)S(1)}, u32[]{:S(2)}, u32[]{:S(2)}) collective-permute-start(f32[32,128]{1,0:T(8,128)S(1)} %add.27), channel_id=1, source_target_pairs={{0,1},{1,0},{2,3},{3,2},{4,5},{5,4},{6,7},{7,6},{8,9},{9,8},{10,11... | collective-permute-start | bytes 49160 | tf_op jit(solution)/shard_map/ppermute | solution.py:309
  153.5 3.7 %collective-permute-start.19 = (f32[32,128]{1,0:T(8,128)S(1)}, f32[32,128]{1,0:T(8,128)S(1)}, u32[]{:S(2)}, u32[]{:S(2)}) collective-permute-start(f32[32,128]{1,0:T(8,128)S(1)} %add.28), channel_id=1, source_target_pairs={{0,2},{1,3},{2,0},{3,1},{4,6},{5,7},{6,4},{7,5},{8,10},{9,11},{10,... | collective-permute-start | bytes 49160 | tf_op jit(solution)/shard_map/ppermute | solution.py:309
  157.3 5.2 %collective-permute-start.20 = (f32[32,128]{1,0:T(8,128)S(1)}, f32[32,128]{1,0:T(8,128)S(1)}, u32[]{:S(2)}, u32[]{:S(2)}) collective-permute-start(f32[32,128]{1,0:T(8,128)S(1)} %add.29), channel_id=1, source_target_pairs={{0,4},{1,5},{2,6},{3,7},{4,0},{5,1},{6,2},{7,3},{8,12},{9,13},{10,... | collective-permute-start | bytes 49160 | tf_op jit(solution)/shard_map/ppermute | solution.py:309
  162.5 10.5 %collective-permute-start.21 = (f32[32,128]{1,0:T(8,128)S(1)}, f32[32,128]{1,0:T(8,128)S(1)}, u32[]{:S(2)}, u32[]{:S(2)}) collective-permute-start(f32[32,128]{1,0:T(8,128)S(1)} %add.30), channel_id=1, source_target_pairs={{0,8},{1,9},{2,10},{3,11},{4,12},{5,13},{6,14},{7,15},{8,0},{9,1},... | collective-permute-start | bytes 49160 | tf_op jit(solution)/shard_map/ppermute | solution.py:309
  (4 other events, 3.9 us)

commit v2 on v1

--- a/solution.py
+++ b/solution.py
@@ -178,7 +178,7 @@
 INNER = {4: (0,), 2: (0,), 1: (0,), 6: (2, 4), 5: (1, 4), 3: (1, 2), 7: (3, 5, 6)}
 
 
-def inner_kernel(targets, sources_of, two_way, counts, fa, pay, fb, acc_in, token, acc, token_out, out, tiles, steps, owner):
+def inner_kernel(targets, sources_of, two_way, counts, fa, pay, fb, acc_in, after, acc, done, out, tiles, steps, owner):
     if acc_in is None:
         out[...] = jnp.zeros_like(out)
     else:
@@ -189,9 +189,10 @@
         fa, pay, fb, pay, out, tiles, steps, owner,
     )
     acc[...] = out[0:BOXES]
-
-
-def outer_kernel(faces, fb, acc_in, *refs):
+    done[...] = jnp.zeros_like(done)
+
+
+def outer_kernel(faces, fb, acc_in, after, *refs):
     halos = refs[:len(faces)]
     acc, fa, vec, tiles, steps, owner, chunk_no = refs[len(faces):]
     points = fb.shape[-1]
@@ -295,13 +296,31 @@
             total_sum = total_sum + weighted[:, j * 128:(j + 1) * 128]
         live_points = live_points + counts[b]
     lane128 = lax.broadcasted_iota(jnp.int32, (32, 128), 1)
-    sums[...] = jnp.where(lane128 == 0, jnp.sum(total_sum, axis=1, keepdims=True), live_points.astype(F32))
+    row128 = lax.broadcasted_iota(jnp.int32, (32, 128), 0)
+    spread = jnp.where(lane128 == row128, jnp.sum(total_sum, axis=1, keepdims=True), 0.0)
+    flat = jnp.sum(spread, axis=0, keepdims=True)
+    sums[...] = jnp.where(lane128[0:1] == 32, live_points.astype(F32), flat)
 
 
 VMEM = pl.BlockSpec(memory_space=pltpu.VMEM)
 SMEM = pl.BlockSpec(memory_space=pltpu.SMEM)
 ANY = pl.BlockSpec(memory_space=pl.ANY)
-PARAMS = pltpu.CompilerParams(vmem_limit_bytes=48 * 2**20)
+PARAMS = pltpu.CompilerParams(vmem_limit_bytes=20 * 2**20)
+
+
+COST = pl.CostEstimate(flops=12 * 10**9, bytes_accessed=4 * 2**20, transcendentals=10**7)
+
+
+def join(name, *arrays):
+    return pl.pallas_call(
+        lambda *refs: None,
+        out_shape=[jax.ShapeDtypeStruct(a.shape, a.dtype) for a in arrays],
+        in_specs=[ANY] * len(arrays),
+        out_specs=[ANY] * len(arrays),
+        input_output_aliases={i: i for i in range(len(arrays))},
+        compiler_params=pltpu.CompilerParams(vmem_limit_bytes=2**20),
+        name=name,
+    )(*arrays)
 
 
 def xor_permute(value, axis, bits):
@@ -335,9 +354,8 @@
 
     acc_shape = shape((BOXES, 32, points), F32)
 
-    def inner(name, targets, sources_of, two_way, acc, token):
+    def inner(name, targets, sources_of, two_way, acc, after):
         has_acc = acc is not None
-        tokens = [token]
 
         def kernel(*refs):
             refs = list(refs)
@@ -346,13 +364,12 @@
             acc_ref = rest.pop(0) if has_acc else None
             inner_kernel(targets, sources_of, two_way, *head, acc_ref, *rest)
 
-        args = [count, fa, pay, fb] + ([acc] if has_acc else []) + tokens
+        args = [count, fa, pay, fb] + ([acc] if has_acc else []) + [after]
         return pl.pallas_call(
             kernel,
-            out_shape=[acc_shape, shape(token.shape, token.dtype)],
+            out_shape=[acc_shape, shape((8, 128), F32)],
             in_specs=[SMEM, VMEM, VMEM, VMEM] + [VMEM] * has_acc + [ANY],
-            out_specs=[VMEM, ANY],
-            input_output_aliases={len(args) - 1: 1},
+            out_specs=[VMEM, VMEM],
             scratch_shapes=[
                 pltpu.VMEM((BOXES + 1, 32, points), F32),
                 pltpu.VMEM((2, 2 * CHUNK, points), BF16),
@@ -360,35 +377,43 @@
                 pltpu.SMEM((128,), jnp.int32),
             ],
             compiler_params=PARAMS,
+            cost_estimate=COST,
             name=name,
         )(*args)
 
-    got = []
-    for (axis, sign) in FACES:
+    def halo(d):
+        axis, sign = FACES[d]
         name = ("gx", "gy", "gz")[axis]
         size = lax.axis_size(name)
         if sign < 0:
-            pairs = [(i, i + 1) for i in range(size - 1)]
-            got.append(lax.ppermute(faces[2 * axis + 1], name, pairs))
-        else:
-            pairs = [(i + 1, i) for i in range(size - 1)]
-            got.append(lax.ppermute(faces[2 * axis], name, pairs))
-
+            return lax.ppermute(faces[2 * axis + 1], name, [(i, i + 1) for i in range(size - 1)])
+        return lax.ppermute(faces[2 * axis], name, [(i + 1, i) for i in range(size - 1)])
+
+    got = [None] * 6
     block = mom.reshape(1, 64, 256)
-    block = jnp.concatenate([block, xor_permute(block, "gz", 8)], axis=0)
-    acc, block = inner("self_tiles", list(range(BOXES)), lambda b: [b], False, None, block)
-    block = jnp.concatenate([block] + [xor_permute(block, "gy", k) for k in (1, 2, 3)], axis=0)
-    acc, block = inner("pairs_low", [1, 2, 4, 3], lambda b: INNER[b], True, acc, block)
-    block = jnp.concatenate([block] + [xor_permute(block, "gz", 2 * k) for k in (1, 2, 3)], axis=0)
-    acc, block = inner("pairs_high", [5, 6, 7], lambda b: INNER[b], True, acc, block)
+    twin = xor_permute(block, "gz", 8)
+    got[0], got[1] = halo(0), halo(1)
+    acc, tick = inner("self_tiles", list(range(BOXES)), lambda b: [b], False, None, mom)
+    tick, twin, got[0], got[1] = join("join_first", tick, twin, got[0], got[1])
+    block = jnp.concatenate([block, twin], axis=0)
+    more = [xor_permute(block, "gy", k) for k in (1, 2, 3)]
+    got[4], got[5] = halo(4), halo(5)
+    acc, tick = inner("pairs_low", [1, 2, 4, 3], lambda b: INNER[b], True, acc, tick)
+    tick, got[4], got[5], *more = join("join_second", tick, got[4], got[5], *more)
+    block = jnp.concatenate([block] + more, axis=0)
+    more = [xor_permute(block, "gz", 2 * k) for k in (1, 2, 3)]
+    got[2], got[3] = halo(2), halo(3)
+    acc, tick = inner("pairs_high", [5, 6, 7], lambda b: INNER[b], True, acc, tick)
+    tick, got[2], got[3], *more = join("join_third", tick, got[2], got[3], *more)
+    block = jnp.concatenate([block] + more, axis=0)
     other = xor_permute(block, "gz", 1)
 
-    def outer(name, which, acc):
+    def outer(name, which, acc, after):
         nsrc = 4 * len(which) + 1
         return pl.pallas_call(
             functools.partial(outer_kernel, [FACES[d] for d in which]),
             out_shape=acc_shape,
-            in_specs=[VMEM] * (2 + len(which)),
+            in_specs=[VMEM, VMEM, ANY] + [VMEM] * len(which),
             out_specs=VMEM,
             scratch_shapes=[
                 pltpu.VMEM((nsrc, FEATS, points), BF16),
@@ -399,13 +424,14 @@
                 pltpu.SMEM((32,), jnp.int32),
             ],
             compiler_params=PARAMS,
+            cost_estimate=COST,
             name=name,
-        )(fb, acc, *[got[d] for d in which])
-
-    acc = outer("face_tiles", [0, 1, 2, 3, 4, 5], acc)
+        )(fb, acc, after, *[got[d] for d in which])
+
+    acc = outer("face_tiles", [0, 1, 2, 3, 4, 5], acc, tick)
     kv, sums = pl.pallas_call(
         far_kernel,
-        out_shape=[shape((BOXES, 32, points), BF16), shape((32, 128), F32)],
+        out_shape=[shape((BOXES, 32, points), BF16), shape((1, 128), F32)],
         in_specs=[SMEM, SMEM, SMEM, ANY, ANY, VMEM, VMEM, VMEM],
         out_specs=[VMEM, VMEM],
         scratch_shapes=[
@@ -417,10 +443,11 @@
         compiler_params=PARAMS,
         name="far_total",
     )(count, req_box.reshape(128), req_tgt.reshape(128), block, other, acc, tab, pay)
-    for axis, bits in (("gx", (1, 2)), ("gy", (1, 2)), ("gz", (1, 2, 4, 8))):
-        for bit in bits:
-            sums = sums + xor_permute(sums, axis, bit)
-    quad = sums[:, 0] / sums[:, 1]
+    devices = lax.axis_size("gx") * lax.axis_size("gy") * lax.axis_size("gz")
+    spread = jnp.broadcast_to(sums, (devices, 128))
+    gathered = lax.all_to_all(spread, ("gx", "gy", "gz"), 0, 0, tiled=True)
+    whole = jnp.sum(gathered, axis=0)
+    quad = whole[0:32] / whole[32]
     return kv.reshape(probes.shape), quad
 
 

time: 174 us -> 136 us (0.78)
  the two profiles are of different devices: /device:TPU:6 before, /device:TPU:1 now
where the time goes in v2:
time: 136 us
  Pallas kernels  58.1 us (43%)
  blocking collectives  33.7 us (25%)
  starting transfers between devices  33.1 us (24%)
  local copies, waits for them, and re-layouts  8.56 us (6%)
    all_to_all x1, blocking collectives, shards(): gathered = lax.all_to_all(spread, ('gx', 'gy', 'gz'), 0, 0, tiled=True)  33.7 us
    pallas_call x3, Pallas kernels, inner(): pl.pallas_call(kernel, out_shape=[acc_shape, shape((8, 128), F32)], in_sp...  29.6 us
    pallas_call x1, Pallas kernels, outer(): pl.pallas_call(functools.partial(outer_kernel, [FACES[d] for d in which])...  18.6 us
    ppermute x8, starting transfers between devices, xor_permute(): return lax.ppermute(value, axis, [(i, i ^ bits) for i in range(count)])  17.8 us
    ppermute x3, starting transfers between devices, halo(): lax.ppermute(faces[2 * axis + 1], name, [(i, i + 1) for i in range(size -...  10.7 us
    unnamed x39, local copies, waits for them, and re-layouts  6.82 us
    pallas_call x1, Pallas kernels, shards(): pl.pallas_call(far_kernel, out_shape=[shape((BOXES, 32, points), BF16), s...  6.74 us
    ppermute x3, starting transfers between devices, halo(): lax.ppermute(faces[2 * axis], name, [(i + 1, i) for i in range(size - 1)])  4.51 us
  transfers between devices with their start and end apart: 14, of which 1 were waited for; matrix products, arithmetic and copies ran while one was open for 1% of the time, Pallas kernels for 35%

profile of v2, /device:TPU:1, one launch (start us, length us, event | category | flops | bytes accessed | tf_op | source)
XLA Modules:
  0.0 136.1 jit_solution(5209020987486664948)
XLA Ops:
  2.4 1.0 copy-done
  3.4 3.1 %prep.1 = (bf16[9,48,1024]{2,1,0:T(8,128)(2,1)S(1)}, bf16[9,48,1024]{2,1,0:T(8,128)(2,1)S(1)}, bf16[8,48,1024]{2,1,0:T(8,128)(2,1)S(1)}, bf16[8,64,1024]{2,1,0:T...) custom-call(s32[8]{0:T(128)S(1)} %reshape.31.counts.refs_0_, ...), custom_call_target="tpu_custom_call" | custom-call | tf_op jit(solution)/shard_map/prep/pallas_call | solution.py:338
  6.5 7.8 %collective-permute-start = (bf16[1,64,256]{2,1,0:T(8,128)(2,1)S(1)}, bf16[1,64,256]{2,1,0:T(8,128)(2,1)S(1)}, u32[]{:S(2)}, u32[]{:S(2)}) collective-permute-start(bf16[1,64,256]{2,1,0:T(8,128)(2,1)S(1)} %bitcast.15), channel_id=1, source_target_pairs={{0,8},{1,9},{2,10},{3,11},{4,12},{5,13},{6,14},{7,15},{8,0},{9,1},... | collective-permute-start | bytes 98312 | tf_op jit(solution)/shard_map/ppermute | solution.py:328
  14.4 3.2 %collective-permute-start.1 = (bf16[4,48,1024]{2,1,0:T(8,128)(2,1)}, bf16[4,48,1024]{2,1,0:T(8,128)(2,1)S(1)}, u32[]{:S(2)}, u32[]{:S(2)}) collective-permute-start(bf16[4,48,1024]{2,1,0:T(8,128)(2,1)} %get-tuple-element.42), channel_id=1, source_target_pairs={{0,64},{64,128},{128,192},{1,65},{65,129},{129,193},{2,66},{66,130... | collective-permute-start | bytes 1179656 | tf_op jit(solution)/shard_map/ppermute | solution.py:389
  17.6 1.3 collective-permute-start.2
  18.9 4.2 %collective-permute-start.3 = (bf16[4,48,1024]{2,1,0:T(8,128)(2,1)}, bf16[4,48,1024]{2,1,0:T(8,128)(2,1)}, u32[]{:S(2)}, u32[]{:S(2)}) collective-permute-start(bf16[4,48,1024]{2,1,0:T(8,128)(2,1)} %get-tuple-element.48), channel_id=1, source_target_pairs={{0,1},{1,2},{2,3},{3,4},{4,5},{5,6},{6,7},{7,8},{8,9},{9,10},{10,1... | collective-permute-start | bytes 1179656 | tf_op jit(solution)/shard_map/ppermute | solution.py:389
  23.1 1.9 %collective-permute-start.4 = (bf16[4,48,1024]{2,1,0:T(8,128)(2,1)}, bf16[4,48,1024]{2,1,0:T(8,128)(2,1)}, u32[]{:S(2)}, u32[]{:S(2)}) collective-permute-start(bf16[4,48,1024]{2,1,0:T(8,128)(2,1)} %get-tuple-element.49), channel_id=1, source_target_pairs={{1,0},{2,1},{3,2},{4,3},{5,4},{6,5},{7,6},{8,7},{9,8},{10,9},{11,1... | collective-permute-start | bytes 1179656 | tf_op jit(solution)/shard_map/ppermute | solution.py:390
  25.1 9.0 %self_tiles.1 = (f32[8,32,1024]{2,1,0:T(8,128)S(1)}, f32[8,128]{1,0:T(8,128)S(1)}) custom-call(s32[8]{0:T(128)S(1)} %reshape.31.counts.refs_0_, bf16[9,48,1024]{2,1,0:T(8,128)(2,1)S(1)} %get-tuple-element.38.refs_1_, bf16[9,48,1024]{2,1,0:T(8,128)(2,1)S(1)} %get-tuple-element.39.refs_2_.pay, bf16[8,48,1024]{2,1,0:T(8,128)(2,1)S(1)} %get-tuple-element.40.refs_3_.fb, ...), custom_call_target="tpu_custom_call" | custom-call | flops 12000000000 | bytes 4194304 | tf_op jit(solution)/shard_map/self_tiles/pallas_call | solution.py:368
  34.1 1.0 copy-done.10
  36.8 1.4 %collective-permute-start.5 = (bf16[2,64,256]{2,1,0:T(8,128)(2,1)S(1)}, bf16[2,64,256]{2,1,0:T(8,128)(2,1)S(1)}, u32[]{:S(2)}, u32[]{:S(2)}) collective-permute-start(bf16[2,64,256]{2,1,0:T(8,128)(2,1)S(1)} %pad_maximum_fusion), channel_id=1, source_target_pairs={{0,16},{16,0},{32,48},{48,32},{1,17},{17,1},{33,49},{49,33},{2,18}... | collective-permute-start | bytes 196616 | tf_op jit(solution)/shard_map/ppermute | solution.py:328
  38.2 2.2 %collective-permute-start.7 = (bf16[2,64,256]{2,1,0:T(8,128)(2,1)S(1)}, bf16[2,64,256]{2,1,0:T(8,128)(2,1)S(1)}, u32[]{:S(2)}, u32[]{:S(2)}) collective-permute-start(bf16[2,64,256]{2,1,0:T(8,128)(2,1)S(1)} %pad_maximum_fusion), channel_id=1, source_target_pairs={{0,48},{16,32},{32,16},{48,0},{1,49},{17,33},{33,17},{49,1},{2,50}... | collective-permute-start | bytes 196616 | tf_op jit(solution)/shard_map/ppermute | solution.py:328
  40.4 1.1 copy-done.4
  41.6 1.2 copy-done.11
  42.8 9.0 %pairs_low.1 = (f32[8,32,1024]{2,1,0:T(8,128)S(1)}, f32[8,128]{1,0:T(8,128)S(1)}) custom-call(s32[8]{0:T(128)S(1)} %reshape.31.counts.refs_0_, bf16[9,48,1024]{2,1,0:T(8,128)(2,1)S(1)} %copy-done.2, bf16[9,48,1024]{2,1,0:T(8,128)(2,1)S(1)} %get-tuple-element.39.refs_2_.pay, bf16[8,48,1024]{2,1,0:T(8,128)(2,1)S(1)} %copy-done.4, ...), custom_call_target="tpu_custom_call" | custom-call | flops 12000000000 | bytes 4194304 | tf_op jit(solution)/shard_map/pairs_low/pallas_call | solution.py:368
  51.9 3.3 %collective-permute-start.8 = (bf16[4,48,1024]{2,1,0:T(8,128)(2,1)S(1)}, bf16[4,48,1024]{2,1,0:T(8,128)(2,1)S(1)}, u32[]{:S(2)}, u32[]{:S(2)}) collective-permute-start(bf16[4,48,1024]{2,1,0:T(8,128)(2,1)S(1)} %copy-done.9), channel_id=1, source_target_pairs={{0,16},{16,32},{32,48},{1,17},{17,33},{33,49},{2,18},{18,34},{34,5... | collective-permute-start | bytes 1179656 | tf_op jit(solution)/shard_map/ppermute | solution.py:389
  55.2 1.3 collective-permute-start.9
  57.2 2.0 %collective-permute-start.11 = (bf16[8,64,256]{2,1,0:T(8,128)(2,1)S(1)}, bf16[8,64,256]{2,1,0:T(8,128)(2,1)S(1)}, u32[]{:S(2)}, u32[]{:S(2)}) collective-permute-start(bf16[8,64,256]{2,1,0:T(8,128)(2,1)S(1)} %get-tuple-element.72), channel_id=1, source_target_pairs={{0,4},{1,5},{2,6},{3,7},{4,0},{5,1},{6,2},{7,3},{8,12},{9,13},{10,... | collective-permute-start | bytes 786440 | tf_op jit(solution)/shard_map/ppermute | solution.py:328
  59.2 1.3 collective-permute-start.12
  60.5 11.7 %pairs_high.1 = (f32[8,32,1024]{2,1,0:T(8,128)S(1)}, f32[8,128]{1,0:T(8,128)S(1)}) custom-call(s32[8]{0:T(128)S(1)} %reshape.31.counts.refs_0_, bf16[9,48,1024]{2,1,0:T(8,128)(2,1)S(1)} %copy-done.2, bf16[9,48,1024]{2,1,0:T(8,128)(2,1)S(1)} %get-tuple-element.39.refs_2_.pay, bf16[8,48,1024]{2,1,0:T(8,128)(2,1)S(1)} %copy-done.5, ...), custom_call_target="tpu_custom_call" | custom-call | flops 12000000000 | bytes 4194304 | tf_op jit(solution)/shard_map/pairs_high/pallas_call | solution.py:368
  72.8 2.4 %collective-permute-start.13 = (bf16[32,64,256]{2,1,0:T(8,128)(2,1)S(1)}, bf16[32,64,256]{2,1,0:T(8,128)(2,1)S(1)}, u32[]{:S(2)}, u32[]{:S(2)}) collective-permute-start(bf16[32,64,256]{2,1,0:T(8,128)(2,1)S(1)} %constant_dynamic-update-slice_fusion.5.here), channel_id=1, source_target_pairs={{0,1},{1,0},{2,3},{3,2},{4,5},{5,4},{6,7},{7,6},{8,9},{9,8},{10,11... | collective-permute-start | bytes 3145736 | tf_op jit(solution)/shard_map/ppermute | solution.py:328
  75.2 18.6 %face_tiles.1.near = f32[8,32,1024]{2,1,0:T(8,128)S(1)} custom-call(bf16[8,48,1024]{2,1,0:T(8,128)(2,1)S(1)} %copy-done.5, f32[8,32,1024]{2,1,0:T(8,128)S(1)} %get-tuple-element.61.acc_in, f32[8,128]{1,0:T(8,128)S(1)} %get-tuple-element.62.after, bf16[4,48,1024]{2,1,0:T(8,128)(2,1)S(1)} %get-tuple-element.63.refs_0_, ...), custom_call_target="tpu_custom_call" | custom-call | flops 12000000000 | bytes 4194304 | tf_op jit(solution)/shard_map/face_tiles/pallas_call | solution.py:413
  93.8 6.7 %far_total.1 = (bf16[8,32,1024]{2,1,0:T(8,128)(2,1)}, f32[1,128]{1,0:T(1,128)S(1)}) custom-call(s32[8]{0:T(128)S(1)} %reshape.31.counts.refs_0_, s32[128]{0:T(128)S(1)} %reshape.32.req_box, s32[128]{0:T(128)S(1)} %reshape.33.req_tgt, bf16[32,64,256]{2,1,0:T(8,128)(2,1)S(1)} %constant_dynamic-update-slice_fusion.5.here, ...), custom_call_target="tpu_custom_call" | custom-call | tf_op jit(solution)/shard_map/far_total/pallas_call | solution.py:432
  100.6 33.7 %all_to_all.6 = f32[256,1,128]{2,1,0:T(1,128)S(1)} all-to-all(f32[256,1,128]{2,1,0:T(1,128)S(1)} %broadcast_in_dim.2), channel_id=1, replica_groups=mesh['gx'=4,'gy'=4,'gz'=16] {'gx','gy','gz'}, dimensions={0} | all-to-all | bytes 262144 | tf_op jit(solution)/shard_map/all_to_all | solution.py:448
  135.0 1.1 slice_divide_fusion
  (63 shorter events, 5.4 us)
Async XLA Ops:
  6.5 27.5 %copy-start.1 = (bf16[9,48,1024]{2,1,0:T(8,128)(2,1)}, bf16[9,48,1024]{2,1,0:T(8,128)(2,1)S(1)}, u32[]{:S(2)}) copy-start(bf16[9,48,1024]{2,1,0:T(8,128)(2,1)S(1)} %get-tuple-element.38.refs_1_) | copy-start | bytes 2654212
  6.5 27.5 %copy-start.3 = (bf16[8,48,1024]{2,1,0:T(8,128)(2,1)}, bf16[8,48,1024]{2,1,0:T(8,128)(2,1)S(1)}, u32[]{:S(2)}) copy-start(bf16[8,48,1024]{2,1,0:T(8,128)(2,1)S(1)} %get-tuple-element.40.refs_3_.fb) | copy-start | bytes 2359300
  6.5 27.5 %copy-start.6 = (bf16[4,48,1024]{2,1,0:T(8,128)(2,1)}, bf16[4,48,1024]{2,1,0:T(8,128)(2,1)S(1)}, u32[]{:S(2)}) copy-start(bf16[4,48,1024]{2,1,0:T(8,128)(2,1)S(1)} %get-tuple-element.57) | copy-start | bytes 1179652
  6.5 27.5 %copy-start.8 = (bf16[4,48,1024]{2,1,0:T(8,128)(2,1)}, bf16[4,48,1024]{2,1,0:T(8,128)(2,1)S(1)}, u32[]{:S(2)}) copy-start(bf16[4,48,1024]{2,1,0:T(8,128)(2,1)S(1)} %get-tuple-element.56) | copy-start | bytes 1179652
  6.5 30.2 %collective-permute-start = (bf16[1,64,256]{2,1,0:T(8,128)(2,1)S(1)}, bf16[1,64,256]{2,1,0:T(8,128)(2,1)S(1)}, u32[]{:S(2)}, u32[]{:S(2)}) collective-permute-start(bf16[1,64,256]{2,1,0:T(8,128)(2,1)S(1)} %bitcast.15), channel_id=1, source_target_pairs={{0,8},{1,9},{2,10},{3,11},{4,12},{5,13},{6,14},{7,15},{8,0},{9,1},... | collective-permute-start | bytes 98312 | tf_op jit(solution)/shard_map/ppermute | solution.py:328
  14.4 22.4 %collective-permute-start.1 = (bf16[4,48,1024]{2,1,0:T(8,128)(2,1)}, bf16[4,48,1024]{2,1,0:T(8,128)(2,1)S(1)}, u32[]{:S(2)}, u32[]{:S(2)}) collective-permute-start(bf16[4,48,1024]{2,1,0:T(8,128)(2,1)} %get-tuple-element.42), channel_id=1, source_target_pairs={{0,64},{64,128},{128,192},{1,65},{65,129},{129,193},{2,66},{66,130... | collective-permute-start | bytes 1179656 | tf_op jit(solution)/shard_map/ppermute | solution.py:389
  17.6 19.2 %collective-permute-start.2 = (bf16[4,48,1024]{2,1,0:T(8,128)(2,1)}, bf16[4,48,1024]{2,1,0:T(8,128)(2,1)}, u32[]{:S(2)}, u32[]{:S(2)}) collective-permute-start(bf16[4,48,1024]{2,1,0:T(8,128)(2,1)} %get-tuple-element.43), channel_id=1, source_target_pairs={{64,0},{128,64},{192,128},{65,1},{129,65},{193,129},{66,2},{130,66... | collective-permute-start | bytes 1179656 | tf_op jit(solution)/shard_map/ppermute | solution.py:390
  18.9 33.0 %collective-permute-start.3 = (bf16[4,48,1024]{2,1,0:T(8,128)(2,1)}, bf16[4,48,1024]{2,1,0:T(8,128)(2,1)}, u32[]{:S(2)}, u32[]{:S(2)}) collective-permute-start(bf16[4,48,1024]{2,1,0:T(8,128)(2,1)} %get-tuple-element.48), channel_id=1, source_target_pairs={{0,1},{1,2},{2,3},{3,4},{4,5},{5,6},{6,7},{7,8},{8,9},{9,10},{10,1... | collective-permute-start | bytes 1179656 | tf_op jit(solution)/shard_map/ppermute | solution.py:389
  23.1 32.0 %collective-permute-start.4 = (bf16[4,48,1024]{2,1,0:T(8,128)(2,1)}, bf16[4,48,1024]{2,1,0:T(8,128)(2,1)}, u32[]{:S(2)}, u32[]{:S(2)}) collective-permute-start(bf16[4,48,1024]{2,1,0:T(8,128)(2,1)} %get-tuple-element.49), channel_id=1, source_target_pairs={{1,0},{2,1},{3,2},{4,3},{5,4},{6,5},{7,6},{8,7},{9,8},{10,9},{11,1... | collective-permute-start | bytes 1179656 | tf_op jit(solution)/shard_map/ppermute | solution.py:390
  36.7 3.7 %copy-start.2 = (bf16[9,48,1024]{2,1,0:T(8,128)(2,1)S(1)}, bf16[9,48,1024]{2,1,0:T(8,128)(2,1)}, u32[]{:S(2)}) copy-start(bf16[9,48,1024]{2,1,0:T(8,128)(2,1)} %copy-done.1) | copy-start | bytes 2654212
  36.8 19.7 %collective-permute-start.5 = (bf16[2,64,256]{2,1,0:T(8,128)(2,1)S(1)}, bf16[2,64,256]{2,1,0:T(8,128)(2,1)S(1)}, u32[]{:S(2)}, u32[]{:S(2)}) collective-permute-start(bf16[2,64,256]{2,1,0:T(8,128)(2,1)S(1)} %pad_maximum_fusion), channel_id=1, source_target_pairs={{0,16},{16,0},{32,48},{48,32},{1,17},{17,1},{33,49},{49,33},{2,18}... | collective-permute-start | bytes 196616 | tf_op jit(solution)/shard_map/ppermute | solution.py:328
  38.2 18.2 %collective-permute-start.6 = (bf16[2,64,256]{2,1,0:T(8,128)(2,1)S(1)}, bf16[2,64,256]{2,1,0:T(8,128)(2,1)S(1)}, u32[]{:S(2)}, u32[]{:S(2)}) collective-permute-start(bf16[2,64,256]{2,1,0:T(8,128)(2,1)S(1)} %pad_maximum_fusion), channel_id=1, source_target_pairs={{0,32},{16,48},{32,0},{48,16},{1,33},{17,49},{33,1},{49,17},{2,34}... | collective-permute-start | bytes 196616 | tf_op jit(solution)/shard_map/ppermute | solution.py:328
  38.2 18.2 %collective-permute-start.7 = (bf16[2,64,256]{2,1,0:T(8,128)(2,1)S(1)}, bf16[2,64,256]{2,1,0:T(8,128)(2,1)S(1)}, u32[]{:S(2)}, u32[]{:S(2)}) collective-permute-start(bf16[2,64,256]{2,1,0:T(8,128)(2,1)S(1)} %pad_maximum_fusion), channel_id=1, source_target_pairs={{0,48},{16,32},{32,16},{48,0},{1,49},{17,33},{33,17},{49,1},{2,50}... | collective-permute-start | bytes 196616 | tf_op jit(solution)/shard_map/ppermute | solution.py:328
  41.6 1.2 copy-start.11
  42.8 9.0 %copy-start.12 = (bf16[8,64,256]{2,1,0:T(8,128)(2,1)S(1)}, bf16[8,64,256]{2,1,0:T(8,128)(2,1)}, u32[]{:S(2)}) copy-start(bf16[8,64,256]{2,1,0:T(8,128)(2,1)} %get-tuple-element.80) | copy-start | bytes 786436
  42.8 9.1 %copy-start.9 = (bf16[4,48,1024]{2,1,0:T(8,128)(2,1)S(1)}, bf16[4,48,1024]{2,1,0:T(8,128)(2,1)}, u32[]{:S(2)}) copy-start(bf16[4,48,1024]{2,1,0:T(8,128)(2,1)} %copy-done.8) | copy-start | bytes 1179652
  42.8 12.3 %copy-start.7 = (bf16[4,48,1024]{2,1,0:T(8,128)(2,1)S(1)}, bf16[4,48,1024]{2,1,0:T(8,128)(2,1)}, u32[]{:S(2)}) copy-start(bf16[4,48,1024]{2,1,0:T(8,128)(2,1)} %copy-done.6) | copy-start | bytes 1179652
  51.9 20.3 %collective-permute-start.8 = (bf16[4,48,1024]{2,1,0:T(8,128)(2,1)S(1)}, bf16[4,48,1024]{2,1,0:T(8,128)(2,1)S(1)}, u32[]{:S(2)}, u32[]{:S(2)}) collective-permute-start(bf16[4,48,1024]{2,1,0:T(8,128)(2,1)S(1)} %copy-done.9), channel_id=1, source_target_pairs={{0,16},{16,32},{32,48},{1,17},{17,33},{33,49},{2,18},{18,34},{34,5... | collective-permute-start | bytes 1179656 | tf_op jit(solution)/shard_map/ppermute | solution.py:389
  55.2 17.1 %collective-permute-start.9 = (bf16[4,48,1024]{2,1,0:T(8,128)(2,1)S(1)}, bf16[4,48,1024]{2,1,0:T(8,128)(2,1)S(1)}, u32[]{:S(2)}, u32[]{:S(2)}) collective-permute-start(bf16[4,48,1024]{2,1,0:T(8,128)(2,1)S(1)} %copy-done.7), channel_id=1, source_target_pairs={{16,0},{32,16},{48,32},{17,1},{33,17},{49,33},{18,2},{34,18},{50,3... | collective-permute-start | bytes 1179656 | tf_op jit(solution)/shard_map/ppermute | solution.py:390
  56.5 4.0 %copy-start.5 = (bf16[8,48,1024]{2,1,0:T(8,128)(2,1)S(1)}, bf16[8,48,1024]{2,1,0:T(8,128)(2,1)}, u32[]{:S(2)}) copy-start(bf16[8,48,1024]{2,1,0:T(8,128)(2,1)} %copy-done.3) | copy-start | bytes 2359300
  56.6 15.7 %collective-permute-start.10 = (bf16[8,64,256]{2,1,0:T(8,128)(2,1)S(1)}, bf16[8,64,256]{2,1,0:T(8,128)(2,1)S(1)}, u32[]{:S(2)}, u32[]{:S(2)}) collective-permute-start(bf16[8,64,256]{2,1,0:T(8,128)(2,1)S(1)} %get-tuple-element.72), channel_id=1, source_target_pairs={{0,2},{1,3},{2,0},{3,1},{4,6},{5,7},{6,4},{7,5},{8,10},{9,11},{10,... | collective-permute-start | bytes 786440 | tf_op jit(solution)/shard_map/ppermute | solution.py:328
  57.2 15.0 %collective-permute-start.11 = (bf16[8,64,256]{2,1,0:T(8,128)(2,1)S(1)}, bf16[8,64,256]{2,1,0:T(8,128)(2,1)S(1)}, u32[]{:S(2)}, u32[]{:S(2)}) collective-permute-start(bf16[8,64,256]{2,1,0:T(8,128)(2,1)S(1)} %get-tuple-element.72), channel_id=1, source_target_pairs={{0,4},{1,5},{2,6},{3,7},{4,0},{5,1},{6,2},{7,3},{8,12},{9,13},{10,... | collective-permute-start | bytes 786440 | tf_op jit(solution)/shard_map/ppermute | solution.py:328
  59.2 13.5 %collective-permute-start.12 = (bf16[8,64,256]{2,1,0:T(8,128)(2,1)S(1)}, bf16[8,64,256]{2,1,0:T(8,128)(2,1)S(1)}, u32[]{:S(2)}, u32[]{:S(2)}) collective-permute-start(bf16[8,64,256]{2,1,0:T(8,128)(2,1)S(1)} %get-tuple-element.72), channel_id=1, source_target_pairs={{0,6},{1,7},{2,4},{3,5},{4,2},{5,3},{6,0},{7,1},{8,14},{9,15},{10,... | collective-permute-start | bytes 786440 | tf_op jit(solution)/shard_map/ppermute | solution.py:328
  72.8 21.0 %collective-permute-start.13 = (bf16[32,64,256]{2,1,0:T(8,128)(2,1)S(1)}, bf16[32,64,256]{2,1,0:T(8,128)(2,1)S(1)}, u32[]{:S(2)}, u32[]{:S(2)}) collective-permute-start(bf16[32,64,256]{2,1,0:T(8,128)(2,1)S(1)} %constant_dynamic-update-slice_fusion.5.here), channel_id=1, source_target_pairs={{0,1},{1,0},{2,3},{3,2},{4,5},{5,4},{6,7},{7,6},{8,9},{9,8},{10,11... | collective-permute-start | bytes 3145736 | tf_op jit(solution)/shard_map/ppermute | solution.py:328
  (5 other events, 4.5 us)

commit v3 on v2

v3 whole, which is shorter than its diff:
```python
import functools
import math

import jax
import jax.numpy as jnp
from jax import lax
from jax.experimental import pallas as pl
from jax.experimental.pallas import tpu as pltpu
from jax.sharding import PartitionSpec as P

ORDER = 4
CHUNK = 128
BOXES = 8
FEATS = 48
ROWS = 48
F32 = jnp.float32
BF16 = jnp.bfloat16
NODES = [math.cos((2.0 * a + 1.0) * math.pi / (2.0 * ORDER)) for a in range(ORDER)]


def box_id(axis, at, first, second):
    place = [0, 0, 0]
    rest = [d for d in range(3) if d != axis]
    place[axis] = at
    place[rest[0]] = first
    place[rest[1]] = second
    return (place[0] * 2 + place[1]) * 2 + place[2]


def face_boxes(axis, at):
    return [box_id(axis, at, i, j) for i in range(2) for j in range(2)]


def split3(value):
    high = value.astype(BF16).astype(F32)
    rest = value - high
    mid = rest.astype(BF16).astype(F32)
    return high, mid, rest - mid


def row_ids(points):
    return lax.broadcasted_iota(jnp.int32, (8, points), 0)


def source_rows(pos, row):
    p1, p2, p3 = split3(pos)
    n1, n2, n3 = split3(1.0 + jnp.sum(pos * pos, axis=0, keepdims=True))
    s1 = jnp.where(row < 3, p1, jnp.where(row == 3, n1, jnp.where(row == 4, n2, jnp.where(row == 5, n3, 1.0))))
    s2 = p2 + pltpu.roll(p3, 3, 0)
    return jnp.concatenate([s1, s1, s2, s2, s1, jnp.zeros_like(s1)], axis=0).astype(BF16)


def target_rows(pos, row):
    p1, p2, p3 = split3(-2.0 * pos)
    m1, m2, m3 = split3(jnp.sum(pos * pos, axis=0, keepdims=True))
    qa = jnp.where(row < 3, p1, jnp.where(row < 6, 1.0, jnp.where(row == 6, m1, m2)))
    qb = jnp.where(row < 3, p2, jnp.where(row == 6, m3, 0.0))
    qc = p1 + pltpu.roll(p1, 3, 0)
    return jnp.concatenate([qa, qb, qc, p2, p3, jnp.zeros_like(qa)], axis=0).astype(BF16)


def prep_kernel(counts, offs_hbm, probes_hbm, pay, fa, fb, tab, mom, momf, f0, f1, f2, pad, offs, probes, sems):
    points = offs.shape[-1]
    row = row_ids(points)
    lane = lax.broadcasted_iota(jnp.int32, (1, points), 1)
    faces = (f0, f1, f2)
    all_offs = pltpu.make_async_copy(offs_hbm, offs, sems.at[BOXES])
    all_offs.start()
    loads = []
    for k in range(BOXES):
        load = pltpu.make_async_copy(probes_hbm.at[k // 4, k // 2 % 2, k % 2], probes.at[k], sems.at[k])
        load.start()
        loads.append(load)
    pay[BOXES] = jnp.zeros_like(pay[BOXES])
    all_offs.wait()
    for k in range(BOXES):
        place = (k // 4, k // 2 % 2, k % 2)
        pad[...] = jnp.zeros_like(pad)
        pad[0:3, :] = offs[place[0], place[1], place[2]]
        off = pad[...]
        shift = jnp.where(row == 0, place[0] - 1.0, jnp.where(row == 1, place[1] - 1.0, jnp.where(row == 2, place[2] - 1.0, 0.0)))
        pos = off + shift
        src = source_rows(pos, row)
        fa[k] = src
        fb[k] = target_rows(pos, row)
        if k == 0:
            fa[BOXES] = src
        count = counts[place]
        chunks = ((count + CHUNK - 1) // CHUNK).astype(F32)
        p1, p2, p3 = split3(pos)
        rows_a = jnp.where(row == 6, chunks, p1 + pltpu.roll(p2, 3, 0))
        tail = jnp.concatenate([rows_a, p3], axis=0).astype(BF16)
        loads[k].wait()
        vec = jnp.where(lane < count, probes[k].astype(F32), 0.0).astype(BF16)
        pay[k, 0:32, :] = vec
        pay[k, 32:48, :] = tail
        for axis in range(3):
            if place[axis] == 0:
                other = [d for d in range(3) if d != axis]
                slot = place[other[0]] * 2 + place[other[1]]
                faces[axis][slot, 0:32, :] = vec
                faces[axis][slot, 32:48, :] = tail
        unit = 2.0 * off - 1.0
        t2 = 2.0 * unit * unit - 1.0
        t3 = 2.0 * unit * t2 - unit
        weights = []
        for c in NODES:
            e2 = 2.0 * c * c - 1.0
            e3 = 2.0 * c * e2 - c
            weights.append(0.25 + 0.5 * (c * unit + e2 * t2 + e3 * t3))
        third = jnp.zeros_like(off)
        for d in range(ORDER):
            third = jnp.where(row % 4 == d, weights[d][2:3, :], third)
        seconds = []
        for half in range(2):
            seconds.append(jnp.where(row < 4, weights[2 * half][1:2, :], weights[2 * half + 1][1:2, :]))
        parts = []
        for a in range(ORDER):
            for half in range(2):
                parts.append(weights[a][0:1, :] * seconds[half] * third)
        table = jnp.concatenate(parts, axis=0).astype(BF16)
        tab[k] = table
        moment = lax.dot_general(table, vec, (((1,), (1,)), ((), ())), preferred_element_type=F32)
        momf[:, k * 32:(k + 1) * 32] = moment
    mom[...] = momf[...].astype(BF16)


WIDTHS = (512, 768, 1024)
REGION = 160


def run_steps(targets, sources_of, chunks_of, width_of, dummy, fa, vec, fb, own, out, back, tiles, steps, owner, filled):
    for c in range(len(WIDTHS)):
        filled[c] = 0
    for b in targets:
        count_b = width_of(b)
        kind = jnp.int32(0)
        for width in WIDTHS[:-1]:
            kind = kind + (count_b > width).astype(jnp.int32)
        base = kind * REGION
        at = base + filled[kind]
        for s in sources_of(b):
            count = chunks_of(s)

            def put(c, carry, s=s, b=b, at=at):
                steps[at + c] = s * 8 + c
                owner[(at + c) >> 1] = b
                return carry

            lax.fori_loop(0, count, put, 0)
            at = at + count
        steps[at] = dummy * 8
        at = at + (at & 1)
        filled[kind] = at - base
    for c in range(len(WIDTHS)):
        end = c * REGION + filled[c]
        for extra in range(6):
            steps[end + extra] = dummy * 8
            owner[(end + extra) >> 1] = targets[0]

    def columns(index):
        return pl.ds(pl.multiple_of((index & 7) * CHUNK, CHUNK), CHUNK)

    for c, width in enumerate(WIDTHS):
        first_step = c * (REGION // 2)
        total = filled[c] >> 1

        def make(t, slot, width=width):
            target = fb[owner[t], :, 0:width]
            for h in range(2):
                index = steps[2 * t + h]
                source = fa[index >> 3, :, columns(index)]
                squares = lax.dot_general(source, target, (((0,), (0,)), ((), ())), preferred_element_type=F32)
                tiles[slot, h * CHUNK:(h + 1) * CHUNK, 0:width] = lax.rsqrt(squares).astype(BF16)

        def use(t, slot, width=width):
            b = owner[t]
            first = steps[2 * t]
            second = steps[2 * t + 1]
            tile = tiles[slot, :, 0:width]
            both = jnp.concatenate([vec[first >> 3, 0:32, columns(first)], vec[second >> 3, 0:32, columns(second)]], axis=1)
            out[b, :, 0:width] += jnp.dot(both, tile, preferred_element_type=F32)
            if back is not None:
                sent = lax.dot_general(own[b, 0:32, 0:width], tile, (((1,), (1,)), ((), ())), preferred_element_type=F32)
                back[first >> 3, :, columns(first)] += sent[:, 0:CHUNK]
                back[second >> 3, :, columns(second)] += sent[:, CHUNK:]

        @pl.when(total > 0)
        def _(make=make, use=use, first_step=first_step, total=total):
            make(first_step, 0)

            def body(k, carry):
                t = first_step + 2 * k
                make(t + 1, 1)
                use(t, 0)
                make(t + 2, 0)
                use(t + 1, 1)
                return carry

            lax.fori_loop(0, (total + 1) >> 1, body, 0)


INNER = {4: (0,), 2: (0,), 1: (0,), 6: (2, 4), 5: (1, 4), 3: (1, 2), 7: (3, 5, 6)}


def count_of(counts, k):
    return counts[k // 4, k // 2 % 2, k % 2]


def inner_kernel(targets, sources_of, two_way, counts, fa, pay, fb, acc_in, after, acc, done, out, tiles, steps, owner, filled):
    if acc_in is None:
        out[...] = jnp.zeros_like(out)
    else:
        out[0:BOXES] = acc_in[...]
        out[BOXES] = jnp.zeros_like(out[BOXES])
    run_steps(
        targets, sources_of, lambda s: (count_of(counts, s) + CHUNK - 1) >> 7, lambda b: count_of(counts, b), BOXES,
        fa, pay, fb, pay, out, out if two_way else None, tiles, steps, owner, filled,
    )
    acc[...] = out[0:BOXES]
    done[...] = jnp.zeros_like(done)


def outer_kernel(counts, fb, pay, acc_self, acc_in, after, halo0, halo1, halo2, near, b0, b1, b2, probe_sums,
                 fa, vec, plus, back, tiles, steps, owner, filled, chunk_no):
    halos = (halo0, halo1, halo2)
    points = fb.shape[-1]
    row = row_ids(points)
    plus[...] = jnp.zeros_like(plus)
    back[...] = jnp.zeros_like(back)
    sources = {b: [] for b in range(BOXES)}
    spare = 12
    for axis in range(3):
        halo = halos[axis]
        targets = face_boxes(axis, 1)
        for i in range(4):
            s = axis * 4 + i
            sources[targets[i]].append(s)
            tail = halo[i, 32:48, :].astype(F32)
            rows_a = tail[0:8]
            pos = rows_a + pltpu.roll(rows_a, 5, 0) + tail[8:16]
            pos = jnp.where(row < 3, pos + jnp.where(row == axis, 2.0, 0.0), 0.0)
            feats = source_rows(pos, row)
            fa[s] = feats
            if s == 0:
                fa[spare] = feats
            vec[s] = halo[i, 0:32, :]
            chunk_no[s] = jnp.max(rows_a[6:7, 0:128]).astype(jnp.int32)
    vec[spare] = jnp.zeros_like(vec[spare])
    order = [b for b in range(BOXES) if sources[b]]
    run_steps(
        order, lambda b: sources[b], lambda s: chunk_no[s], lambda b: count_of(counts, b), spare,
        fa, vec, fb, pay, plus, back, tiles, steps, owner, filled,
    )
    total = jnp.zeros((32, 128), F32)
    for b in range(BOXES):
        extra = plus[b]
        base = acc_self[b] + acc_in[b]
        near[b] = base + extra
        weighted = pay[b, 0:32, :].astype(F32) * (base + 2.0 * extra)
        for j in range(points // 128):
            total = total + weighted[:, j * 128:(j + 1) * 128]
    probe_sums[...] = total
    for axis, ref in enumerate((b0, b1, b2)):
        ref[...] = back[4 * axis:4 * axis + 4]


def local_kernel(counts, req_box, req_tgt, here, there, momf, probe_sums, loc, sums, slab, far_acc, live, sems):
    first_copy = pltpu.make_async_copy(here, slab.at[pl.ds(0, 32)], sems.at[0])
    second_copy = pltpu.make_async_copy(there, slab.at[pl.ds(32, 32)], sems.at[1])
    first_copy.start()
    second_copy.start()
    my_y = lax.axis_index("gy")
    my_z = lax.axis_index("gz")
    far_acc[...] = jnp.zeros_like(far_acc)

    def keep(i, n):
        live[n] = i
        return n + (req_box[i >> 6, i & 63] >= 0).astype(jnp.int32)

    used = lax.fori_loop(0, 128, keep, jnp.int32(0))
    shape = (64, 64)
    source_q = lax.broadcasted_iota(jnp.int32, shape, 1)
    target_q = lax.broadcasted_iota(jnp.int32, shape, 0)

    def node(index):
        value = jnp.full(shape, 0.5 + 0.5 * NODES[0], F32)
        for a in range(1, ORDER):
            value = jnp.where(index == a, 0.5 + 0.5 * NODES[a], value)
        return value

    gaps = [node((source_q >> s) & 3) - node((target_q >> s) & 3) for s in (4, 2, 0)]
    group = lax.broadcasted_iota(jnp.int32, (64, 256), 1) >> 5
    first_copy.wait()
    second_copy.wait()

    def step(g, carry):
        for u in range(4):
            k = g * 4 + u
            i = live[jnp.minimum(k, used - 1)]
            peer = i & 63
            box = req_box[i >> 6, peer]
            tgt = req_tgt[i >> 6, peer]
            peer_y = peer >> 4
            peer_z = peer & 15
            dx = (box >> 2) - (tgt >> 2)
            dy = (peer_y - my_y) * 2 + ((box >> 1) & 1) - ((tgt >> 1) & 1)
            dz = (peer_z - my_z) * 2 + (box & 1) - (tgt & 1)
            ex = gaps[0] + dx.astype(F32)
            ey = gaps[1] + dy.astype(F32)
            ez = gaps[2] + dz.astype(F32)
            coupling = lax.rsqrt(1.0 + ex * ex + ey * ey + ez * ez).astype(BF16)
            rel_y = peer_y ^ my_y
            rel_z = peer_z ^ my_z
            at = (rel_z & 1) * 32 + ((rel_z >> 1) & 3) * 8 + rel_y * 2 + (rel_z >> 3)
            term = jnp.dot(coupling, slab[at], preferred_element_type=F32)
            wanted = jnp.where(k < used, box, -1)
            far_acc[tgt] += jnp.where(group == wanted, term, 0.0)
        return carry

    lax.fori_loop(0, (used + 3) >> 2, step, 0)
    lane = lax.broadcasted_iota(jnp.int32, (64, 128), 1)
    far_sums = jnp.zeros((64, 128), F32)
    live_points = jnp.int32(0)
    for b in range(BOXES):
        wide = far_acc[b]
        half = wide[:, 0:128] + wide[:, 128:256]
        half = half + pltpu.roll(half, 64, 1)
        half = half + pltpu.roll(half, 32, 1)
        rounded = half.astype(BF16)
        loc[b] = rounded
        moment = momf[:, (b // 4) * 128:(b // 4 + 1) * 128]
        far_sums = far_sums + jnp.where((lane >> 5) == b % 4, rounded.astype(F32) * moment, 0.0)
        live_points = live_points + count_of(counts, b)
    folded = jnp.sum(far_sums, axis=0, keepdims=True)
    folded = folded + pltpu.roll(folded, 64, 1)
    folded = folded + pltpu.roll(folded, 32, 1)
    lane32 = lax.broadcasted_iota(jnp.int32, (32, 128), 1)
    row32 = lax.broadcasted_iota(jnp.int32, (32, 128), 0)
    per_probe = jnp.sum(probe_sums[...], axis=1, keepdims=True)
    flat = jnp.sum(jnp.where(lane32 == row32, per_probe, 0.0), axis=0, keepdims=True)
    sums[...] = jnp.where(lane32[0:1] < 32, flat + folded, jnp.where(lane32[0:1] == 32, live_points.astype(F32), 0.0))


def total_kernel(counts, near, r0, r1, r2, loc, tab, kv):
    points = tab.shape[-1]
    lane = lax.broadcasted_iota(jnp.int32, (1, points), 1)
    for b in range(BOXES):
        place = (b // 4, b // 2 % 2, b % 2)
        far = lax.dot_general(loc[b][:, 0:32], tab[b], (((0,), (0,)), ((), ())), preferred_element_type=F32)
        total = near[b] + far
        for axis, ref in enumerate((r0, r1, r2)):
            if place[axis] == 0:
                other = [d for d in range(3) if d != axis]
                total = total + ref[place[other[0]] * 2 + place[other[1]]]
        kv[b] = jnp.where(lane < count_of(counts, b), total * (1.0 / math.sqrt(7.0 * points)), 0.0).astype(BF16)


VMEM = pl.BlockSpec(memory_space=pltpu.VMEM)
SMEM = pl.BlockSpec(memory_space=pltpu.SMEM)
ANY = pl.BlockSpec(memory_space=pl.ANY)
PARAMS = pltpu.CompilerParams(vmem_limit_bytes=20 * 2**20)


COST = pl.CostEstimate(flops=12 * 10**9, bytes_accessed=4 * 2**20, transcendentals=10**7)


def join(name, *arrays):
    return pl.pallas_call(
        lambda *refs: None,
        out_shape=[jax.ShapeDtypeStruct(a.shape, a.dtype) for a in arrays],
        in_specs=[ANY] * len(arrays),
        out_specs=[ANY] * len(arrays),
        input_output_aliases={i: i for i in range(len(arrays))},
        compiler_params=pltpu.CompilerParams(vmem_limit_bytes=2**20),
        name=name,
    )(*arrays)


def xor_permute(value, axis, bits):
    count = lax.axis_size(axis)
    return lax.ppermute(value, axis, [(i, i ^ bits) for i in range(count)])


def shards(offsets, probes, counts, req_box, req_tgt):
    points = offsets.shape[-1]
    shape = jax.ShapeDtypeStruct
    face = shape((4, ROWS, points), BF16)
    pay, fa, fb, tab, mom, momf, *faces = pl.pallas_call(
        prep_kernel,
        out_shape=[
            shape((BOXES + 1, ROWS, points), BF16),
            shape((BOXES + 1, FEATS, points), BF16),
            shape((BOXES, FEATS, points), BF16),
            shape((BOXES, 64, points), BF16),
            shape((64, 256), BF16),
            shape((64, 256), F32),
        ] + [face] * 3,
        in_specs=[SMEM, ANY, ANY],
        out_specs=[VMEM] * 9,
        scratch_shapes=[
            pltpu.VMEM((8, points), F32),
            pltpu.VMEM(offsets.shape, F32),
            pltpu.VMEM((BOXES, 32, points), BF16),
            pltpu.SemaphoreType.DMA((BOXES + 1,)),
        ],
        compiler_params=PARAMS,
        name="prep",
    )(counts, offsets, probes)

    acc_shape = shape((BOXES, 32, points), F32)
    lists = [
        pltpu.VMEM((2, 2 * CHUNK, points), BF16),
        pltpu.SMEM((len(WIDTHS) * REGION,), jnp.int32),
        pltpu.SMEM((len(WIDTHS) * REGION // 2,), jnp.int32),
        pltpu.SMEM((8,), jnp.int32),
    ]

    def inner(name, targets, sources_of, two_way, acc, after):
        has_acc = acc is not None

        def kernel(*refs):
            refs = list(refs)
            head = refs[:4]
            rest = refs[4:]
            acc_ref = rest.pop(0) if has_acc else None
            inner_kernel(targets, sources_of, two_way, *head, acc_ref, *rest)

        args = [counts, fa, pay, fb] + ([acc] if has_acc else []) + [after]
        return pl.pallas_call(
            kernel,
            out_shape=[acc_shape, shape((8, 128), F32)],
            in_specs=[SMEM, VMEM, VMEM, VMEM] + [VMEM] * has_acc + [ANY],
            out_specs=[VMEM, VMEM],
            scratch_shapes=[pltpu.VMEM((BOXES + 1, 32, points), F32)] + lists,
            compiler_params=PARAMS,
            cost_estimate=COST,
            name=name,
        )(*args)

    def along(axis, value, step):
        name = ("gx", "gy", "gz")[axis]
        size = lax.axis_size(name)
        return lax.ppermute(value, name, [(i, i + step) for i in range(size) if 0 <= i + step < size])

    block = mom.reshape(1, 64, 256)
    twin = xor_permute(block, "gz", 8)
    got = [along(axis, faces[axis], -1) for axis in range(3)]
    acc_self, tick = inner("self_tiles", list(range(BOXES)), lambda b: [b], False, None, mom)
    tick, twin = join("join_first", tick, twin)
    block = jnp.concatenate([block, twin], axis=0)
    more = [xor_permute(block, "gy", k) for k in (1, 2, 3)]
    acc, tick = inner("pairs_low", [1, 2, 4, 3], lambda b: INNER[b], True, None, tick)
    tick, got[0], got[1], got[2], *more = join("join_second", tick, *got, *more)
    block = jnp.concatenate([block] + more, axis=0)
    more = [xor_permute(block, "gz", 2 * k) for k in (1, 2, 3)]
    acc, tick = inner("pairs_high", [5, 6, 7], lambda b: INNER[b], True, acc, tick)
    tick, *more = join("join_third", tick, *more)
    block = jnp.concatenate([block] + more, axis=0)
    other = xor_permute(block, "gz", 1)
    near, *backs, probe_sums = pl.pallas_call(
        outer_kernel,
        out_shape=[acc_shape] + [shape((4, 32, points), F32)] * 3 + [shape((32, 128), F32)],
        in_specs=[SMEM, VMEM, VMEM, VMEM, VMEM, ANY, VMEM, VMEM, VMEM],
        out_specs=[VMEM] * 5,
        scratch_shapes=[
            pltpu.VMEM((13, FEATS, points), BF16),
            pltpu.VMEM((13, 32, points), BF16),
            pltpu.VMEM((BOXES, 32, points), F32),
            pltpu.VMEM((13, 32, points), F32),
        ] + lists + [pltpu.SMEM((16,), jnp.int32)],
        compiler_params=PARAMS,
        cost_estimate=COST,
        name="face_tiles",
    )(counts, fb, pay, acc_self, acc, tick, *got)
    returned = [along(axis, backs[axis], 1) for axis in range(3)]
    loc, sums = pl.pallas_call(
        local_kernel,
        out_shape=[shape((BOXES, 64, 128), BF16), shape((1, 128), F32)],
        in_specs=[SMEM, SMEM, SMEM, ANY, ANY, VMEM, VMEM],
        out_specs=[VMEM, VMEM],
        scratch_shapes=[
            pltpu.VMEM((64, 64, 256), BF16),
            pltpu.VMEM((BOXES, 64, 256), F32),
            pltpu.SMEM((136,), jnp.int32),
            pltpu.SemaphoreType.DMA((2,)),
        ],
        compiler_params=PARAMS,
        name="locals",
    )(counts, *[jnp.swapaxes(r, 3, 4).reshape(2, 64) for r in (req_box, req_tgt)], block, other, momf, probe_sums)
    devices = lax.axis_size("gx") * lax.axis_size("gy") * lax.axis_size("gz")
    spread = jnp.broadcast_to(sums, (devices, 128))
    gathered = lax.all_to_all(spread, ("gx", "gy", "gz"), 0, 0, tiled=True)
    kv = pl.pallas_call(
        total_kernel,
        out_shape=shape((BOXES, 32, points), BF16),
        in_specs=[SMEM] + [VMEM] * 6,
        out_specs=VMEM,
        compiler_params=PARAMS,
        cost_estimate=COST,
        name="total",
    )(counts, near, *returned, loc, tab)
    whole = jnp.sum(gathered, axis=0)
    quad = whole[0:32] * (1.0 / math.sqrt(7.0 * points)) / whole[32]
    return kv.reshape(probes.shape), quad


def solution(mesh):
    placed = (
        P("gx", "gy", "gz", None, None),
        P("gx", "gy", "gz", None, None),
        P("gx", "gy", "gz"),
        P("gx", "gy", "gz", None, None),
        P("gx", "gy", "gz", None, None),
    )
    return jax.shard_map(
        shards,
        mesh=mesh,
        in_specs=placed,
        out_specs=(P("gx", "gy", "gz", None, None), P()),
        check_vma=False,
    )
```

time: 136 us -> 124 us (0.912)
  blocking collectives: 33.7 us -> 0 us
  starting transfers between devices: 33.1 us -> 49 us
  waiting for transfers between devices: 0.48 us -> 13.4 us
  Pallas kernels: 58.1 us -> 53.8 us
  local copies, waits for them, and re-layouts: 8.56 us -> 5.35 us
    all_to_all x1 -> x0, blocking collectives: 33.7 us -> none  [shards(): gathered = lax.all_to_all(spread, ('gx', 'gy', 'gz'), 0, 0, tiled=True)]
    all_to_all x0 -> x1, starting transfers between devices: none -> 13.5 us  [shards(): gathered = lax.all_to_all(spread, ('gx', 'gy', 'gz'), 0, 0, tiled=True)]
    all_to_all x0 -> x1, waiting for transfers between devices: none -> 9.29 us  [shards(): gathered = lax.all_to_all(spread, ('gx', 'gy', 'gz'), 0, 0, tiled=True)]
    ppermute x8, starting transfers between devices: 17.8 us -> 22.8 us  [xor_permute(): return lax.ppermute(value, axis, [(i, i ^ bits) for i in range(count)])]
    pallas_call x3, Pallas kernels: 29.6 us -> 24.8 us  [inner(): pl.pallas_call(kernel, out_shape=[acc_shape, shape((8, 128), F32)], in_sp...]
    ppermute x8, waiting for transfers between devices: 0.46 us -> 4.14 us  [xor_permute(): return lax.ppermute(value, axis, [(i, i ^ bits) for i in range(count)])]
    unnamed x39 -> x20, local copies, waits for them, and re-layouts: 6.82 us -> 3.97 us
    ppermute x6, starting transfers between devices: 15.2 us -> 12.6 us  [along(): lax.ppermute(value, name, [(i, i + step) for i in range(size) if 0 <= i +...]
  transfers between devices with their start and end apart: 14 -> 15, of which waited for: 1 -> 5; matrix products, arithmetic and copies ran while one was open for 1% -> 1% of each run, Pallas kernels for 35% -> 40%
where the time goes in v3:
time: 124 us
  Pallas kernels  53.8 us (43%)
  starting transfers between devices  49 us (40%)
  waiting for transfers between devices  13.4 us (11%)
  local copies, waits for them, and re-layouts  5.35 us (4%)
    pallas_call x3, Pallas kernels, inner(): pl.pallas_call(kernel, out_shape=[acc_shape, shape((8, 128), F32)], in_sp...  24.8 us
    ppermute x8, starting transfers between devices, xor_permute(): return lax.ppermute(value, axis, [(i, i ^ bits) for i in range(count)])  22.8 us
    pallas_call x1, Pallas kernels, shards(): pl.pallas_call(outer_kernel, out_shape=[acc_shape] + [shape((4, 32, point...  16.4 us
    all_to_all x1, starting transfers between devices, shards(): gathered = lax.all_to_all(spread, ('gx', 'gy', 'gz'), 0, 0, tiled=True)  13.5 us
    ppermute x6, starting transfers between devices, along(): lax.ppermute(value, name, [(i, i + step) for i in range(size) if 0 <= i +...  12.6 us
    all_to_all x1, waiting for transfers between devices, shards(): gathered = lax.all_to_all(spread, ('gx', 'gy', 'gz'), 0, 0, tiled=True)  9.29 us
    pallas_call x1, Pallas kernels, shards(): pl.pallas_call(local_kernel, out_shape=[shape((BOXES, 64, 128), BF16), sh...  5.97 us
    pallas_call x1, Pallas kernels, shards(): pl.pallas_call(prep_kernel, out_shape=[shape((BOXES + 1, ROWS, points), B...  4.29 us
  transfers between devices with their start and end apart: 15, of which 5 were waited for; matrix products, arithmetic and copies ran while one was open for 1% of the time, Pallas kernels for 40%

profile of v3, /device:TPU:1, one launch (start us, length us, event | category | flops | bytes accessed | tf_op | source)
XLA Modules:
  0.0 123.7 jit_solution(15449999441994316851)
XLA Ops:
  1.6 1.0 copy-done
  2.6 4.3 %prep.1 = (bf16[9,48,1024]{2,1,0:T(8,128)(2,1)S(1)}, bf16[9,48,1024]{2,1,0:T(8,128)(2,1)S(1)}, bf16[8,48,1024]{2,1,0:T(8,128)(2,1)S(1)}, bf16[8,64,1024]{2,1,0:T...) custom-call(s32[2,2,2]{2,1,0:T(2,128)S(1)} %copy-done.1, ...), custom_call_target="tpu_custom_call" | custom-call | tf_op jit(solution)/shard_map/prep/pallas_call | solution.py:389
  6.9 7.8 %collective-permute-start = (bf16[1,64,256]{2,1,0:T(8,128)(2,1)S(1)}, bf16[1,64,256]{2,1,0:T(8,128)(2,1)S(1)}, u32[]{:S(2)}, u32[]{:S(2)}) collective-permute-start(bf16[1,64,256]{2,1,0:T(8,128)(2,1)S(1)} %bitcast.13), channel_id=1, source_target_pairs={{0,8},{1,9},{2,10},{3,11},{4,12},{5,13},{6,14},{7,15},{8,0},{9,1},... | collective-permute-start | bytes 98312 | tf_op jit(solution)/shard_map/ppermute | solution.py:382
  14.8 1.3 %collective-permute-start.1 = (bf16[4,48,1024]{2,1,0:T(8,128)(2,1)S(1)}, bf16[4,48,1024]{2,1,0:T(8,128)(2,1)S(1)}, u32[]{:S(2)}, u32[]{:S(2)}) collective-permute-start(bf16[4,48,1024]{2,1,0:T(8,128)(2,1)S(1)} %get-tuple-element.46), channel_id=1, source_target_pairs={{64,0},{128,64},{192,128},{65,1},{129,65},{193,129},{66,2},{130,66... | collective-permute-start | bytes 1179656 | tf_op jit(solution)/shard_map/ppermute | solution.py:444
  16.1 1.3 %collective-permute-start.2 = (bf16[4,48,1024]{2,1,0:T(8,128)(2,1)S(1)}, bf16[4,48,1024]{2,1,0:T(8,128)(2,1)S(1)}, u32[]{:S(2)}, u32[]{:S(2)}) collective-permute-start(bf16[4,48,1024]{2,1,0:T(8,128)(2,1)S(1)} %get-tuple-element.47), channel_id=1, source_target_pairs={{16,0},{32,16},{48,32},{17,1},{33,17},{49,33},{18,2},{34,18},{50,3... | collective-permute-start | bytes 1179656 | tf_op jit(solution)/shard_map/ppermute | solution.py:444
  17.4 2.9 %collective-permute-start.3 = (bf16[4,48,1024]{2,1,0:T(8,128)(2,1)S(1)}, bf16[4,48,1024]{2,1,0:T(8,128)(2,1)S(1)}, u32[]{:S(2)}, u32[]{:S(2)}) collective-permute-start(bf16[4,48,1024]{2,1,0:T(8,128)(2,1)S(1)} %get-tuple-element.48), channel_id=1, source_target_pairs={{1,0},{2,1},{3,2},{4,3},{5,4},{6,5},{7,6},{8,7},{9,8},{10,9},{11,1... | collective-permute-start | bytes 1179656 | tf_op jit(solution)/shard_map/ppermute | solution.py:444
  20.2 8.1 %self_tiles.1 = (f32[8,32,1024]{2,1,0:T(8,128)S(1)}, f32[8,128]{1,0:T(8,128)S(1)}) custom-call(s32[2,2,2]{2,1,0:T(2,128)S(1)} %copy-done.1, bf16[9,48,1024]{2,1,0:T(8,128)(2,1)S(1)} %get-tuple-element.39.refs_1_, bf16[9,48,1024]{2,1,0:T(8,128)(2,1)S(1)} %get-tuple-element.38.refs_2_.pay, bf16[8,48,1024]{2,1,0:T(8,128)(2,1)S(1)} %get-tuple-element.37.refs_3_.fb, ...), custom_call_target="tpu_custom_call" | custom-call | flops 12000000000 | bytes 4194304 | tf_op jit(solution)/shard_map/self_tiles/pallas_call | solution.py:430
  28.4 3.7 %collective-permute-start.6 = (bf16[2,64,256]{2,1,0:T(8,128)(2,1)S(1)}, bf16[2,64,256]{2,1,0:T(8,128)(2,1)S(1)}, u32[]{:S(2)}, u32[]{:S(2)}) collective-permute-start(bf16[2,64,256]{2,1,0:T(8,128)(2,1)S(1)} %pad_maximum_fusion), channel_id=1, source_target_pairs={{0,48},{16,32},{32,16},{48,0},{1,49},{17,33},{33,17},{49,1},{2,50}... | collective-permute-start | bytes 196616 | tf_op jit(solution)/shard_map/ppermute | solution.py:382
  33.0 7.9 %pairs_low.1 = (f32[8,32,1024]{2,1,0:T(8,128)S(1)}, f32[8,128]{1,0:T(8,128)S(1)}) custom-call(s32[2,2,2]{2,1,0:T(2,128)S(1)} %copy-done.1, bf16[9,48,1024]{2,1,0:T(8,128)(2,1)S(1)} %get-tuple-element.39.refs_1_, bf16[9,48,1024]{2,1,0:T(8,128)(2,1)S(1)} %get-tuple-element.38.refs_2_.pay, bf16[8,48,1024]{2,1,0:T(8,128)(2,1)S(1)} %get-tuple-element.37.refs_3_.fb, ...), custom_call_target="tpu_custom_call" | custom-call | flops 12000000000 | bytes 4194304 | tf_op jit(solution)/shard_map/pairs_low/pallas_call | solution.py:430
  42.2 1.8 %collective-permute-done.4.refs_4_ = bf16[2,64,256]{2,1,0:T(8,128)(2,1)S(1)} collective-permute-done((bf16[2,64,256]{2,1,0:T(8,128)(2,1)S(1)}, bf16[2,64,256]{2,1,0:T(8,128)(2,1)S(1)}, u32[]{:S(2)}, u32[]{:S(2)}) %collective-permute-start.4) | collective-permute-done | bytes 65568 | tf_op jit(solution)/shard_map/ppermute | solution.py:382
  44.2 4.4 %collective-permute-start.9 = (bf16[8,64,256]{2,1,0:T(8,128)(2,1)S(1)}, bf16[8,64,256]{2,1,0:T(8,128)(2,1)S(1)}, u32[]{:S(2)}, u32[]{:S(2)}) collective-permute-start(bf16[8,64,256]{2,1,0:T(8,128)(2,1)S(1)} %get-tuple-element.73), channel_id=1, source_target_pairs={{0,6},{1,7},{2,4},{3,5},{4,2},{5,3},{6,0},{7,1},{8,14},{9,15},{10,... | collective-permute-start | bytes 786440 | tf_op jit(solution)/shard_map/ppermute | solution.py:382
  49.2 8.8 %pairs_high.1 = (f32[8,32,1024]{2,1,0:T(8,128)S(1)}, f32[8,128]{1,0:T(8,128)S(1)}) custom-call(s32[2,2,2]{2,1,0:T(2,128)S(1)} %copy-done.1, bf16[9,48,1024]{2,1,0:T(8,128)(2,1)S(1)} %get-tuple-element.39.refs_1_, bf16[9,48,1024]{2,1,0:T(8,128)(2,1)S(1)} %get-tuple-element.38.refs_2_.pay, bf16[8,48,1024]{2,1,0:T(8,128)(2,1)S(1)} %get-tuple-element.37.refs_3_.fb, ...), custom_call_target="tpu_custom_call" | custom-call | flops 12000000000 | bytes 4194304 | tf_op jit(solution)/shard_map/pairs_high/pallas_call | solution.py:430
  58.1 1.4 %collective-permute-done.9.refs_3_ = bf16[8,64,256]{2,1,0:T(8,128)(2,1)S(1)} collective-permute-done((bf16[8,64,256]{2,1,0:T(8,128)(2,1)S(1)}, bf16[8,64,256]{2,1,0:T(8,128)(2,1)S(1)}, u32[]{:S(2)}, u32[]{:S(2)}) %collective-permute-start.9) | collective-permute-done | bytes 262176 | tf_op jit(solution)/shard_map/ppermute | solution.py:382
  59.8 4.5 %collective-permute-start.13 = (bf16[32,64,256]{2,1,0:T(8,128)(2,1)S(1)}, bf16[32,64,256]{2,1,0:T(8,128)(2,1)S(1)}, u32[]{:S(2)}, u32[]{:S(2)}) collective-permute-start(bf16[32,64,256]{2,1,0:T(8,128)(2,1)S(1)} %constant_dynamic-update-slice_fusion.5.here), channel_id=1, source_target_pairs={{0,1},{1,0},{2,3},{3,2},{4,5},{5,4},{6,7},{7,6},{8,9},{9,8},{10,11... | collective-permute-start | bytes 3145736 | tf_op jit(solution)/shard_map/ppermute | solution.py:382
  64.4 16.4 %face_tiles.1 = (f32[8,32,1024]{2,1,0:T(8,128)S(1)}, f32[4,32,1024]{2,1,0:T(8,128)S(1)}, f32[4,32,1024]{2,1,0:T(8,128)S(1)}, f32[4,32,1024]{2,1,0:T(8,128)S(1)}, f32[32,128]{1,0:T(8,128)S(1)}) custom-call(s32[2,2,2]{2,1,0:T(2,128)S(1)} %copy-done.1, bf16[8,48,1024]{2,1,0:T(8,128)(2,1)S(1)} %get-tuple-element.37.refs_3_.fb, ...), custom_call_target="tpu_custom_call" | custom-call | flops 12000000000 | bytes 4194304 | tf_op jit(solution)/shard_map/face_tiles/pallas_call | solution.py:461
  80.7 1.3 %collective-permute-start.10 = (f32[4,32,1024]{2,1,0:T(8,128)S(1)}, f32[4,32,1024]{2,1,0:T(8,128)S(1)}, u32[]{:S(2)}, u32[]{:S(2)}) collective-permute-start(f32[4,32,1024]{2,1,0:T(8,128)S(1)} %get-tuple-element.61), channel_id=1, source_target_pairs={{0,64},{64,128},{128,192},{1,65},{65,129},{129,193},{2,66},{66,130... | collective-permute-start | bytes 1572872 | tf_op jit(solution)/shard_map/ppermute | solution.py:444
  82.1 2.1 %collective-permute-start.11 = (f32[4,32,1024]{2,1,0:T(8,128)S(1)}, f32[4,32,1024]{2,1,0:T(8,128)}, u32[]{:S(2)}, u32[]{:S(2)}) collective-permute-start(f32[4,32,1024]{2,1,0:T(8,128)S(1)} %get-tuple-element.62), channel_id=1, source_target_pairs={{0,16},{16,32},{32,48},{1,17},{17,33},{33,49},{2,18},{18,34},{34,5... | collective-permute-start | bytes 1572872 | tf_op jit(solution)/shard_map/ppermute | solution.py:444
  84.2 3.8 %collective-permute-start.12 = (f32[4,32,1024]{2,1,0:T(8,128)S(1)}, f32[4,32,1024]{2,1,0:T(8,128)}, u32[]{:S(2)}, u32[]{:S(2)}) collective-permute-start(f32[4,32,1024]{2,1,0:T(8,128)S(1)} %get-tuple-element.63), channel_id=1, source_target_pairs={{0,1},{1,2},{2,3},{3,4},{4,5},{5,6},{6,7},{7,8},{8,9},{9,10},{10,1... | collective-permute-start | bytes 1572872 | tf_op jit(solution)/shard_map/ppermute | solution.py:444
  88.6 6.0 %locals.1 = (bf16[8,64,128]{2,1,0:T(8,128)(2,1)S(1)}, f32[1,128]{1,0:T(1,128)S(1)}) custom-call(s32[2,2,2]{2,1,0:T(2,128)S(1)} %copy-done.1, s32[2,64]{1,0:T(2,128)S(1)} %bitcast.15, s32[2,64]{1,0:T(2,128)S(1)} %bitcast.16, bf16[32,64,256]{2,1,0:T(8,128)(2,1)S(1)} %constant_dynamic-update-slice_fusion.5.here, ...), custom_call_target="tpu_custom_call" | custom-call | tf_op jit(solution)/shard_map/locals/pallas_call | solution.py:477
  95.3 13.5 %all-to-all-start = ((f32[256,1,128]{2,1,0:T(1,128)}), f32[256,1,128]{2,1,0:T(1,128)S(1)}, u32[]{:S(2)}, u32[]{:S(2)}) async-start(f32[256,1,128]{2,1,0:T(1,128)} %broadcast_in_dim.2), calls=%async_computation | async-start | bytes 262144 | tf_op jit(solution)/shard_map/all_to_all | solution.py:493
  108.9 1.2 copy-done.5
  110.2 2.4 %total.1 = bf16[8,32,1024]{2,1,0:T(8,128)(2,1)} custom-call(s32[2,2,2]{2,1,0:T(2,128)S(1)} %copy-done.1, f32[8,32,1024]{2,1,0:T(8,128)S(1)} %copy-done.5, f32[4,32,1024]{2,1,0:T(8,128)S(1)} %collective-permute-done.10.r0, f32[4,32,1024]{2,1,0:T(8,128)} %collective-permute-done.11.r1, f32[4,32,1024]{2,1,0:T(8,128)} %collective-permute-done.12.r2, ...), custom_call_target="tpu_custom_call" | custom-call | flops 12000000000 | bytes 4194304 | tf_op jit(solution)/shard_map/total/pallas_call | solution.py:494
  112.6 9.3 %all-to-all-done = f32[256,1,128]{2,1,0:T(1,128)S(1)} async-done(((f32[256,1,128]{2,1,0:T(1,128)}), f32[256,1,128]{2,1,0:T(1,128)S(1)}, u32[]{:S(2)}, u32[]{:S(2)}) %all-to-all-start) | async-done | bytes 131104 | tf_op jit(solution)/shard_map/all_to_all | solution.py:493
  122.6 1.2 multiply_divide_fusion
  (42 shorter events, 6.4 us)
Async XLA Ops:
  0.6 1.0 copy-start.1
  1.6 1.0 copy-start
  6.9 21.4 %collective-permute-start = (bf16[1,64,256]{2,1,0:T(8,128)(2,1)S(1)}, bf16[1,64,256]{2,1,0:T(8,128)(2,1)S(1)}, u32[]{:S(2)}, u32[]{:S(2)}) collective-permute-start(bf16[1,64,256]{2,1,0:T(8,128)(2,1)S(1)} %bitcast.13), channel_id=1, source_target_pairs={{0,8},{1,9},{2,10},{3,11},{4,12},{5,13},{6,14},{7,15},{8,0},{9,1},... | collective-permute-start | bytes 98312 | tf_op jit(solution)/shard_map/ppermute | solution.py:382
  14.8 29.3 %collective-permute-start.1 = (bf16[4,48,1024]{2,1,0:T(8,128)(2,1)S(1)}, bf16[4,48,1024]{2,1,0:T(8,128)(2,1)S(1)}, u32[]{:S(2)}, u32[]{:S(2)}) collective-permute-start(bf16[4,48,1024]{2,1,0:T(8,128)(2,1)S(1)} %get-tuple-element.46), channel_id=1, source_target_pairs={{64,0},{128,64},{192,128},{65,1},{129,65},{193,129},{66,2},{130,66... | collective-permute-start | bytes 1179656 | tf_op jit(solution)/shard_map/ppermute | solution.py:444
  16.1 28.0 %collective-permute-start.2 = (bf16[4,48,1024]{2,1,0:T(8,128)(2,1)S(1)}, bf16[4,48,1024]{2,1,0:T(8,128)(2,1)S(1)}, u32[]{:S(2)}, u32[]{:S(2)}) collective-permute-start(bf16[4,48,1024]{2,1,0:T(8,128)(2,1)S(1)} %get-tuple-element.47), channel_id=1, source_target_pairs={{16,0},{32,16},{48,32},{17,1},{33,17},{49,33},{18,2},{34,18},{50,3... | collective-permute-start | bytes 1179656 | tf_op jit(solution)/shard_map/ppermute | solution.py:444
  17.4 26.7 %collective-permute-start.3 = (bf16[4,48,1024]{2,1,0:T(8,128)(2,1)S(1)}, bf16[4,48,1024]{2,1,0:T(8,128)(2,1)S(1)}, u32[]{:S(2)}, u32[]{:S(2)}) collective-permute-start(bf16[4,48,1024]{2,1,0:T(8,128)(2,1)S(1)} %get-tuple-element.48), channel_id=1, source_target_pairs={{1,0},{2,1},{3,2},{4,3},{5,4},{6,5},{7,6},{8,7},{9,8},{10,9},{11,1... | collective-permute-start | bytes 1179656 | tf_op jit(solution)/shard_map/ppermute | solution.py:444
  28.4 12.5 %collective-permute-start.6 = (bf16[2,64,256]{2,1,0:T(8,128)(2,1)S(1)}, bf16[2,64,256]{2,1,0:T(8,128)(2,1)S(1)}, u32[]{:S(2)}, u32[]{:S(2)}) collective-permute-start(bf16[2,64,256]{2,1,0:T(8,128)(2,1)S(1)} %pad_maximum_fusion), channel_id=1, source_target_pairs={{0,48},{16,32},{32,16},{48,0},{1,49},{17,33},{33,17},{49,1},{2,50}... | collective-permute-start | bytes 196616 | tf_op jit(solution)/shard_map/ppermute | solution.py:382
  32.1 10.1 %collective-permute-start.5 = (bf16[2,64,256]{2,1,0:T(8,128)(2,1)S(1)}, bf16[2,64,256]{2,1,0:T(8,128)(2,1)S(1)}, u32[]{:S(2)}, u32[]{:S(2)}) collective-permute-start(bf16[2,64,256]{2,1,0:T(8,128)(2,1)S(1)} %pad_maximum_fusion), channel_id=1, source_target_pairs={{0,32},{16,48},{32,0},{48,16},{1,33},{17,49},{33,1},{49,17},{2,34}... | collective-permute-start | bytes 196616 | tf_op jit(solution)/shard_map/ppermute | solution.py:382
  40.9 3.2 %collective-permute-start.4 = (bf16[2,64,256]{2,1,0:T(8,128)(2,1)S(1)}, bf16[2,64,256]{2,1,0:T(8,128)(2,1)S(1)}, u32[]{:S(2)}, u32[]{:S(2)}) collective-permute-start(bf16[2,64,256]{2,1,0:T(8,128)(2,1)S(1)} %pad_maximum_fusion), channel_id=1, source_target_pairs={{0,16},{16,0},{32,48},{48,32},{1,17},{17,1},{33,49},{49,33},{2,18}... | collective-permute-start | bytes 196616 | tf_op jit(solution)/shard_map/ppermute | solution.py:382
  44.2 15.3 %collective-permute-start.9 = (bf16[8,64,256]{2,1,0:T(8,128)(2,1)S(1)}, bf16[8,64,256]{2,1,0:T(8,128)(2,1)S(1)}, u32[]{:S(2)}, u32[]{:S(2)}) collective-permute-start(bf16[8,64,256]{2,1,0:T(8,128)(2,1)S(1)} %get-tuple-element.73), channel_id=1, source_target_pairs={{0,6},{1,7},{2,4},{3,5},{4,2},{5,3},{6,0},{7,1},{8,14},{9,15},{10,... | collective-permute-start | bytes 786440 | tf_op jit(solution)/shard_map/ppermute | solution.py:382
  48.6 10.9 %collective-permute-start.8 = (bf16[8,64,256]{2,1,0:T(8,128)(2,1)S(1)}, bf16[8,64,256]{2,1,0:T(8,128)(2,1)S(1)}, u32[]{:S(2)}, u32[]{:S(2)}) collective-permute-start(bf16[8,64,256]{2,1,0:T(8,128)(2,1)S(1)} %get-tuple-element.73), channel_id=1, source_target_pairs={{0,4},{1,5},{2,6},{3,7},{4,0},{5,1},{6,2},{7,3},{8,12},{9,13},{10,... | collective-permute-start | bytes 786440 | tf_op jit(solution)/shard_map/ppermute | solution.py:382
  48.7 11.0 %collective-permute-start.7 = (bf16[8,64,256]{2,1,0:T(8,128)(2,1)S(1)}, bf16[8,64,256]{2,1,0:T(8,128)(2,1)S(1)}, u32[]{:S(2)}, u32[]{:S(2)}) collective-permute-start(bf16[8,64,256]{2,1,0:T(8,128)(2,1)S(1)} %get-tuple-element.73), channel_id=1, source_target_pairs={{0,2},{1,3},{2,0},{3,1},{4,6},{5,7},{6,4},{7,5},{8,10},{9,11},{10,... | collective-permute-start | bytes 786440 | tf_op jit(solution)/shard_map/ppermute | solution.py:382
  59.8 28.1 %collective-permute-start.13 = (bf16[32,64,256]{2,1,0:T(8,128)(2,1)S(1)}, bf16[32,64,256]{2,1,0:T(8,128)(2,1)S(1)}, u32[]{:S(2)}, u32[]{:S(2)}) collective-permute-start(bf16[32,64,256]{2,1,0:T(8,128)(2,1)S(1)} %constant_dynamic-update-slice_fusion.5.here), channel_id=1, source_target_pairs={{0,1},{1,0},{2,3},{3,2},{4,5},{5,4},{6,7},{7,6},{8,9},{9,8},{10,11... | collective-permute-start | bytes 3145736 | tf_op jit(solution)/shard_map/ppermute | solution.py:382
  64.4 23.6 %copy-start.3 = (s32[1,1,1,64,2]{3,4,2,1,0:T(2,128)S(1)}, s32[1,1,1,64,2]{3,4,2,1,0:T(2,128)}, u32[]{:S(2)}) copy-start(s32[1,1,1,64,2]{3,4,2,1,0:T(2,128)} %param.9) | copy-start | bytes 1540
  80.7 13.9 %copy-start.4 = (f32[8,32,1024]{2,1,0:T(8,128)}, f32[8,32,1024]{2,1,0:T(8,128)S(1)}, u32[]{:S(2)}) copy-start(f32[8,32,1024]{2,1,0:T(8,128)S(1)} %get-tuple-element.60.near) | copy-start | bytes 3145732
  80.7 28.2 %collective-permute-start.10 = (f32[4,32,1024]{2,1,0:T(8,128)S(1)}, f32[4,32,1024]{2,1,0:T(8,128)S(1)}, u32[]{:S(2)}, u32[]{:S(2)}) collective-permute-start(f32[4,32,1024]{2,1,0:T(8,128)S(1)} %get-tuple-element.61), channel_id=1, source_target_pairs={{0,64},{64,128},{128,192},{1,65},{65,129},{129,193},{2,66},{66,130... | collective-permute-start | bytes 1572872 | tf_op jit(solution)/shard_map/ppermute | solution.py:444
  82.1 26.8 %collective-permute-start.11 = (f32[4,32,1024]{2,1,0:T(8,128)S(1)}, f32[4,32,1024]{2,1,0:T(8,128)}, u32[]{:S(2)}, u32[]{:S(2)}) collective-permute-start(f32[4,32,1024]{2,1,0:T(8,128)S(1)} %get-tuple-element.62), channel_id=1, source_target_pairs={{0,16},{16,32},{32,48},{1,17},{17,33},{33,49},{2,18},{18,34},{34,5... | collective-permute-start | bytes 1572872 | tf_op jit(solution)/shard_map/ppermute | solution.py:444
  84.2 24.7 %collective-permute-start.12 = (f32[4,32,1024]{2,1,0:T(8,128)S(1)}, f32[4,32,1024]{2,1,0:T(8,128)}, u32[]{:S(2)}, u32[]{:S(2)}) collective-permute-start(f32[4,32,1024]{2,1,0:T(8,128)S(1)} %get-tuple-element.63), channel_id=1, source_target_pairs={{0,1},{1,2},{2,3},{3,4},{4,5},{5,6},{6,7},{7,8},{8,9},{9,10},{10,1... | collective-permute-start | bytes 1572872 | tf_op jit(solution)/shard_map/ppermute | solution.py:444
  88.0 0.7 copy-start.2
  95.3 26.5 %all-to-all-start = ((f32[256,1,128]{2,1,0:T(1,128)}), f32[256,1,128]{2,1,0:T(1,128)S(1)}, u32[]{:S(2)}, u32[]{:S(2)}) async-start(f32[256,1,128]{2,1,0:T(1,128)} %broadcast_in_dim.2), calls=%async_computation | async-start | bytes 262144 | tf_op jit(solution)/shard_map/all_to_all | solution.py:493
  108.9 1.2 copy-start.5

commit v4 on v3

--- a/solution.py
+++ b/solution.py
@@ -59,20 +59,12 @@
     return jnp.concatenate([qa, qb, qc, p2, p3, jnp.zeros_like(qa)], axis=0).astype(BF16)
 
 
-def prep_kernel(counts, offs_hbm, probes_hbm, pay, fa, fb, tab, mom, momf, f0, f1, f2, pad, offs, probes, sems):
+def prep_kernel(counts, offs, probes, pay, fa, fb, tab, mom, momf, f0, f1, f2, pad):
     points = offs.shape[-1]
     row = row_ids(points)
     lane = lax.broadcasted_iota(jnp.int32, (1, points), 1)
     faces = (f0, f1, f2)
-    all_offs = pltpu.make_async_copy(offs_hbm, offs, sems.at[BOXES])
-    all_offs.start()
-    loads = []
-    for k in range(BOXES):
-        load = pltpu.make_async_copy(probes_hbm.at[k // 4, k // 2 % 2, k % 2], probes.at[k], sems.at[k])
-        load.start()
-        loads.append(load)
     pay[BOXES] = jnp.zeros_like(pay[BOXES])
-    all_offs.wait()
     for k in range(BOXES):
         place = (k // 4, k // 2 % 2, k % 2)
         pad[...] = jnp.zeros_like(pad)
@@ -90,8 +82,7 @@
         p1, p2, p3 = split3(pos)
         rows_a = jnp.where(row == 6, chunks, p1 + pltpu.roll(p2, 3, 0))
         tail = jnp.concatenate([rows_a, p3], axis=0).astype(BF16)
-        loads[k].wait()
-        vec = jnp.where(lane < count, probes[k].astype(F32), 0.0).astype(BF16)
+        vec = jnp.where(lane < count, probes[place].astype(F32), 0.0).astype(BF16)
         pay[k, 0:32, :] = vec
         pay[k, 32:48, :] = tail
         for axis in range(3):
@@ -125,11 +116,11 @@
     mom[...] = momf[...].astype(BF16)
 
 
-WIDTHS = (512, 768, 1024)
+WIDTHS = (768, 1024)
 REGION = 160
 
 
-def run_steps(targets, sources_of, chunks_of, width_of, dummy, fa, vec, fb, own, out, back, tiles, steps, owner, filled):
+def run_steps(targets, sources_of, chunks_of, width_of, dummy, fa, vec, fb, own, out, back, tiles, flips, steps, owner, filled):
     for c in range(len(WIDTHS)):
         filled[c] = 0
     for b in targets:
@@ -154,7 +145,7 @@
         filled[kind] = at - base
     for c in range(len(WIDTHS)):
         end = c * REGION + filled[c]
-        for extra in range(6):
+        for extra in range(8):
             steps[end + extra] = dummy * 8
             owner[(end + extra) >> 1] = targets[0]
 
@@ -165,13 +156,15 @@
         first_step = c * (REGION // 2)
         total = filled[c] >> 1
 
+        def flip(t, slot):
+            for h in range(2):
+                index = steps[2 * t + h]
+                flips[slot, h * CHUNK:(h + 1) * CHUNK, :] = fa[index >> 3, :, columns(index)].T
+
         def make(t, slot, width=width):
             target = fb[owner[t], :, 0:width]
-            for h in range(2):
-                index = steps[2 * t + h]
-                source = fa[index >> 3, :, columns(index)]
-                squares = lax.dot_general(source, target, (((0,), (0,)), ((), ())), preferred_element_type=F32)
-                tiles[slot, h * CHUNK:(h + 1) * CHUNK, 0:width] = lax.rsqrt(squares).astype(BF16)
+            squares = jnp.dot(flips[slot], target, preferred_element_type=F32)
+            tiles[slot, :, 0:width] = lax.rsqrt(squares).astype(BF16)
 
         def use(t, slot, width=width):
             b = owner[t]
@@ -186,14 +179,18 @@
                 back[second >> 3, :, columns(second)] += sent[:, CHUNK:]
 
         @pl.when(total > 0)
-        def _(make=make, use=use, first_step=first_step, total=total):
+        def _(flip=flip, make=make, use=use, first_step=first_step, total=total):
+            flip(first_step, 0)
+            flip(first_step + 1, 1)
             make(first_step, 0)
 
             def body(k, carry):
                 t = first_step + 2 * k
                 make(t + 1, 1)
+                flip(t + 2, 0)
                 use(t, 0)
                 make(t + 2, 0)
+                flip(t + 3, 1)
                 use(t + 1, 1)
                 return carry
 
@@ -207,7 +204,7 @@
     return counts[k // 4, k // 2 % 2, k % 2]
 
 
-def inner_kernel(targets, sources_of, two_way, counts, fa, pay, fb, acc_in, after, acc, done, out, tiles, steps, owner, filled):
+def inner_kernel(targets, sources_of, two_way, counts, fa, pay, fb, acc_in, after, acc, done, out, tiles, flips, steps, owner, filled):
     if acc_in is None:
         out[...] = jnp.zeros_like(out)
     else:
@@ -215,14 +212,14 @@
         out[BOXES] = jnp.zeros_like(out[BOXES])
     run_steps(
         targets, sources_of, lambda s: (count_of(counts, s) + CHUNK - 1) >> 7, lambda b: count_of(counts, b), BOXES,
-        fa, pay, fb, pay, out, out if two_way else None, tiles, steps, owner, filled,
+        fa, pay, fb, pay, out, out if two_way else None, tiles, flips, steps, owner, filled,
     )
     acc[...] = out[0:BOXES]
     done[...] = jnp.zeros_like(done)
 
 
 def outer_kernel(counts, fb, pay, acc_self, acc_in, after, halo0, halo1, halo2, near, b0, b1, b2, probe_sums,
-                 fa, vec, plus, back, tiles, steps, owner, filled, chunk_no):
+                 fa, vec, plus, back, tiles, flips, steps, owner, filled, chunk_no):
     halos = (halo0, halo1, halo2)
     points = fb.shape[-1]
     row = row_ids(points)
@@ -250,7 +247,7 @@
     order = [b for b in range(BOXES) if sources[b]]
     run_steps(
         order, lambda b: sources[b], lambda s: chunk_no[s], lambda b: count_of(counts, b), spare,
-        fa, vec, fb, pay, plus, back, tiles, steps, owner, filled,
+        fa, vec, fb, pay, plus, back, tiles, flips, steps, owner, filled,
     )
     total = jnp.zeros((32, 128), F32)
     for b in range(BOXES):
@@ -295,8 +292,8 @@
     second_copy.wait()
 
     def step(g, carry):
-        for u in range(4):
-            k = g * 4 + u
+        for u in range(8):
+            k = g * 8 + u
             i = live[jnp.minimum(k, used - 1)]
             peer = i & 63
             box = req_box[i >> 6, peer]
@@ -318,7 +315,7 @@
             far_acc[tgt] += jnp.where(group == wanted, term, 0.0)
         return carry
 
-    lax.fori_loop(0, (used + 3) >> 2, step, 0)
+    lax.fori_loop(0, (used + 7) >> 3, step, 0)
     lane = lax.broadcasted_iota(jnp.int32, (64, 128), 1)
     far_sums = jnp.zeros((64, 128), F32)
     live_points = jnp.int32(0)
@@ -396,13 +393,10 @@
             shape((64, 256), BF16),
             shape((64, 256), F32),
         ] + [face] * 3,
-        in_specs=[SMEM, ANY, ANY],
+        in_specs=[SMEM, VMEM, VMEM],
         out_specs=[VMEM] * 9,
         scratch_shapes=[
             pltpu.VMEM((8, points), F32),
-            pltpu.VMEM(offsets.shape, F32),
-            pltpu.VMEM((BOXES, 32, points), BF16),
-            pltpu.SemaphoreType.DMA((BOXES + 1,)),
         ],
         compiler_params=PARAMS,
         name="prep",
@@ -411,6 +405,7 @@
     acc_shape = shape((BOXES, 32, points), F32)
     lists = [
         pltpu.VMEM((2, 2 * CHUNK, points), BF16),
+        pltpu.VMEM((2, 2 * CHUNK, FEATS), BF16),
         pltpu.SMEM((len(WIDTHS) * REGION,), jnp.int32),
         pltpu.SMEM((len(WIDTHS) * REGION // 2,), jnp.int32),
         pltpu.SMEM((8,), jnp.int32),
@@ -447,11 +442,11 @@
     twin = xor_permute(block, "gz", 8)
     got = [along(axis, faces[axis], -1) for axis in range(3)]
     acc_self, tick = inner("self_tiles", list(range(BOXES)), lambda b: [b], False, None, mom)
-    tick, twin = join("join_first", tick, twin)
+    tick, twin, got[0], got[1], got[2] = join("join_first", tick, twin, *got)
     block = jnp.concatenate([block, twin], axis=0)
     more = [xor_permute(block, "gy", k) for k in (1, 2, 3)]
     acc, tick = inner("pairs_low", [1, 2, 4, 3], lambda b: INNER[b], True, None, tick)
-    tick, got[0], got[1], got[2], *more = join("join_second", tick, *got, *more)
+    tick, *more = join("join_second", tick, *more)
     block = jnp.concatenate([block] + more, axis=0)
     more = [xor_permute(block, "gz", 2 * k) for k in (1, 2, 3)]
     acc, tick = inner("pairs_high", [5, 6, 7], lambda b: INNER[b], True, acc, tick)

time: 124 us -> 122 us (0.984)
  waiting for transfers between devices: 13.4 us -> 10 us
  starting transfers between devices: 49 us -> 50.6 us
    all_to_all x1, starting transfers between devices: 13.5 us -> 8 us  [shards(): gathered = lax.all_to_all(spread, ('gx', 'gy', 'gz'), 0, 0, tiled=True)]
    ppermute x8, waiting for transfers between devices: 4.14 us -> 0.02 us  [xor_permute(): return lax.ppermute(value, axis, [(i, i ^ bits) for i in range(count)])]
    ppermute x6, starting transfers between devices: 12.6 us -> 16.6 us  [along(): lax.ppermute(value, name, [(i, i + step) for i in range(size) if 0 <= i +...]
    ppermute x8, starting transfers between devices: 22.8 us -> 26 us  [xor_permute(): return lax.ppermute(value, axis, [(i, i ^ bits) for i in range(count)])]
    pallas_call x1, Pallas kernels: 4.29 us -> 2.18 us  [shards(): pl.pallas_call(prep_kernel, out_shape=[shape((BOXES + 1, ROWS, points), B...]
    pallas_call x3, Pallas kernels: 24.8 us -> 26.6 us  [inner(): pl.pallas_call(kernel, out_shape=[acc_shape, shape((8, 128), F32)], in_sp...]
  transfers between devices with their start and end apart: 15 -> 15, of which waited for: 5 -> 1; matrix products, arithmetic and copies ran while one was open for 1% -> 1% of each run, Pallas kernels for 40% -> 42%
where the time goes in v4:
time: 122 us; the launch traced here: 121 us
  Pallas kernels  52.8 us (43%)
  starting transfers between devices  50.6 us (41%)
  waiting for transfers between devices  10 us (8%)
  local copies, waits for them, and re-layouts  5.36 us (4%)
    pallas_call x3, Pallas kernels, inner(): pl.pallas_call(kernel, out_shape=[acc_shape, shape((8, 128), F32)], in_sp...  26.6 us
    ppermute x8, starting transfers between devices, xor_permute(): return lax.ppermute(value, axis, [(i, i ^ bits) for i in range(count)])  26 us
    ppermute x6, starting transfers between devices, along(): lax.ppermute(value, name, [(i, i + step) for i in range(size) if 0 <= i +...  16.6 us
    pallas_call x1, Pallas kernels, shards(): pl.pallas_call(outer_kernel, out_shape=[acc_shape] + [shape((4, 32, point...  16.6 us
    all_to_all x1, waiting for transfers between devices, shards(): gathered = lax.all_to_all(spread, ('gx', 'gy', 'gz'), 0, 0, tiled=True)  10 us
    all_to_all x1, starting transfers between devices, shards(): gathered = lax.all_to_all(spread, ('gx', 'gy', 'gz'), 0, 0, tiled=True)  8 us
    pallas_call x1, Pallas kernels, shards(): pl.pallas_call(local_kernel, out_shape=[shape((BOXES, 64, 128), BF16), sh...  5.01 us
    unnamed x20, local copies, waits for them, and re-layouts  3.97 us
  transfers between devices with their start and end apart: 15, of which 1 were waited for; matrix products, arithmetic and copies ran while one was open for 1% of the time, Pallas kernels for 42%

profile of v4, /device:TPU:1, one launch (start us, length us, event | category | flops | bytes accessed | tf_op | source)
XLA Modules:
  0.0 121.0 jit_solution(13568943716029233494)
XLA Ops:
  0.6 1.0 copy.22.offs
  1.6 1.0 copy-done
  2.6 2.2 %prep.1 = (bf16[9,48,1024]{2,1,0:T(8,128)(2,1)S(1)}, bf16[9,48,1024]{2,1,0:T(8,128)(2,1)S(1)}, bf16[8,48,1024]{2,1,0:T(8,128)(2,1)S(1)}, bf16[8,64,1024]{2,1,0:T...) custom-call(s32[2,2,2]{2,1,0:T(2,128)S(1)} %copy-done.1, ...), custom_call_target="tpu_custom_call" | custom-call | tf_op jit(solution)/shard_map/prep/pallas_call | solution.py:386
  4.8 7.8 %collective-permute-start = (bf16[1,64,256]{2,1,0:T(8,128)(2,1)S(1)}, bf16[1,64,256]{2,1,0:T(8,128)(2,1)S(1)}, u32[]{:S(2)}, u32[]{:S(2)}) collective-permute-start(bf16[1,64,256]{2,1,0:T(8,128)(2,1)S(1)} %bitcast.13), channel_id=1, source_target_pairs={{0,8},{1,9},{2,10},{3,11},{4,12},{5,13},{6,14},{7,15},{8,0},{9,1},... | collective-permute-start | bytes 98312 | tf_op jit(solution)/shard_map/ppermute | solution.py:379
  12.7 1.3 %collective-permute-start.1 = (bf16[4,48,1024]{2,1,0:T(8,128)(2,1)S(1)}, bf16[4,48,1024]{2,1,0:T(8,128)(2,1)S(1)}, u32[]{:S(2)}, u32[]{:S(2)}) collective-permute-start(bf16[4,48,1024]{2,1,0:T(8,128)(2,1)S(1)} %get-tuple-element.43), channel_id=1, source_target_pairs={{64,0},{128,64},{192,128},{65,1},{129,65},{193,129},{66,2},{130,66... | collective-permute-start | bytes 1179656 | tf_op jit(solution)/shard_map/ppermute | solution.py:439
  13.9 1.3 %collective-permute-start.2 = (bf16[4,48,1024]{2,1,0:T(8,128)(2,1)S(1)}, bf16[4,48,1024]{2,1,0:T(8,128)(2,1)S(1)}, u32[]{:S(2)}, u32[]{:S(2)}) collective-permute-start(bf16[4,48,1024]{2,1,0:T(8,128)(2,1)S(1)} %get-tuple-element.44), channel_id=1, source_target_pairs={{16,0},{32,16},{48,32},{17,1},{33,17},{49,33},{18,2},{34,18},{50,3... | collective-permute-start | bytes 1179656 | tf_op jit(solution)/shard_map/ppermute | solution.py:439
  15.2 2.9 %collective-permute-start.3 = (bf16[4,48,1024]{2,1,0:T(8,128)(2,1)S(1)}, bf16[4,48,1024]{2,1,0:T(8,128)(2,1)S(1)}, u32[]{:S(2)}, u32[]{:S(2)}) collective-permute-start(bf16[4,48,1024]{2,1,0:T(8,128)(2,1)S(1)} %get-tuple-element.45), channel_id=1, source_target_pairs={{1,0},{2,1},{3,2},{4,3},{5,4},{6,5},{7,6},{8,7},{9,8},{10,9},{11,1... | collective-permute-start | bytes 1179656 | tf_op jit(solution)/shard_map/ppermute | solution.py:439
  18.1 8.0 %self_tiles.1 = (f32[8,32,1024]{2,1,0:T(8,128)S(1)}, f32[8,128]{1,0:T(8,128)S(1)}) custom-call(s32[2,2,2]{2,1,0:T(2,128)S(1)} %copy-done.1, bf16[9,48,1024]{2,1,0:T(8,128)(2,1)S(1)} %get-tuple-element.39.refs_1_, bf16[9,48,1024]{2,1,0:T(8,128)(2,1)S(1)} %get-tuple-element.38.refs_2_.pay, bf16[8,48,1024]{2,1,0:T(8,128)(2,1)S(1)} %get-tuple-element.37.refs_3_.fb, ...), custom_call_target="tpu_custom_call" | custom-call | flops 12000000000 | bytes 4194304 | tf_op jit(solution)/shard_map/self_tiles/pallas_call | solution.py:425
  26.2 3.4 %collective-permute-start.6 = (bf16[2,64,256]{2,1,0:T(8,128)(2,1)S(1)}, bf16[2,64,256]{2,1,0:T(8,128)(2,1)S(1)}, u32[]{:S(2)}, u32[]{:S(2)}) collective-permute-start(bf16[2,64,256]{2,1,0:T(8,128)(2,1)S(1)} %pad_maximum_fusion), channel_id=1, source_target_pairs={{0,48},{16,32},{32,16},{48,0},{1,49},{17,33},{33,17},{49,1},{2,50}... | collective-permute-start | bytes 196616 | tf_op jit(solution)/shard_map/ppermute | solution.py:379
  29.6 1.6 %collective-permute-start.5 = (bf16[2,64,256]{2,1,0:T(8,128)(2,1)S(1)}, bf16[2,64,256]{2,1,0:T(8,128)(2,1)S(1)}, u32[]{:S(2)}, u32[]{:S(2)}) collective-permute-start(bf16[2,64,256]{2,1,0:T(8,128)(2,1)S(1)} %pad_maximum_fusion), channel_id=1, source_target_pairs={{0,32},{16,48},{32,0},{48,16},{1,33},{17,49},{33,1},{49,17},{2,34}... | collective-permute-start | bytes 196616 | tf_op jit(solution)/shard_map/ppermute | solution.py:379
  31.2 8.5 %pairs_low.1 = (f32[8,32,1024]{2,1,0:T(8,128)S(1)}, f32[8,128]{1,0:T(8,128)S(1)}) custom-call(s32[2,2,2]{2,1,0:T(2,128)S(1)} %copy-done.1, bf16[9,48,1024]{2,1,0:T(8,128)(2,1)S(1)} %get-tuple-element.39.refs_1_, bf16[9,48,1024]{2,1,0:T(8,128)(2,1)S(1)} %get-tuple-element.38.refs_2_.pay, bf16[8,48,1024]{2,1,0:T(8,128)(2,1)S(1)} %get-tuple-element.37.refs_3_.fb, ...), custom_call_target="tpu_custom_call" | custom-call | flops 12000000000 | bytes 4194304 | tf_op jit(solution)/shard_map/pairs_low/pallas_call | solution.py:425
  39.8 12.2 %collective-permute-start.9 = (bf16[8,64,256]{2,1,0:T(8,128)(2,1)S(1)}, bf16[8,64,256]{2,1,0:T(8,128)(2,1)S(1)}, u32[]{:S(2)}, u32[]{:S(2)}) collective-permute-start(bf16[8,64,256]{2,1,0:T(8,128)(2,1)S(1)} %get-tuple-element.73), channel_id=1, source_target_pairs={{0,6},{1,7},{2,4},{3,5},{4,2},{5,3},{6,0},{7,1},{8,14},{9,15},{10,... | collective-permute-start | bytes 786440 | tf_op jit(solution)/shard_map/ppermute | solution.py:379
  52.7 10.1 %pairs_high.1 = (f32[8,32,1024]{2,1,0:T(8,128)S(1)}, f32[8,128]{1,0:T(8,128)S(1)}) custom-call(s32[2,2,2]{2,1,0:T(2,128)S(1)} %copy-done.1, bf16[9,48,1024]{2,1,0:T(8,128)(2,1)S(1)} %get-tuple-element.39.refs_1_, bf16[9,48,1024]{2,1,0:T(8,128)(2,1)S(1)} %get-tuple-element.38.refs_2_.pay, bf16[8,48,1024]{2,1,0:T(8,128)(2,1)S(1)} %get-tuple-element.37.refs_3_.fb, ...), custom_call_target="tpu_custom_call" | custom-call | flops 12000000000 | bytes 4194304 | tf_op jit(solution)/shard_map/pairs_high/pallas_call | solution.py:425
  63.3 16.6 %face_tiles.1 = (f32[8,32,1024]{2,1,0:T(8,128)S(1)}, f32[4,32,1024]{2,1,0:T(8,128)S(1)}, f32[4,32,1024]{2,1,0:T(8,128)S(1)}, f32[4,32,1024]{2,1,0:T(8,128)S(1)}, f32[32,128]{1,0:T(8,128)S(1)}) custom-call(s32[2,2,2]{2,1,0:T(2,128)S(1)} %copy-done.1, bf16[8,48,1024]{2,1,0:T(8,128)(2,1)S(1)} %get-tuple-element.37.refs_3_.fb, ...), custom_call_target="tpu_custom_call" | custom-call | flops 12000000000 | bytes 4194304 | tf_op jit(solution)/shard_map/face_tiles/pallas_call | solution.py:456
  79.9 1.3 %collective-permute-start.10 = (f32[4,32,1024]{2,1,0:T(8,128)S(1)}, f32[4,32,1024]{2,1,0:T(8,128)S(1)}, u32[]{:S(2)}, u32[]{:S(2)}) collective-permute-start(f32[4,32,1024]{2,1,0:T(8,128)S(1)} %get-tuple-element.61), channel_id=1, source_target_pairs={{0,64},{64,128},{128,192},{1,65},{65,129},{129,193},{2,66},{66,130... | collective-permute-start | bytes 1572872 | tf_op jit(solution)/shard_map/ppermute | solution.py:439
  81.2 5.1 %collective-permute-start.11 = (f32[4,32,1024]{2,1,0:T(8,128)S(1)}, f32[4,32,1024]{2,1,0:T(8,128)}, u32[]{:S(2)}, u32[]{:S(2)}) collective-permute-start(f32[4,32,1024]{2,1,0:T(8,128)S(1)} %get-tuple-element.62), channel_id=1, source_target_pairs={{0,16},{16,32},{32,48},{1,17},{17,33},{33,49},{2,18},{18,34},{34,5... | collective-permute-start | bytes 1572872 | tf_op jit(solution)/shard_map/ppermute | solution.py:439
  86.3 4.8 %collective-permute-start.12 = (f32[4,32,1024]{2,1,0:T(8,128)S(1)}, f32[4,32,1024]{2,1,0:T(8,128)}, u32[]{:S(2)}, u32[]{:S(2)}) collective-permute-start(f32[4,32,1024]{2,1,0:T(8,128)S(1)} %get-tuple-element.63), channel_id=1, source_target_pairs={{0,1},{1,2},{2,3},{3,4},{4,5},{5,6},{6,7},{7,8},{8,9},{9,10},{10,1... | collective-permute-start | bytes 1572872 | tf_op jit(solution)/shard_map/ppermute | solution.py:439
  91.7 5.0 %locals.1 = (bf16[8,64,128]{2,1,0:T(8,128)(2,1)S(1)}, f32[1,128]{1,0:T(1,128)S(1)}) custom-call(s32[2,2,2]{2,1,0:T(2,128)S(1)} %copy-done.1, s32[2,64]{1,0:T(2,128)S(1)} %bitcast.15, s32[2,64]{1,0:T(2,128)S(1)} %bitcast.16, bf16[32,64,256]{2,1,0:T(8,128)(2,1)S(1)} %constant_dynamic-update-slice_fusion.5.here, ...), custom_call_target="tpu_custom_call" | custom-call | tf_op jit(solution)/shard_map/locals/pallas_call | solution.py:472
  96.8 0.7 broadcast_in_dim.2
  97.5 8.0 %all-to-all-start = ((f32[256,1,128]{2,1,0:T(1,128)}), f32[256,1,128]{2,1,0:T(1,128)S(1)}, u32[]{:S(2)}, u32[]{:S(2)}) async-start(f32[256,1,128]{2,1,0:T(1,128)} %broadcast_in_dim.2), calls=%async_computation | async-start | bytes 262144 | tf_op jit(solution)/shard_map/all_to_all | solution.py:488
  105.5 1.2 %copy-done.5 = f32[8,32,1024]{2,1,0:T(8,128)S(1)} copy-done((f32[8,32,1024]{2,1,0:T(8,128)S(1)}, f32[8,32,1024]{2,1,0:T(8,128)}, u32[]{:S(2)}) %copy-start.5) | copy-done | bytes 1048600
  106.7 2.4 %total.1 = bf16[8,32,1024]{2,1,0:T(8,128)(2,1)} custom-call(s32[2,2,2]{2,1,0:T(2,128)S(1)} %copy-done.1, f32[8,32,1024]{2,1,0:T(8,128)S(1)} %copy-done.5, f32[4,32,1024]{2,1,0:T(8,128)S(1)} %collective-permute-done.10.r0, f32[4,32,1024]{2,1,0:T(8,128)} %collective-permute-done.11.r1, f32[4,32,1024]{2,1,0:T(8,128)} %collective-permute-done.12.r2, ...), custom_call_target="tpu_custom_call" | custom-call | flops 12000000000 | bytes 4194304 | tf_op jit(solution)/shard_map/total/pallas_call | solution.py:489
  109.2 10.0 %all-to-all-done = f32[256,1,128]{2,1,0:T(1,128)S(1)} async-done(((f32[256,1,128]{2,1,0:T(1,128)}), f32[256,1,128]{2,1,0:T(1,128)S(1)}, u32[]{:S(2)}, u32[]{:S(2)}) %all-to-all-start) | async-done | bytes 131104 | tf_op jit(solution)/shard_map/all_to_all | solution.py:488
  119.9 1.2 multiply_divide_fusion
  (42 shorter events, 2.5 us)
Async XLA Ops:
  0.6 1.0 copy-start.1
  1.6 1.0 copy-start
  4.8 21.3 %collective-permute-start = (bf16[1,64,256]{2,1,0:T(8,128)(2,1)S(1)}, bf16[1,64,256]{2,1,0:T(8,128)(2,1)S(1)}, u32[]{:S(2)}, u32[]{:S(2)}) collective-permute-start(bf16[1,64,256]{2,1,0:T(8,128)(2,1)S(1)} %bitcast.13), channel_id=1, source_target_pairs={{0,8},{1,9},{2,10},{3,11},{4,12},{5,13},{6,14},{7,15},{8,0},{9,1},... | collective-permute-start | bytes 98312 | tf_op jit(solution)/shard_map/ppermute | solution.py:379
  12.7 13.5 %collective-permute-start.1 = (bf16[4,48,1024]{2,1,0:T(8,128)(2,1)S(1)}, bf16[4,48,1024]{2,1,0:T(8,128)(2,1)S(1)}, u32[]{:S(2)}, u32[]{:S(2)}) collective-permute-start(bf16[4,48,1024]{2,1,0:T(8,128)(2,1)S(1)} %get-tuple-element.43), channel_id=1, source_target_pairs={{64,0},{128,64},{192,128},{65,1},{129,65},{193,129},{66,2},{130,66... | collective-permute-start | bytes 1179656 | tf_op jit(solution)/shard_map/ppermute | solution.py:439
  13.9 12.2 %collective-permute-start.2 = (bf16[4,48,1024]{2,1,0:T(8,128)(2,1)S(1)}, bf16[4,48,1024]{2,1,0:T(8,128)(2,1)S(1)}, u32[]{:S(2)}, u32[]{:S(2)}) collective-permute-start(bf16[4,48,1024]{2,1,0:T(8,128)(2,1)S(1)} %get-tuple-element.44), channel_id=1, source_target_pairs={{16,0},{32,16},{48,32},{17,1},{33,17},{49,33},{18,2},{34,18},{50,3... | collective-permute-start | bytes 1179656 | tf_op jit(solution)/shard_map/ppermute | solution.py:439
  15.2 10.9 %collective-permute-start.3 = (bf16[4,48,1024]{2,1,0:T(8,128)(2,1)S(1)}, bf16[4,48,1024]{2,1,0:T(8,128)(2,1)S(1)}, u32[]{:S(2)}, u32[]{:S(2)}) collective-permute-start(bf16[4,48,1024]{2,1,0:T(8,128)(2,1)S(1)} %get-tuple-element.45), channel_id=1, source_target_pairs={{1,0},{2,1},{3,2},{4,3},{5,4},{6,5},{7,6},{8,7},{9,8},{10,9},{11,1... | collective-permute-start | bytes 1179656 | tf_op jit(solution)/shard_map/ppermute | solution.py:439
  26.2 13.5 %collective-permute-start.6 = (bf16[2,64,256]{2,1,0:T(8,128)(2,1)S(1)}, bf16[2,64,256]{2,1,0:T(8,128)(2,1)S(1)}, u32[]{:S(2)}, u32[]{:S(2)}) collective-permute-start(bf16[2,64,256]{2,1,0:T(8,128)(2,1)S(1)} %pad_maximum_fusion), channel_id=1, source_target_pairs={{0,48},{16,32},{32,16},{48,0},{1,49},{17,33},{33,17},{49,1},{2,50}... | collective-permute-start | bytes 196616 | tf_op jit(solution)/shard_map/ppermute | solution.py:379
  29.6 10.1 %collective-permute-start.5 = (bf16[2,64,256]{2,1,0:T(8,128)(2,1)S(1)}, bf16[2,64,256]{2,1,0:T(8,128)(2,1)S(1)}, u32[]{:S(2)}, u32[]{:S(2)}) collective-permute-start(bf16[2,64,256]{2,1,0:T(8,128)(2,1)S(1)} %pad_maximum_fusion), channel_id=1, source_target_pairs={{0,32},{16,48},{32,0},{48,16},{1,33},{17,49},{33,1},{49,17},{2,34}... | collective-permute-start | bytes 196616 | tf_op jit(solution)/shard_map/ppermute | solution.py:379
  31.2 8.5 %collective-permute-start.4 = (bf16[2,64,256]{2,1,0:T(8,128)(2,1)S(1)}, bf16[2,64,256]{2,1,0:T(8,128)(2,1)S(1)}, u32[]{:S(2)}, u32[]{:S(2)}) collective-permute-start(bf16[2,64,256]{2,1,0:T(8,128)(2,1)S(1)} %pad_maximum_fusion), channel_id=1, source_target_pairs={{0,16},{16,0},{32,48},{48,32},{1,17},{17,1},{33,49},{49,33},{2,18}... | collective-permute-start | bytes 196616 | tf_op jit(solution)/shard_map/ppermute | solution.py:379
  39.8 23.1 %collective-permute-start.9 = (bf16[8,64,256]{2,1,0:T(8,128)(2,1)S(1)}, bf16[8,64,256]{2,1,0:T(8,128)(2,1)S(1)}, u32[]{:S(2)}, u32[]{:S(2)}) collective-permute-start(bf16[8,64,256]{2,1,0:T(8,128)(2,1)S(1)} %get-tuple-element.73), channel_id=1, source_target_pairs={{0,6},{1,7},{2,4},{3,5},{4,2},{5,3},{6,0},{7,1},{8,14},{9,15},{10,... | collective-permute-start | bytes 786440 | tf_op jit(solution)/shard_map/ppermute | solution.py:379
  52.0 10.8 %collective-permute-start.8 = (bf16[8,64,256]{2,1,0:T(8,128)(2,1)S(1)}, bf16[8,64,256]{2,1,0:T(8,128)(2,1)S(1)}, u32[]{:S(2)}, u32[]{:S(2)}) collective-permute-start(bf16[8,64,256]{2,1,0:T(8,128)(2,1)S(1)} %get-tuple-element.73), channel_id=1, source_target_pairs={{0,4},{1,5},{2,6},{3,7},{4,0},{5,1},{6,2},{7,3},{8,12},{9,13},{10,... | collective-permute-start | bytes 786440 | tf_op jit(solution)/shard_map/ppermute | solution.py:379
  52.0 10.9 %collective-permute-start.7 = (bf16[8,64,256]{2,1,0:T(8,128)(2,1)S(1)}, bf16[8,64,256]{2,1,0:T(8,128)(2,1)S(1)}, u32[]{:S(2)}, u32[]{:S(2)}) collective-permute-start(bf16[8,64,256]{2,1,0:T(8,128)(2,1)S(1)} %get-tuple-element.73), channel_id=1, source_target_pairs={{0,2},{1,3},{2,0},{3,1},{4,6},{5,7},{6,4},{7,5},{8,10},{9,11},{10,... | collective-permute-start | bytes 786440 | tf_op jit(solution)/shard_map/ppermute | solution.py:379
  63.0 28.1 %collective-permute-start.13 = (bf16[32,64,256]{2,1,0:T(8,128)(2,1)S(1)}, bf16[32,64,256]{2,1,0:T(8,128)(2,1)S(1)}, u32[]{:S(2)}, u32[]{:S(2)}) collective-permute-start(bf16[32,64,256]{2,1,0:T(8,128)(2,1)S(1)} %constant_dynamic-update-slice_fusion.5.here), channel_id=1, source_target_pairs={{0,1},{1,0},{2,3},{3,2},{4,5},{5,4},{6,7},{7,6},{8,9},{9,8},{10,11... | collective-permute-start | bytes 3145736 | tf_op jit(solution)/shard_map/ppermute | solution.py:379
  63.3 27.8 %copy-start.3 = (s32[1,1,1,64,2]{3,4,2,1,0:T(2,128)S(1)}, s32[1,1,1,64,2]{3,4,2,1,0:T(2,128)}, u32[]{:S(2)}) copy-start(s32[1,1,1,64,2]{3,4,2,1,0:T(2,128)} %param.9) | copy-start | bytes 1540
  79.9 16.9 %copy-start.4 = (f32[8,32,1024]{2,1,0:T(8,128)}, f32[8,32,1024]{2,1,0:T(8,128)S(1)}, u32[]{:S(2)}) copy-start(f32[8,32,1024]{2,1,0:T(8,128)S(1)} %get-tuple-element.60.near) | copy-start | bytes 3145732
  79.9 25.6 %collective-permute-start.10 = (f32[4,32,1024]{2,1,0:T(8,128)S(1)}, f32[4,32,1024]{2,1,0:T(8,128)S(1)}, u32[]{:S(2)}, u32[]{:S(2)}) collective-permute-start(f32[4,32,1024]{2,1,0:T(8,128)S(1)} %get-tuple-element.61), channel_id=1, source_target_pairs={{0,64},{64,128},{128,192},{1,65},{65,129},{129,193},{2,66},{66,130... | collective-permute-start | bytes 1572872 | tf_op jit(solution)/shard_map/ppermute | solution.py:439
  81.2 24.3 %collective-permute-start.11 = (f32[4,32,1024]{2,1,0:T(8,128)S(1)}, f32[4,32,1024]{2,1,0:T(8,128)}, u32[]{:S(2)}, u32[]{:S(2)}) collective-permute-start(f32[4,32,1024]{2,1,0:T(8,128)S(1)} %get-tuple-element.62), channel_id=1, source_target_pairs={{0,16},{16,32},{32,48},{1,17},{17,33},{33,49},{2,18},{18,34},{34,5... | collective-permute-start | bytes 1572872 | tf_op jit(solution)/shard_map/ppermute | solution.py:439
  86.3 19.2 %collective-permute-start.12 = (f32[4,32,1024]{2,1,0:T(8,128)S(1)}, f32[4,32,1024]{2,1,0:T(8,128)}, u32[]{:S(2)}, u32[]{:S(2)}) collective-permute-start(f32[4,32,1024]{2,1,0:T(8,128)S(1)} %get-tuple-element.63), channel_id=1, source_target_pairs={{0,1},{1,2},{2,3},{3,4},{4,5},{5,6},{6,7},{7,8},{8,9},{9,10},{10,1... | collective-permute-start | bytes 1572872 | tf_op jit(solution)/shard_map/ppermute | solution.py:439
  91.1 0.7 copy-start.2
  97.5 21.7 %all-to-all-start = ((f32[256,1,128]{2,1,0:T(1,128)}), f32[256,1,128]{2,1,0:T(1,128)S(1)}, u32[]{:S(2)}, u32[]{:S(2)}) async-start(f32[256,1,128]{2,1,0:T(1,128)} %broadcast_in_dim.2), calls=%async_computation | async-start | bytes 262144 | tf_op jit(solution)/shard_map/all_to_all | solution.py:488
  105.5 1.2 %copy-start.5 = (f32[8,32,1024]{2,1,0:T(8,128)S(1)}, f32[8,32,1024]{2,1,0:T(8,128)}, u32[]{:S(2)}) copy-start(f32[8,32,1024]{2,1,0:T(8,128)} %copy-done.4) | copy-start | bytes 3145732
